TPU v7x, 128 devices: a whole 4x4x4 slice. The times are simulated.
128 devices in a mesh: head: 2 (over x_hi), blk: 64 (over x_lo, y, z, core).
Axes of the slice: x: 4 (x_hi: 2, x_lo: 2; x = x_hi * 2 + x_lo), y: 4, z: 4, core: 2. Of those that a mesh axis runs over, the one named last changes fastest.
Arguments:
- acts: bfloat16 [16384, 1536], P(('head', 'blk')), may hold values from -6 to 6
- teacher: bfloat16 [16384, 1536], P(('head', 'blk')), may hold values from -6 to 6
- valid: int32 [1], replicated, may hold values from 8192 to 16384
- doc_starts: int32 [16], replicated, may hold values from 0 to 16383, as said below
- routes: int32 [16384, 4], P(('head', 'blk')), may hold values from 0 to 31, all different within a row; in each aligned block of 128 rows (0 to 127, 128 to 255, ...) at most 24 rows name the same one
- gates: float32 [16384, 4], P(('head', 'blk')), as said below
- w_query: bfloat16 [1536, 1536], P(('head', 'blk')), may hold values from -0.15625 to 0.15625
- key_weight: bfloat16 [1536, 256], P(('head', 'blk')), may hold values from -0.15625 to 0.15625
- value_weight: bfloat16 [1536, 256], P(('head', 'blk')), may hold values from -0.15625 to 0.15625
- w_out: bfloat16 [1536, 1536], P(('head', 'blk')), may hold values from -4 to 4
- gain_attn: bfloat16 [1536], P(('head', 'blk')), may hold values from 0.5 to 1.5
- gain_ffn: bfloat16 [1536], P(('head', 'blk')), may hold values from 0.5 to 1.5
- w_gate: bfloat16 [1536, 24576], P(None, 'blk'), may hold values from -0.15625 to 0.15625
- w_up: bfloat16 [1536, 24576], P(None, 'blk'), may hold values from -0.15625 to 0.15625
- w_down: bfloat16 [24576, 1536], P('blk'), may hold values from -0.875 to 0.875
Outputs:
- activations: bfloat16 [16384, 1536], P(('head', 'blk'))
- grad_acts: float32 [16384, 1536], P(('head', 'blk'))
- grad_query: float32 [1536, 1536], P(('head', 'blk'))
- grad_key: float32 [1536, 256], P(('head', 'blk'))
- grad_value: float32 [1536, 256], P(('head', 'blk'))
- grad_out: float32 [1536, 1536], P(('head', 'blk'))
- grad_gain_attn: float32 [1536], P(('head', 'blk'))
- grad_gain_ffn: float32 [1536], P(('head', 'blk'))
- grad_gate: float32 [1536, 24576], P(None, 'blk')
- grad_up: float32 [1536, 24576], P(None, 'blk')
- grad_down: float32 [24576, 1536], P('blk')
Inputs may be any that keep to these rules, and one draw needn't show every extreme that they name: `doc_starts`: the first entry is 0 and the entries never fall; one document begins before token 128 and covers every token up to 8319. `routes`: a row names 4 different experts; among the rows of one device no expert is named more than 24 times. `gates`: each row is positive and sums to one.
All inputs are finite; a program needn't handle non-finite values.
Results may differ from a plain program's by a relative error of at most 0.023.
Values may be sent and summed in bfloat16 or wider, within the bound.
No kernel may reach another device: no remote copies, remote signals or barrier semaphores. Data moves between devices by JAX's collectives and lax.ppermute only.
A program may use at most 192 MiB of HBM per device.

v0:
```python
import math

import jax
import jax.numpy as jnp
from jax import lax
from jax.sharding import PartitionSpec as P

QUERY_HEADS = 12
KEY_VALUE_HEADS = 2
HEAD_SIZE = 128
WINDOW = 4096


NORM_EPS = 1e-06
ROPE_BASE = 1000000.0
MASKED = -1e30


def from_behind(array, axis, by):
    length = lax.axis_size(axis)
    return lax.ppermute(array, axis, [(i, (i + by) % length) for i in range(length)])


def doc_table(positions, doc_starts):
    before = doc_starts[None, :] <= positions[:, None]
    doc_id = jnp.sum(before.astype(jnp.int32), axis=-1)
    doc_begin = jnp.max(jnp.where(before, doc_starts[None, :], 0), axis=-1)
    return (doc_id, positions - doc_begin)


def rope_tables(offset, head_width):
    inv_freq = jnp.exp(
        jnp.arange(head_width // 2, dtype=jnp.float32) * (-2.0 * math.log(ROPE_BASE) / head_width)
    )
    angle = offset.astype(jnp.float32)[:, None] * inv_freq[None, :]
    return (jnp.cos(angle), jnp.sin(angle))


def rotate(values, cosine_table, sine_table):
    half_width = values.shape[-1] // 2
    first_half = values[..., :half_width]
    second_half = values[..., half_width:]
    cos_rows = cosine_table[:, None, :]
    sin_rows = sine_table[:, None, :]
    return jnp.concatenate(
        [
            first_half * cos_rows - second_half * sin_rows,
            second_half * cos_rows + first_half * sin_rows,
        ],
        axis=-1,
    )


def rotate_back(values, cosine_table, sine_table):
    half_width = values.shape[-1] // 2
    first_half = values[..., :half_width]
    second_half = values[..., half_width:]
    cos_rows = cosine_table[:, None, :]
    sin_rows = sine_table[:, None, :]
    return jnp.concatenate(
        [
            first_half * cos_rows + second_half * sin_rows,
            second_half * cos_rows - first_half * sin_rows,
        ],
        axis=-1,
    )


def norm_forward(values, gain_vec):
    inverse = lax.rsqrt(jnp.mean(values * values, axis=-1, keepdims=True) + NORM_EPS)
    return (values * inverse * gain_vec, inverse)


def norm_backward(values, inverse, gain_vec, incoming_grad):
    scaled = incoming_grad * gain_vec
    input_grad = inverse * scaled - values * inverse * inverse * inverse * jnp.mean(
        scaled * values, axis=-1, keepdims=True
    )
    gain_grad = jnp.sum(incoming_grad * values * inverse, axis=0)
    return (input_grad, gain_grad)


def half_meta(slot_index, tok_rows, cycle_size, doc_starts):
    local_rows = jnp.arange(tok_rows, dtype=jnp.int32)
    halves = jnp.arange(2, dtype=jnp.int32)
    positions = (halves[:, None] * cycle_size + slot_index) * tok_rows + local_rows[None, :]
    doc_id, offset = doc_table(positions.reshape(-1), doc_starts)
    return (positions, doc_id.reshape(2, tok_rows))


def piece_forward(scan_state, query_rows_all, key_block, value_block, allowed, score_scale):
    run_max, run_sum, run_out = scan_state
    scores = (
        jnp.einsum("ntgd,nsd->ntgs", query_rows_all, key_block, preferred_element_type=jnp.float32)
        * score_scale
    )
    key_mask = allowed[:, :, None, :]
    new_max = jnp.maximum(run_max, jnp.max(jnp.where(key_mask, scores, MASKED), axis=-1))
    weights = jnp.where(key_mask, jnp.exp(scores - new_max[..., None]), 0.0)
    shrink = jnp.exp(run_max - new_max)
    run_sum = run_sum * shrink + jnp.sum(weights, axis=-1)
    run_out = run_out * shrink[..., None] + jnp.einsum(
        "ntgs,nsd->ntgd",
        weights.astype(jnp.bfloat16),
        value_block,
        preferred_element_type=jnp.float32,
    )
    return (new_max, run_sum, run_out)


def piece_backward(
    query_rows_all, key_block, value_block, out_grad, log_total, row_delta, allowed, score_scale
):
    scores = (
        jnp.einsum("ntgd,nsd->ntgs", query_rows_all, key_block, preferred_element_type=jnp.float32)
        * score_scale
    )
    key_mask = allowed[:, :, None, :]
    weights = jnp.where(key_mask, jnp.exp(scores - log_total[..., None]), 0.0)
    prob_grad = jnp.einsum(
        "ntgd,nsd->ntgs", out_grad, value_block, preferred_element_type=jnp.float32
    )
    score_grad = (weights * (prob_grad - row_delta[..., None])).astype(jnp.bfloat16)
    query_part = (
        jnp.einsum("ntgs,nsd->ntgd", score_grad, key_block, preferred_element_type=jnp.float32)
        * score_scale
    )
    key_part = (
        jnp.einsum("ntgs,ntgd->nsd", score_grad, query_rows_all, preferred_element_type=jnp.float32)
        * score_scale
    )
    value_part = jnp.einsum(
        "ntgs,ntgd->nsd", weights.astype(jnp.bfloat16), out_grad, preferred_element_type=jnp.float32
    )
    return (query_part, key_part, value_part)


def body(
    acts,
    teacher,
    valid,
    doc_starts,
    routes,
    gates,
    w_query,
    key_weight,
    value_weight,
    w_out,
    gain_attn,
    gain_ffn,
    w_gate,
    w_up,
    w_down,
):
    cycle_size = lax.axis_size("blk")
    tok_rows = acts.shape[0]
    model_dim = acts.shape[1]
    head_index = lax.axis_index("head")
    cycle_index = lax.axis_index("blk")
    total_tokens = tok_rows * lax.axis_size("head") * cycle_size
    query_heads = QUERY_HEADS
    heads_of_key = KEY_VALUE_HEADS
    head_width = HEAD_SIZE
    heads_per_group = query_heads // heads_of_key
    score_scale = head_width ** (-0.5)
    loop_steps = min(cycle_size, (WINDOW + tok_rows - 2) // tok_rows + 1)
    full_query, full_key, full_value, full_out, gain_one, gain_two = (
        lax.all_gather(w_query, ("head", "blk"), axis=0, tiled=True),
        lax.all_gather(key_weight, ("head", "blk"), axis=0, tiled=True),
        lax.all_gather(value_weight, ("head", "blk"), axis=0, tiled=True),
        lax.all_gather(w_out, ("head", "blk"), axis=0, tiled=True),
        lax.all_gather(gain_attn, ("head", "blk"), axis=0, tiled=True),
        lax.all_gather(gain_ffn, ("head", "blk"), axis=0, tiled=True),
    )
    gain_one = gain_one.astype(jnp.float32)
    gain_two = gain_two.astype(jnp.float32)
    own_pos = (head_index * cycle_size + cycle_index) * tok_rows + jnp.arange(
        tok_rows, dtype=jnp.int32
    )
    own_doc, own_offset = doc_table(own_pos, doc_starts)
    cosine_table, sine_table = rope_tables(own_offset, head_width)
    values_in = acts.astype(jnp.float32)
    normed_f, inverse_one = norm_forward(values_in, gain_one)
    normalized_input = normed_f.astype(jnp.bfloat16)
    query_lin = jnp.dot(normalized_input, full_query, preferred_element_type=jnp.float32).reshape(
        tok_rows, query_heads, head_width
    )
    linear_key = jnp.dot(normalized_input, full_key, preferred_element_type=jnp.float32).reshape(
        tok_rows, heads_of_key, head_width
    )
    value_seq = (
        jnp.dot(normalized_input, full_value, preferred_element_type=jnp.float32)
        .astype(jnp.bfloat16)
        .reshape(tok_rows, heads_of_key, head_width)
    )
    query_seq = rotate(query_lin, cosine_table, sine_table).astype(jnp.bfloat16)
    key_seq = rotate(linear_key, cosine_table, sine_table).astype(jnp.bfloat16)
    query_all, key_all, value_all = (
        lax.all_to_all(query_seq, "head", split_axis=1, concat_axis=0, tiled=True),
        lax.all_to_all(key_seq, "head", split_axis=1, concat_axis=0, tiled=True),
        lax.all_to_all(value_seq, "head", split_axis=1, concat_axis=0, tiled=True),
    )
    query_half = query_all.reshape(2, tok_rows, heads_per_group, head_width)
    key_home = key_all.reshape(2, tok_rows, head_width)
    value_home = value_all.reshape(2, tok_rows, head_width)
    query_pos, query_doc = half_meta(cycle_index, tok_rows, cycle_size, doc_starts)

    def make_masks(anchor):
        key_pos, key_doc = half_meta(anchor, tok_rows, cycle_size, doc_starts)
        cross_gap = query_pos[1][:, None] - key_pos[0][None, :]
        cross_mask = ((query_doc[1][:, None] == key_doc[0][None, :]) & (cross_gap < WINDOW))[None]
        pair_gap = query_pos[:, :, None] - key_pos[:, None, :]
        pair_mask = (
            (query_doc[:, :, None] == key_doc[:, None, :]) & (pair_gap >= 0) & (pair_gap < WINDOW)
        )
        return (cross_mask, pair_mask)

    def cross_needed(anchor):
        distance = cycle_size + cycle_index - anchor
        return (distance - 1) * tok_rows + 1 < WINDOW

    def attend_block(anchor, keys_now, values_now, state_now):
        cross_mask, pair_mask = make_masks(anchor)

        def attend_with_cross(inner_state):
            run_max, run_sum, run_out = inner_state
            part_state = piece_forward(
                (run_max[1:], run_sum[1:], run_out[1:]),
                query_half[1:],
                keys_now[:1],
                values_now[:1],
                cross_mask,
                score_scale,
            )
            return (
                jnp.concatenate([run_max[:1], part_state[0]]),
                jnp.concatenate([run_sum[:1], part_state[1]]),
                jnp.concatenate([run_out[:1], part_state[2]]),
            )

        scan_state = lax.cond(
            cross_needed(anchor), attend_with_cross, lambda inner_state: inner_state, state_now
        )
        return lax.cond(
            anchor <= cycle_index,
            lambda inner_state: piece_forward(
                inner_state, query_half, keys_now, values_now, pair_mask, score_scale
            ),
            lambda inner_state: inner_state,
            scan_state,
        )

    def forward_step(carried, step_index):
        keys_now, values_now = (carried[0], carried[1])
        anchor = (cycle_index - step_index) % cycle_size
        scan_state = attend_block(anchor, keys_now, values_now, carried[2:])
        keys_next, values_next = from_behind((keys_now, values_now), "blk", 1)
        visited = None
        return ((keys_next, values_next) + scan_state, visited)

    steps_all = jnp.arange(loop_steps, dtype=jnp.int32)
    start_max = jnp.full((2, tok_rows, heads_per_group), MASKED, jnp.float32)
    start_sum = jnp.zeros((2, tok_rows, heads_per_group), jnp.float32)
    start_out = jnp.zeros((2, tok_rows, heads_per_group, head_width), jnp.float32)
    carried, stored = lax.scan(
        forward_step, (key_home, value_home, start_max, start_sum, start_out), steps_all
    )
    final_state = carried[2:]
    run_max, run_sum, run_out = final_state
    log_total = run_max + jnp.log(run_sum)
    out_half = run_out / run_sum[..., None]
    out_send = out_half.astype(jnp.bfloat16).reshape(2 * tok_rows, heads_per_group, head_width)
    out_seq = lax.all_to_all(out_send, "head", split_axis=0, concat_axis=1, tiled=True).reshape(
        tok_rows, model_dim
    )
    branch = jnp.dot(out_seq, full_out, preferred_element_type=jnp.float32)
    hidden_one = values_in + branch
    normed_two_f, inverse_two = norm_forward(hidden_one, gain_two)
    normed_two = normed_two_f.astype(jnp.bfloat16)
    experts = cycle_size // 2
    route_count = routes.shape[1]
    capacity = tok_rows * route_count * 3 // (2 * experts)
    all_slots = experts * capacity
    flat_routes = routes.reshape(-1)
    chosen = (flat_routes[:, None] == jnp.arange(experts, dtype=jnp.int32)[None, :]).astype(
        jnp.int32
    )
    slot_index = jnp.sum((jnp.cumsum(chosen, axis=0) - chosen) * chosen, axis=1)
    target = flat_routes * capacity + slot_index
    placed = jnp.any(
        target.reshape(tok_rows, route_count)[None, :, :]
        == jnp.arange(all_slots, dtype=jnp.int32)[:, None, None],
        axis=2,
    )
    outgoing = jnp.dot(
        placed.astype(jnp.bfloat16), normed_two, preferred_element_type=jnp.float32
    ).astype(jnp.bfloat16)
    outgoing = jnp.repeat(outgoing.reshape(experts, capacity, model_dim), 2, axis=0)
    incoming = lax.all_to_all(outgoing, "blk", split_axis=0, concat_axis=0, tiled=True).reshape(
        cycle_size * capacity, model_dim
    )
    gate_pre = jnp.dot(incoming, w_gate, preferred_element_type=jnp.float32)
    up_pre = jnp.dot(incoming, w_up, preferred_element_type=jnp.float32)
    hidden_units = (jax.nn.silu(gate_pre) * up_pre).astype(jnp.bfloat16)
    pieces = (
        jnp.dot(hidden_units, w_down, preferred_element_type=jnp.float32)
        .astype(jnp.bfloat16)
        .reshape(cycle_size, capacity, model_dim)
    )
    returned = lax.all_to_all(pieces, "blk", split_axis=0, concat_axis=0, tiled=True)
    expert_out = jnp.sum(
        returned.reshape(experts, 2, capacity, model_dim).astype(jnp.float32), axis=1
    ).reshape(all_slots, model_dim)
    picked = jnp.take(expert_out, target, axis=0).reshape(tok_rows, route_count, model_dim)
    mixture = jnp.sum(picked * gates[:, :, None], axis=1)
    hidden_two = hidden_one + mixture
    valid_count = valid[0]
    live_rows = own_pos < valid_count
    grad_two = jnp.where(
        live_rows[:, None],
        total_tokens / valid_count.astype(jnp.float32) * (hidden_two - teacher.astype(jnp.float32)),
        0.0,
    )
    pair_owner = jnp.arange(tok_rows * route_count, dtype=jnp.int32) // route_count
    gate_flat = gates.reshape(-1)
    grad_slots = (
        jnp.zeros((all_slots, model_dim), jnp.float32)
        .at[target]
        .add(gate_flat[:, None] * jnp.take(grad_two, pair_owner, axis=0))
    )
    grad_pieces = jnp.repeat(
        grad_slots.astype(jnp.bfloat16).reshape(experts, capacity, model_dim), 2, axis=0
    )
    grad_incoming = lax.all_to_all(
        grad_pieces, "blk", split_axis=0, concat_axis=0, tiled=True
    ).reshape(cycle_size * capacity, model_dim)
    grad_hidden = jnp.dot(grad_incoming, w_down.T, preferred_element_type=jnp.float32)
    grad_w_down = jnp.dot(hidden_units.T, grad_incoming, preferred_element_type=jnp.float32)
    sigmoid_gate = jax.nn.sigmoid(gate_pre)
    grad_gate_pre = (
        grad_hidden * up_pre * sigmoid_gate * (1.0 + gate_pre * (1.0 - sigmoid_gate))
    ).astype(jnp.bfloat16)
    grad_up_pre = (grad_hidden * gate_pre * sigmoid_gate).astype(jnp.bfloat16)
    grad_routed = (
        jnp.dot(grad_gate_pre, w_gate.T, preferred_element_type=jnp.float32)
        + jnp.dot(grad_up_pre, w_up.T, preferred_element_type=jnp.float32)
    ).astype(jnp.bfloat16)
    grad_w_gate = jnp.dot(incoming.T, grad_gate_pre, preferred_element_type=jnp.float32)
    grad_w_up = jnp.dot(incoming.T, grad_up_pre, preferred_element_type=jnp.float32)
    grad_back = lax.all_to_all(
        grad_routed.reshape(cycle_size, capacity, model_dim),
        "blk",
        split_axis=0,
        concat_axis=0,
        tiled=True,
    )
    grad_slot_in = jnp.sum(
        grad_back.reshape(experts, 2, capacity, model_dim).astype(jnp.float32), axis=1
    ).reshape(all_slots, model_dim)
    grad_normed_two = jnp.sum(
        jnp.take(grad_slot_in, target, axis=0).reshape(tok_rows, route_count, model_dim), axis=1
    )
    norm_two_grad, grad_gain_two = norm_backward(hidden_one, inverse_two, gain_two, grad_normed_two)
    grad_one = grad_two + norm_two_grad
    grad_branch = grad_one.astype(jnp.bfloat16)
    grad_w_out = jnp.dot(out_seq.T, grad_branch, preferred_element_type=jnp.float32)
    grad_attn_seq = (
        jnp.dot(grad_branch, full_out.T, preferred_element_type=jnp.float32)
        .astype(jnp.bfloat16)
        .reshape(tok_rows, query_heads, head_width)
    )
    grad_attn = lax.all_to_all(
        grad_attn_seq, "head", split_axis=1, concat_axis=0, tiled=True
    ).reshape(2, tok_rows, heads_per_group, head_width)
    row_delta = jnp.sum(grad_attn.astype(jnp.float32) * out_half, axis=-1)

    def add_grads(anchor, keys_now, values_now, query_grad, key_grad, value_grad):
        cross_mask, pair_mask = make_masks(anchor)

        def add_with_cross(inner_state):
            query_part, key_part, value_part = piece_backward(
                query_half[1:],
                keys_now[:1],
                values_now[:1],
                grad_attn[1:],
                log_total[1:],
                row_delta[1:],
                cross_mask,
                score_scale,
            )
            return (
                inner_state[0].at[1].add(query_part[0]),
                inner_state[1].at[0].add(key_part[0]),
                inner_state[2].at[0].add(value_part[0]),
            )

        def with_pair(inner_state):
            pair_query, pair_key, pair_value = piece_backward(
                query_half,
                keys_now,
                values_now,
                grad_attn,
                log_total,
                row_delta,
                pair_mask,
                score_scale,
            )
            return (
                inner_state[0] + pair_query,
                inner_state[1] + pair_key,
                inner_state[2] + pair_value,
            )

        state_now = lax.cond(
            cross_needed(anchor),
            add_with_cross,
            lambda inner_state: inner_state,
            (query_grad, key_grad, value_grad),
        )
        return lax.cond(
            anchor <= cycle_index, with_pair, lambda inner_state: inner_state, state_now
        )

    zero_keys = jnp.zeros((2, tok_rows, head_width), jnp.float32)
    zero_query = jnp.zeros((2, tok_rows, heads_per_group, head_width), jnp.float32)

    def travel_step(carried_back, step_index):
        keys_wide, values_wide, key_grad, value_grad, query_grad = carried_back
        keys_wide, values_wide, key_grad, value_grad = (
            from_behind(keys_wide.astype(jnp.bfloat16), "blk", -1).astype(keys_wide.dtype),
            from_behind(values_wide.astype(jnp.bfloat16), "blk", -1).astype(values_wide.dtype),
            from_behind(key_grad.astype(jnp.bfloat16), "blk", -1).astype(key_grad.dtype),
            from_behind(value_grad.astype(jnp.bfloat16), "blk", -1).astype(value_grad.dtype),
        )
        anchor = (cycle_index - step_index) % cycle_size
        query_grad, key_grad, value_grad = add_grads(
            anchor,
            keys_wide.astype(jnp.bfloat16),
            values_wide.astype(jnp.bfloat16),
            query_grad,
            key_grad,
            value_grad,
        )
        return ((keys_wide, values_wide, key_grad, value_grad, query_grad), None)

    finished, unused = lax.scan(
        travel_step,
        (
            carried[0].astype(jnp.float32),
            carried[1].astype(jnp.float32),
            zero_keys,
            zero_keys,
            zero_query,
        ),
        steps_all,
        reverse=True,
    )
    key_grad, value_grad, query_grad = (finished[2], finished[3], finished[4])
    query_send = query_grad.astype(jnp.bfloat16).reshape(2 * tok_rows, heads_per_group, head_width)
    key_send = key_grad.astype(jnp.bfloat16).reshape(2 * tok_rows, 1, head_width)
    value_send = value_grad.astype(jnp.bfloat16).reshape(2 * tok_rows, 1, head_width)
    query_seq_grad, key_seq_grad, value_seq_grad = (
        lax.all_to_all(query_send, "head", split_axis=0, concat_axis=1, tiled=True),
        lax.all_to_all(key_send, "head", split_axis=0, concat_axis=1, tiled=True),
        lax.all_to_all(value_send, "head", split_axis=0, concat_axis=1, tiled=True),
    )
    query_lin_grad = (
        rotate_back(query_seq_grad.astype(jnp.float32), cosine_table, sine_table)
        .astype(jnp.bfloat16)
        .reshape(tok_rows, model_dim)
    )
    key_lin_grad = (
        rotate_back(key_seq_grad.astype(jnp.float32), cosine_table, sine_table)
        .astype(jnp.bfloat16)
        .reshape(tok_rows, heads_of_key * head_width)
    )
    value_lin_grad = value_seq_grad.reshape(tok_rows, heads_of_key * head_width)
    normed_grad = jnp.dot(query_lin_grad, full_query.T, preferred_element_type=jnp.float32)
    normed_grad = normed_grad + jnp.dot(
        key_lin_grad, full_key.T, preferred_element_type=jnp.float32
    )
    normed_grad = normed_grad + jnp.dot(
        value_lin_grad, full_value.T, preferred_element_type=jnp.float32
    )
    grad_w_query = jnp.dot(normalized_input.T, query_lin_grad, preferred_element_type=jnp.float32)
    grad_w_key = jnp.dot(normalized_input.T, key_lin_grad, preferred_element_type=jnp.float32)
    grad_w_value = jnp.dot(normalized_input.T, value_lin_grad, preferred_element_type=jnp.float32)
    input_norm_grad, grad_gain_one = norm_backward(values_in, inverse_one, gain_one, normed_grad)
    grad_acts = grad_one + input_norm_grad
    shards = (
        lax.psum_scatter(grad_w_query, ("head", "blk"), scatter_dimension=0, tiled=True),
        lax.psum_scatter(grad_w_key, ("head", "blk"), scatter_dimension=0, tiled=True),
        lax.psum_scatter(grad_w_value, ("head", "blk"), scatter_dimension=0, tiled=True),
        lax.psum_scatter(grad_w_out, ("head", "blk"), scatter_dimension=0, tiled=True),
        lax.psum_scatter(grad_gain_one, ("head", "blk"), scatter_dimension=0, tiled=True),
        lax.psum_scatter(grad_gain_two, ("head", "blk"), scatter_dimension=0, tiled=True),
    )
    expert_grads = (
        lax.psum(grad_w_gate.astype(jnp.bfloat16), "head").astype(jnp.float32),
        lax.psum(grad_w_up.astype(jnp.bfloat16), "head").astype(jnp.float32),
        lax.psum(grad_w_down.astype(jnp.bfloat16), "head").astype(jnp.float32),
    )
    return (
        hidden_two.astype(jnp.bfloat16),
        grad_acts,
        shards[0],
        shards[1],
        shards[2],
        shards[3],
        shards[4],
        shards[5],
        expert_grads[0],
        expert_grads[1],
        expert_grads[2],
    )


def solution(mesh):
    return jax.shard_map(
        body,
        mesh=mesh,
        in_specs=(
            P(("head", "blk"), None),
            P(("head", "blk"), None),
            P(),
            P(),
            P(("head", "blk"), None),
            P(("head", "blk"), None),
            P(("head", "blk"), None),
            P(("head", "blk"), None),
            P(("head", "blk"), None),
            P(("head", "blk"), None),
            P(("head", "blk")),
            P(("head", "blk")),
            P(None, "blk"),
            P(None, "blk"),
            P("blk", None),
        ),
        out_specs=(
            P(("head", "blk"), None),
            P(("head", "blk"), None),
            P(("head", "blk"), None),
            P(("head", "blk"), None),
            P(("head", "blk"), None),
            P(("head", "blk"), None),
            P(("head", "blk")),
            P(("head", "blk")),
            P(None, "blk"),
            P(None, "blk"),
            P("blk", None),
        ),
        check_vma=False,
    )
```

profile of v0, /device:TPU:1, one launch (start us, length us, event | category | flops | bytes accessed | tf_op | source)
XLA Modules:
  0.0 3985.6 jit_solution(26541542375317533)
XLA Ops:
  11.4 69.5 %all-reduce.13 = (bf16[1536]{0:T(1024)(128)(2,1)S(1)}, bf16[1536]{0:T(1024)(128)(2,1)}) all-reduce(bf16[1536]{0:T(1024)(128)(2,1)S(1)} %dynamic-update-slice.9, bf16[1536]{0:T(1024)(128)(2,1)S(1)} %dynamic-update-slice.10), channel_id=1, replica_groups=mesh['head'=2,'blk'=64] {'head','blk'}, use_global_device_ids=true, to_apply=%add | all-reduce | flops 3072 | bytes 12288
  80.9 35.0 all-gather
  123.2 36.0 all-gather.1
  182.2 9.7 all-to-all-done.2
  200.2 820.3 %while.46 = (s32[]{:T(128)}, bf16[2,128,128]{2,1,0:T(8,128)(2,1)}, bf16[2,128,128]{2,1,0:T(8,128)(2,1)S(1)}, f32[2,128,6]{1,2,0:T(8,128)S(1)}, f32[2,128,6]{1,2,...) while((s32[]{:T(128)}, bf16[2,128,128]{2,1,0:T(8,128)(2,1)}, ...), condition=%wide.region_13.14_spmd, body=%wide.region_3.13_spmd.sunk | while | flops 154718496 | bytes 10482478 | solution.py:265
  272.8 9.5 collective-permute-start
  322.9 9.5 collective-permute-start
  348.0 9.5 collective-permute-start
  373.0 9.5 collective-permute-start
  398.0 9.5 collective-permute-start
  423.1 9.5 collective-permute-start
  448.1 9.5 collective-permute-start
  1043.6 66.2 %all_to_all.128 = bf16[64,24,1536]{2,1,0:T(8,128)(2,1)S(1)} all-to-all(bf16[64,24,1536]{2,1,0:T(8,128)(2,1)S(1)} %bitcast.298), channel_id=1, replica_groups=mesh['head'=2,'blk'=64] {'blk'}, dimensions={0} | all-to-all | bytes 9437184 | tf_op jit(solution)/shard_map/all_to_all | solution.py:299
  1140.0 49.1 %all-to-all-done.5 = bf16[64,24,1536]{2,1,0:T(8,128)(2,1)} async-done(((bf16[64,24,1536]{2,1,0:T(8,128)(2,1)}), bf16[64,24,1536]{2,1,0:T(8,128)(2,1)}, u32[]{:S(2)}, u32[]{:S(2)}) %all-to-all-start.5) | async-done | bytes 4718624 | tf_op jit(solution)/shard_map/all_to_all | solution.py:310
  1215.9 13.9 scatter_custom_fusion
  1232.8 66.2 %all_to_all.129 = bf16[64,24,1536]{2,1,0:T(8,128)(2,1)S(1)} all-to-all(bf16[64,24,1536]{2,1,0:T(8,128)(2,1)S(1)} %bitcast.299), channel_id=1, replica_groups=mesh['head'=2,'blk'=64] {'blk'}, dimensions={0} | all-to-all | bytes 9437184 | tf_op jit(solution)/shard_map/all_to_all | solution.py:334
  1331.8 45.8 %all-to-all-done.7 = bf16[64,24,1536]{2,1,0:T(8,128)(2,1)} async-done(((bf16[64,24,1536]{2,1,0:T(8,128)(2,1)}), bf16[64,24,1536]{2,1,0:T(8,128)(2,1)}, u32[]{:S(2)}, u32[]{:S(2)}) %all-to-all-start.7) | async-done | bytes 4718624 | tf_op jit(solution)/shard_map/all_to_all | solution.py:350
  1423.9 1533.4 %while.47 = (s32[]{:T(128)}, bf16[2,128,128]{2,1,0:T(8,128)(2,1)}, bf16[2,128,128]{2,1,0:T(8,128)(2,1)}, f32[2,128,128]{2,1,0:T(8,128)S(1)}, f32[2,128,128]{2,1,...) while((s32[]{:T(128)}, bf16[2,128,128]{2,1,0:T(8,128)(2,1)}, ...), condition=%wide.region_32.34_spmd, body=%wide.region_26.33_spmd.sunk | while | flops 380694560 | bytes 13360118 | solution.py:446
  2998.3 370.1 %fusion.126 = (f32[16,1536]{1,0:T(8,128)S(1)}, f32[16,256]{1,0:T(8,128)S(1)}, f32[16,256]{1,0:T(8,128)S(1)}, f32[16,1536]{1,0:T(8,128)S(1)}) fusion(f32[1536,1536]{1,0:T(8,128)} %fusion.119, f32[1536,256]{1,0:T(8,128)} %fusion.117, f32[1536,256]{1,0:T(8,128)} %fusion.115, f32[1536,1536]{1,0:T(8,128)} %fusion.102), kind=kCustom, calls=%all-reduce-scatter.4 | all-reduce-scatter fusion | flops 7340033 | bytes 22249472
  3714.7 62.4 %all-reduce.12 = (f32[1536]{0:T(1024)S(1)}, f32[1536]{0:T(1024)S(1)}) all-reduce(f32[1536]{0:T(1024)S(1)} %get-tuple-element.917, f32[1536]{0:T(1024)S(1)} %copy-done.108), channel_id=6, replica_groups=mesh['head'=2,'blk'=64] {'head','blk'}, use_global_device_ids=true, to_apply=%region_39.41.clone | all-reduce | flops 3072 | bytes 24576
  3778.3 23.8 concatenate.37
  3802.1 24.5 concatenate.36
  3858.8 52.0 %concatenate.38 = f32[524,1536]{1,0:T(8,128)} concatenate(f32[12,1536]{1,0:T(8,128)S(1)} %collective-permute-done.133, f32[16,1536]{1,0:T(8,128)} %copy-done.87, f32[16,1536]{1,0:T(8,128)} %copy-done.84, f32[16,1536]{1,0:T(8,128)} %copy-done.83, f32[16,1536]{1,0:T(8,128)} %copy-done.80, f32[16,1536]{1,0:T(8,128)} %copy-done.75, f32[16,1536]{1,0:T(8,128)} %copy-done.72, ...), dimensions={0} | concatenate | bytes 6438912
  3926.2 51.2 %concatenate.35 = f32[524,1536]{1,0:T(8,128)} concatenate(f32[12,1536]{1,0:T(8,128)S(1)} %collective-permute-done.37, f32[16,1536]{1,0:T(8,128)S(1)} %collective-permute-done.36, f32[16,1536]{1,0:T(8,128)} %copy-done.104, f32[16,1536]{1,0:T(8,128)} %copy-done.103, f32[16,1536]{1,0:T(8,128)} %copy-done.102, f32[16,1536]{1,0:T(8,128)} %copy-done.101, f32[16,1536]{1,0:T(8,128)} %copy-done.100, ...), dimensions={0} | concatenate | bytes 6438912
  (2741 shorter events, 3035.9 us)
Async XLA Ops:
  7.2 157.4 %all-gather.7.cloned.1.call-start = ((), (), s32[]{:S(2)}) async-start(), calls=%async_computation.12 | async-start | bytes 6340608 | tf_op jit(solution)/shard_map/all_gather | solution.py:168
  117.7 61.0 %all-to-all-start = ((bf16[128,2,128]{2,0,1:T(8,128)(2,1)}), bf16[128,2,128]{2,0,1:T(8,128)(2,1)S(1)}, u32[]{:S(2)}, u32[]{:S(2)}) async-start(bf16[128,2,128]{2,0,1:T(8,128)(2,1)} %pad_maximum_fusion.5), calls=%async_computation | async-start | bytes 131072 | tf_op jit(solution)/shard_map/all_to_all | solution.py:200
  121.0 908.6 %all-gather.9.cloned.1.call-start = ((), (), s32[]{:S(2)}) async-start(), calls=%async_computation.13 | async-start | bytes 6340608 | tf_op jit(solution)/shard_map/all_gather | solution.py:171
  1121.1 68.0 %all-to-all-start.5 = ((bf16[64,24,1536]{2,1,0:T(8,128)(2,1)}), bf16[64,24,1536]{2,1,0:T(8,128)(2,1)}, u32[]{:S(2)}, u32[]{:S(2)}) async-start(bf16[64,24,1536]{2,1,0:T(8,128)(2,1)} %bitcast.310), calls=%async_computation.5 | async-start | bytes 9437184 | tf_op jit(solution)/shard_map/all_to_all | solution.py:310
  1309.6 68.0 %all-to-all-start.7 = ((bf16[64,24,1536]{2,1,0:T(8,128)(2,1)}), bf16[64,24,1536]{2,1,0:T(8,128)(2,1)}, u32[]{:S(2)}, u32[]{:S(2)}) async-start(bf16[64,24,1536]{2,1,0:T(8,128)(2,1)} %bitcast.300), calls=%async_computation.7 | async-start | bytes 9437184 | tf_op jit(solution)/shard_map/all_to_all | solution.py:350
  1415.6 2226.8 %all-reduce.18.cloned.1.call-start = ((), (), s32[]{:S(2)}) async-start(), calls=%async_computation.14 | async-start | bytes 7077888 | tf_op jit(solution)/shard_map/psum | solution.py:499
  2072.9 42.6 %collective-permute-start.2 = (bf16[2,128,128]{2,1,0:T(8,128)(2,1)}, bf16[2,128,128]{2,1,0:T(8,128)(2,1)S(1)}, u32[]{:S(2)}, u32[]{:S(2)}) collective-permute-start(bf16[2,128,128]{2,1,0:T(8,128)(2,1)} %get-tuple-element.1389), channel_id=1, source_target_pairs={{0,63},{1,0},{2,1},{3,2},{4,3},{5,4},{6,5},{7,6},{8,7},{9,8},{10,9... | collective-permute-start | bytes 196616 | tf_op jit(solution)/shard_map/while/body/eval_jaxpr/ppermute | solution.py:21
  2165.9 42.6 %collective-permute-start.2 = (bf16[2,128,128]{2,1,0:T(8,128)(2,1)}, bf16[2,128,128]{2,1,0:T(8,128)(2,1)S(1)}, u32[]{:S(2)}, u32[]{:S(2)}) collective-permute-start(bf16[2,128,128]{2,1,0:T(8,128)(2,1)} %get-tuple-element.1389), channel_id=1, source_target_pairs={{0,63},{1,0},{2,1},{3,2},{4,3},{5,4},{6,5},{7,6},{8,7},{9,8},{10,9... | collective-permute-start | bytes 196616 | tf_op jit(solution)/shard_map/while/body/eval_jaxpr/ppermute | solution.py:21
  2352.0 42.6 %collective-permute-start.2 = (bf16[2,128,128]{2,1,0:T(8,128)(2,1)}, bf16[2,128,128]{2,1,0:T(8,128)(2,1)S(1)}, u32[]{:S(2)}, u32[]{:S(2)}) collective-permute-start(bf16[2,128,128]{2,1,0:T(8,128)(2,1)} %get-tuple-element.1389), channel_id=1, source_target_pairs={{0,63},{1,0},{2,1},{3,2},{4,3},{5,4},{6,5},{7,6},{8,7},{9,8},{10,9... | collective-permute-start | bytes 196616 | tf_op jit(solution)/shard_map/while/body/eval_jaxpr/ppermute | solution.py:21
  2538.1 42.6 %collective-permute-start.2 = (bf16[2,128,128]{2,1,0:T(8,128)(2,1)}, bf16[2,128,128]{2,1,0:T(8,128)(2,1)S(1)}, u32[]{:S(2)}, u32[]{:S(2)}) collective-permute-start(bf16[2,128,128]{2,1,0:T(8,128)(2,1)} %get-tuple-element.1389), channel_id=1, source_target_pairs={{0,63},{1,0},{2,1},{3,2},{4,3},{5,4},{6,5},{7,6},{8,7},{9,8},{10,9... | collective-permute-start | bytes 196616 | tf_op jit(solution)/shard_map/while/body/eval_jaxpr/ppermute | solution.py:21
  2724.2 42.6 %collective-permute-start.2 = (bf16[2,128,128]{2,1,0:T(8,128)(2,1)}, bf16[2,128,128]{2,1,0:T(8,128)(2,1)S(1)}, u32[]{:S(2)}, u32[]{:S(2)}) collective-permute-start(bf16[2,128,128]{2,1,0:T(8,128)(2,1)} %get-tuple-element.1389), channel_id=1, source_target_pairs={{0,63},{1,0},{2,1},{3,2},{4,3},{5,4},{6,5},{7,6},{8,7},{9,8},{10,9... | collective-permute-start | bytes 196616 | tf_op jit(solution)/shard_map/while/body/eval_jaxpr/ppermute | solution.py:21
  2817.3 42.6 %collective-permute-start.2 = (bf16[2,128,128]{2,1,0:T(8,128)(2,1)}, bf16[2,128,128]{2,1,0:T(8,128)(2,1)S(1)}, u32[]{:S(2)}, u32[]{:S(2)}) collective-permute-start(bf16[2,128,128]{2,1,0:T(8,128)(2,1)} %get-tuple-element.1389), channel_id=1, source_target_pairs={{0,63},{1,0},{2,1},{3,2},{4,3},{5,4},{6,5},{7,6},{8,7},{9,8},{10,9... | collective-permute-start | bytes 196616 | tf_op jit(solution)/shard_map/while/body/eval_jaxpr/ppermute | solution.py:21
  3524.3 58.0 %collective-permute-start.102 = (f32[16,1536]{1,0:T(8,128)S(1)}, f32[16,1536]{1,0:T(8,128)S(1)}, u32[]{:S(2)}, u32[]{:S(2)}) collective-permute-start(f32[16,1536]{1,0:T(8,128)S(1)} %get-tuple-element.995), channel_id=1, source_target_pairs={{0,1},{1,2},{2,3},{3,4},{4,5},{5,6},{6,7},{7,8},{8,9},{9,10},{10,1... | collective-permute-start | bytes 294920
  3526.9 59.4 %collective-permute-start.103 = (f32[16,1536]{1,0:T(8,128)S(1)}, f32[16,1536]{1,0:T(8,128)S(1)}, u32[]{:S(2)}, u32[]{:S(2)}) collective-permute-start(f32[16,1536]{1,0:T(8,128)S(1)} %get-tuple-element.995), channel_id=1, source_target_pairs={{0,2},{1,3},{2,4},{3,5},{4,6},{5,7},{6,8},{7,9},{8,10},{9,11},{10,... | collective-permute-start | bytes 294920
  3701.0 125.6 %collective-permute-start.21 = (f32[16,1536]{1,0:T(8,128)S(1)}, f32[16,1536]{1,0:T(8,128)}, u32[]{:S(2)}, u32[]{:S(2)}) collective-permute-start(f32[16,1536]{1,0:T(8,128)S(1)} %get-tuple-element.992), channel_id=1, source_target_pairs={{0,16},{1,17},{2,18},{3,19},{4,20},{5,21},{6,22},{7,23},{8,24},{9,... | collective-permute-start | bytes 294920
  3703.2 128.8 %collective-permute-start.22 = (f32[16,1536]{1,0:T(8,128)S(1)}, f32[16,1536]{1,0:T(8,128)}, u32[]{:S(2)}, u32[]{:S(2)}) collective-permute-start(f32[16,1536]{1,0:T(8,128)S(1)} %get-tuple-element.992), channel_id=1, source_target_pairs={{0,17},{1,18},{2,19},{3,20},{4,21},{5,22},{6,23},{7,24},{8,25},{9,... | collective-permute-start | bytes 294920
  3705.5 128.4 %collective-permute-start.23 = (f32[16,1536]{1,0:T(8,128)S(1)}, f32[16,1536]{1,0:T(8,128)}, u32[]{:S(2)}, u32[]{:S(2)}) collective-permute-start(f32[16,1536]{1,0:T(8,128)S(1)} %get-tuple-element.992), channel_id=1, source_target_pairs={{0,18},{1,19},{2,20},{3,21},{4,22},{5,23},{6,24},{7,25},{8,26},{9,... | collective-permute-start | bytes 294920
  3707.4 132.6 %collective-permute-start.24 = (f32[16,1536]{1,0:T(8,128)S(1)}, f32[16,1536]{1,0:T(8,128)}, u32[]{:S(2)}, u32[]{:S(2)}) collective-permute-start(f32[16,1536]{1,0:T(8,128)S(1)} %get-tuple-element.992), channel_id=1, source_target_pairs={{0,19},{1,20},{2,21},{3,22},{4,23},{5,24},{6,25},{7,26},{8,27},{9,... | collective-permute-start | bytes 294920
  3710.8 130.9 %collective-permute-start.25 = (f32[16,1536]{1,0:T(8,128)S(1)}, f32[16,1536]{1,0:T(8,128)}, u32[]{:S(2)}, u32[]{:S(2)}) collective-permute-start(f32[16,1536]{1,0:T(8,128)S(1)} %get-tuple-element.992), channel_id=1, source_target_pairs={{0,20},{1,21},{2,22},{3,23},{4,24},{5,25},{6,26},{7,27},{8,28},{9,... | collective-permute-start | bytes 294920
  3845.6 65.1 %collective-permute-start.31 = (f32[16,1536]{1,0:T(8,128)S(1)}, f32[16,1536]{1,0:T(8,128)S(1)}, u32[]{:S(2)}, u32[]{:S(2)}) collective-permute-start(f32[16,1536]{1,0:T(8,128)S(1)} %get-tuple-element.992), channel_id=1, source_target_pairs={{0,26},{1,27},{2,28},{3,29},{4,30},{5,31},{6,32},{7,33},{8,34},{9,... | collective-permute-start | bytes 294920
  3847.9 64.2 %collective-permute-start.32 = (f32[16,1536]{1,0:T(8,128)S(1)}, f32[16,1536]{1,0:T(8,128)S(1)}, u32[]{:S(2)}, u32[]{:S(2)}) collective-permute-start(f32[16,1536]{1,0:T(8,128)S(1)} %get-tuple-element.992), channel_id=1, source_target_pairs={{0,27},{1,28},{2,29},{3,30},{4,31},{5,32},{6,33},{7,34},{8,35},{9,... | collective-permute-start | bytes 294920
  3851.3 62.9 %collective-permute-start.33 = (f32[16,1536]{1,0:T(8,128)S(1)}, f32[16,1536]{1,0:T(8,128)S(1)}, u32[]{:S(2)}, u32[]{:S(2)}) collective-permute-start(f32[16,1536]{1,0:T(8,128)S(1)} %get-tuple-element.992), channel_id=1, source_target_pairs={{0,28},{1,29},{2,30},{3,31},{4,32},{5,33},{6,34},{7,35},{8,36},{9,... | collective-permute-start | bytes 294920
  3854.7 61.2 %collective-permute-start.34 = (f32[16,1536]{1,0:T(8,128)S(1)}, f32[16,1536]{1,0:T(8,128)S(1)}, u32[]{:S(2)}, u32[]{:S(2)}) collective-permute-start(f32[16,1536]{1,0:T(8,128)S(1)} %get-tuple-element.992), channel_id=1, source_target_pairs={{0,29},{1,30},{2,31},{3,32},{4,33},{5,34},{6,35},{7,36},{8,37},{9,... | collective-permute-start | bytes 294920
  3856.4 62.7 %collective-permute-start.35 = (f32[16,1536]{1,0:T(8,128)S(1)}, f32[16,1536]{1,0:T(8,128)S(1)}, u32[]{:S(2)}, u32[]{:S(2)}) collective-permute-start(f32[16,1536]{1,0:T(8,128)S(1)} %get-tuple-element.992), channel_id=1, source_target_pairs={{0,30},{1,31},{2,32},{3,33},{4,34},{5,35},{6,36},{7,37},{8,38},{9,... | collective-permute-start | bytes 294920
  (582 other events, 19558.8 us)
Sparse Core Ops, SparseCore 0:
  11.0 71.9 all-gather.6
  124.8 68.3 all-gather.8
  1421.7 106.9 all-reduce.17
where the time goes:
time: 4020 us; the launch traced here: 3990 us
  starting transfers between devices  2210 us (55%)
  blocking collectives  706 us (18%)
  local copies, waits for them, and re-layouts  436 us (11%)
  other arithmetic  235 us (6%)
  matrix products  204 us (5%)
  waiting for transfers between devices  122 us (3%)
  loops' own time  54.5 us (1%)
    ppermute x198, starting transfers between devices, from_behind(): lax.ppermute(array, axis, [(i, (i + by) % length) for i in range(length)])  1790 us
    unnamed x3, blocking collectives  502 us
    unnamed x128, starting transfers between devices  370 us
    unnamed x367, local copies, waits for them, and re-layouts  184 us
  transfers between devices with their start and end apart: 339, of which 11 were waited for; matrix products, arithmetic and copies ran while one was open for 27% of the time, Pallas kernels for 0%

commit v1 on v0

v1 whole, which is shorter than its diff:
```python
import math

import jax
import jax.numpy as jnp
import numpy as np
from jax import lax
from jax.experimental import pallas as pl
from jax.experimental.pallas import tpu as pltpu
from jax.sharding import PartitionSpec as P

HEAD_SIZE = 128
GROUP = 6
HALF_WIDTH = GROUP * HEAD_SIZE
WINDOW = 4096
CAP = 24

NORM_EPS = 1e-06
ROPE_BASE = 1000000.0
MASKED = -1e30
SCALE = HEAD_SIZE ** (-0.5)
SCALE_LOG2 = SCALE * math.log2(math.e)

ALL = ("xh", "xl", "y", "z", "c")
CHIPS = ("xh", "xl", "y", "z")
HALF_CHIPS = ("xl", "y", "z")
PLANE_CHIPS = ("y", "z")
SWAP = [(0, 1), (1, 0)]

f32 = jnp.float32
bf16 = jnp.bfloat16


def dot(a, b, dims=((1,), (0,))):
    return lax.dot_general(a, b, (dims, ((), ())), preferred_element_type=f32)


NT = ((1,), (1,))
TN = ((0,), (0,))


def core_swap(value):
    return lax.ppermute(value, "c", SWAP)


def exchange(value, axes):
    return lax.all_to_all(value, axes, 0, 0, tiled=True)


def in_order(core, own, other):
    return jnp.concatenate([jnp.where(core == 0, own, other), jnp.where(core == 0, other, own)])


def doc_begin(positions, doc_starts):
    before = doc_starts[None, :] <= positions[:, None]
    return jnp.max(jnp.where(before, doc_starts[None, :], 0), axis=-1)


def rope_tables(offset):
    inv_freq = jnp.exp(
        jnp.arange(HEAD_SIZE // 2, dtype=f32) * (-2.0 * math.log(ROPE_BASE) / HEAD_SIZE)
    )
    angle = offset.astype(f32)[:, None] * inv_freq[None, :]
    cosine, sine = jnp.cos(angle), jnp.sin(angle)
    return jnp.concatenate([cosine, cosine], axis=1), jnp.concatenate([-sine, sine], axis=1)


def rotate(values, cosine, sine):
    half = HEAD_SIZE // 2
    turned = jnp.concatenate([values[..., half:], values[..., :half]], axis=-1)
    return values * cosine + turned * sine


def rotate_heads(values, cosine, sine):
    heads = values.reshape(values.shape[0], -1, HEAD_SIZE)
    return rotate(heads, cosine[:, None, :], sine[:, None, :]).reshape(values.shape)


def norm_backward(values, inverse, gain_row, incoming_grad):
    scaled = incoming_grad * gain_row
    input_grad = inverse * scaled - values * inverse * inverse * inverse * jnp.mean(
        scaled * values, axis=-1, keepdims=True
    )
    gain_grad = jnp.sum(incoming_grad * values * inverse, axis=0, keepdims=True)
    return (input_grad, gain_grad)


def allowed_pairs(start, first_query, low_ref, shape):
    key_pos = start + lax.broadcasted_iota(jnp.int32, shape, 0)
    query_pos = first_query + lax.broadcasted_iota(jnp.int32, shape, 1)
    return (key_pos >= low_ref[0:1, :]) & (key_pos <= query_pos)


def attend_kernel(meta_ref, low_ref, query_ref, keys_ref, own_ref, out_ref, low_out_ref, log_ref, score_ref):
    blocks, rows = keys_ref.shape[0] + 1, query_ref.shape[0]
    query = query_ref[...]

    def block_of(j):
        return own_ref if j == blocks - 1 else keys_ref.at[j]

    top = None
    for j in range(blocks):
        key = block_of(j)[:, :HEAD_SIZE]
        score_ref[j] = dot(key, query, NT)

        @pl.when(meta_ref[1, j] == 1)
        def _(j=j):
            allowed = allowed_pairs(meta_ref[0, j], meta_ref[0, blocks], low_ref, (rows, rows))
            score_ref[j] = jnp.where(allowed, score_ref[j], MASKED)

        part = jnp.max(score_ref[j].reshape(rows // 8, 8, rows), axis=0)
        top = part if top is None else jnp.maximum(top, part)
    top = jnp.max(top, axis=0, keepdims=True) * SCALE_LOG2
    total = jnp.zeros((8, rows), f32)
    mixed = jnp.zeros((HEAD_SIZE, rows), f32)
    for j in range(blocks):
        weights = jnp.exp2(score_ref[j] * SCALE_LOG2 - top)
        total = total + jnp.sum(weights.reshape(rows // 8, 8, rows), axis=0)
        mixed = mixed + dot(block_of(j)[:, HEAD_SIZE:], weights.astype(bf16), TN)
    total = jnp.sum(total, axis=0, keepdims=True)
    log_ref[0] = jnp.broadcast_to(top + jnp.log2(total), (8, rows))
    mixed = (mixed / total).T
    out_ref[...] = mixed
    low_out_ref[...] = mixed.astype(bf16)


def attend(meta, low, query, keys, own):
    blocks, rows = keys.shape[0] + 1, query.shape[0]
    whole = lambda *shape: pl.BlockSpec(shape, lambda h, meta: (0,) * len(shape))
    by_head = pl.BlockSpec((rows, HEAD_SIZE), lambda h, meta: (0, h))
    return pl.pallas_call(
        attend_kernel,
        grid_spec=pltpu.PrefetchScalarGridSpec(
            num_scalar_prefetch=1,
            grid=(GROUP,),
            in_specs=[whole(8, rows), by_head, whole(*keys.shape), whole(*own.shape)],
            out_specs=[by_head, by_head, pl.BlockSpec((1, 8, rows), lambda h, meta: (h, 0, 0))],
            scratch_shapes=[pltpu.VMEM((blocks, rows, rows), f32)],
        ),
        out_shape=[
            jax.ShapeDtypeStruct((rows, HALF_WIDTH), f32),
            jax.ShapeDtypeStruct((rows, HALF_WIDTH), bf16),
            jax.ShapeDtypeStruct((GROUP, 8, rows), f32),
        ],
        compiler_params=pltpu.CompilerParams(vmem_limit_bytes=48 * 1024 * 1024),
        name="attend",
    )(meta, low, query, keys, own)


def attend_back_kernel(
    meta_ref, low_ref, query_ref, keys_ref, out_ref, grad_ref, log_ref,
    query_grad_ref, keys_grad_ref, delta_ref, sum_ref,
):
    j, blocks, rows = pl.program_id(0), pl.num_programs(0), query_ref.shape[0]

    @pl.when(j == 0)
    def _():
        sum_ref[...] = jnp.zeros_like(sum_ref)
        for h in range(GROUP):
            at = slice(h * HEAD_SIZE, (h + 1) * HEAD_SIZE)
            product = (grad_ref[:, at].astype(f32) * out_ref[:, at]).T
            delta_ref[h] = jnp.broadcast_to(jnp.sum(product, axis=0, keepdims=True), (8, rows))

    key, value = keys_ref[0, :, :HEAD_SIZE], keys_ref[0, :, HEAD_SIZE:]

    def step(masked):
        key_grad = jnp.zeros((rows, HEAD_SIZE), f32)
        value_grad = jnp.zeros((rows, HEAD_SIZE), f32)
        turned_key = key.T
        for h in range(GROUP):
            at = slice(h * HEAD_SIZE, (h + 1) * HEAD_SIZE)
            query, out_grad = query_ref[:, at], grad_ref[:, at]
            weights = jnp.exp2(dot(key, query, NT) * SCALE_LOG2 - log_ref[h, 0:1, :])
            if masked:
                allowed = allowed_pairs(meta_ref[0, j], meta_ref[0, blocks], low_ref, (rows, rows))
                weights = jnp.where(allowed, weights, 0.0)
            score_grad = (weights * (dot(value, out_grad, NT) - delta_ref[h, 0:1, :])).astype(bf16)
            sum_ref[h] = sum_ref[h] + dot(turned_key, score_grad)
            key_grad = key_grad + dot(score_grad, query)
            value_grad = value_grad + dot(weights.astype(bf16), out_grad)
        keys_grad_ref[0, :, :HEAD_SIZE] = (key_grad * SCALE).astype(bf16)
        keys_grad_ref[0, :, HEAD_SIZE:] = value_grad.astype(bf16)

    @pl.when(meta_ref[1, j] == 1)
    def _():
        step(True)

    @pl.when(meta_ref[1, j] == 0)
    def _():
        step(False)

    @pl.when(j == blocks - 1)
    def _():
        for h in range(GROUP):
            query_grad_ref[:, h * HEAD_SIZE : (h + 1) * HEAD_SIZE] = (sum_ref[h] * SCALE).T


def attend_back(meta, low, query, keys, out, out_grad, log_total):
    blocks, rows = keys.shape[0], query.shape[0]
    whole = lambda *shape: pl.BlockSpec(shape, lambda j, meta: (0,) * len(shape))
    by_block = pl.BlockSpec((1, rows, 2 * HEAD_SIZE), lambda j, meta: (j, 0, 0))
    wide = whole(rows, HALF_WIDTH)
    return pl.pallas_call(
        attend_back_kernel,
        grid_spec=pltpu.PrefetchScalarGridSpec(
            num_scalar_prefetch=1,
            grid=(blocks,),
            in_specs=[whole(8, rows), wide, by_block, wide, wide, whole(GROUP, 8, rows)],
            out_specs=[wide, by_block],
            scratch_shapes=[
                pltpu.VMEM((GROUP, 8, rows), f32),
                pltpu.VMEM((GROUP, HEAD_SIZE, rows), f32),
            ],
        ),
        out_shape=[
            jax.ShapeDtypeStruct((rows, HALF_WIDTH), f32),
            jax.ShapeDtypeStruct(keys.shape, bf16),
        ],
        compiler_params=pltpu.CompilerParams(vmem_limit_bytes=48 * 1024 * 1024),
        name="attend_back",
    )(meta, low, query, keys, out, out_grad, log_total)


def to_column_halves(value, half, core):
    width = value.shape[1] // 2
    left, right = value[:, :width], value[:, width:]
    same = lax.ppermute(
        jnp.where(core == 0, left, right), ("xh", "c"), [(a * 2 + k, k * 2 + a) for a in range(2) for k in range(2)]
    )
    cross = lax.ppermute(
        jnp.where(core == 0, right, left), ("xh", "c"), [(a * 2 + k, (1 - k) * 2 + a) for a in range(2) for k in range(2)]
    )
    return jnp.concatenate([jnp.where(half == 0, same, cross), jnp.where(half == 0, cross, same)])


def from_column_halves(value, half, core):
    rows = value.shape[0] // 2
    upper, lower = value[:rows], value[rows:]
    same = lax.ppermute(
        jnp.where(half == 0, upper, lower), ("xh", "c"), [(h * 2 + c, c * 2 + h) for h in range(2) for c in range(2)]
    )
    cross = lax.ppermute(
        jnp.where(half == 0, lower, upper), ("xh", "c"), [(h * 2 + c, c * 2 + 1 - h) for h in range(2) for c in range(2)]
    )
    return jnp.concatenate(
        [jnp.where(core == 0, same, cross), jnp.where(core == 0, cross, same)], axis=1
    )


def body(
    acts, teacher, valid, doc_starts, routes, gates,
    w_query, key_weight, value_weight, w_out, gain_attn, gain_ffn, w_gate, w_up, w_down,
):
    half, core = lax.axis_index("xh"), lax.axis_index("c")
    plane, spot = lax.axis_index(("xh", "xl")), lax.axis_index(PLANE_CHIPS)
    chip = lax.axis_index(CHIPS)
    tok_rows, model_dim = acts.shape
    chip_rows = 2 * tok_rows
    spots = lax.axis_size(PLANE_CHIPS)
    planes = lax.axis_size(("xh", "xl"))
    chips = spots * planes
    total_tokens = chips * chip_rows
    shard_rows = w_query.shape[0]

    gain_pair = jnp.pad(jnp.stack([gain_attn, gain_ffn], axis=1), ((0, 0), (0, HEAD_SIZE - 2)))
    by_core = jnp.stack(
        [
            jnp.concatenate(
                [
                    key_weight[:, k * HEAD_SIZE : (k + 1) * HEAD_SIZE],
                    value_weight[:, k * HEAD_SIZE : (k + 1) * HEAD_SIZE],
                    gain_pair,
                    w_query[:, k * HALF_WIDTH : (k + 1) * HALF_WIDTH],
                ],
                axis=1,
            )
            for k in range(2)
        ]
    )
    own_weights = exchange(by_core, "c").reshape(2 * shard_rows, -1)
    kv_width = 3 * HEAD_SIZE
    kv_part, query_part = own_weights[:, :kv_width], own_weights[:, kv_width:]
    full_kv = exchange(jnp.broadcast_to(kv_part[None], (chips,) + kv_part.shape), CHIPS).reshape(
        model_dim, kv_width
    )
    out_part = to_column_halves(w_out, half, core)
    gathered = lax.all_gather(jnp.concatenate([query_part, out_part], axis=1), CHIPS)
    full_query = gathered.reshape(model_dim, -1)[:, :HALF_WIDTH]
    full_out = gathered.reshape(2, HALF_WIDTH, -1)[:, :, HALF_WIDTH:]

    pick = (np.arange(kv_width)[None, :] == 2 * HEAD_SIZE + np.arange(2)[:, None]).astype(np.float32)
    gain_rows = dot(jnp.asarray(pick, bf16), full_kv, NT)
    gain_one, gain_two = gain_rows[0:1], gain_rows[1:2]

    first_token = chip * chip_rows
    chip_pos = first_token + jnp.arange(chip_rows, dtype=jnp.int32)
    begin = doc_begin(chip_pos, doc_starts)
    cosine, sine = rope_tables(chip_pos - begin)
    low = jnp.maximum(begin, chip_pos - (WINDOW - 1))
    low_rows = jnp.broadcast_to(low[None, :], (8, chip_rows))
    block_at = jnp.arange(spots, dtype=jnp.int32)
    block_plane = jnp.where(block_at < spot, plane, plane - 1)
    starts = jnp.concatenate([(block_plane * spots + block_at) * chip_rows, first_token[None]])
    needs_mask = ((starts < jnp.max(low)) | (starts + chip_rows > first_token)).astype(jnp.int32)
    meta = jnp.stack(
        [
            jnp.concatenate([starts, first_token[None]]),
            jnp.concatenate([needs_mask, jnp.zeros((1,), jnp.int32)]),
        ]
    )

    experts = 32
    all_slots = experts * CAP
    flat_routes = routes.reshape(-1)
    chosen = (flat_routes[:, None] == jnp.arange(experts, dtype=jnp.int32)[None, :]).astype(jnp.int32)
    slot_index = jnp.sum((jnp.cumsum(chosen, axis=0) - chosen) * chosen, axis=1)
    target = (flat_routes * CAP + slot_index).reshape(routes.shape)
    hits = target[None, :, :] == jnp.arange(all_slots, dtype=jnp.int32)[:, None, None]
    placed = jnp.any(hits, axis=2).astype(bf16)
    slot_gate = jnp.sum(jnp.where(hits, gates[None], 0.0), axis=(1, 2))[:, None]
    hits_by_token = target[:, None, :] == jnp.arange(all_slots, dtype=jnp.int32)[None, :, None]
    token_gate = jnp.sum(jnp.where(hits_by_token, gates[:, None, :], 0.0), axis=2)
    token_gate_high = token_gate.astype(bf16)
    token_gate_low = (token_gate - token_gate_high.astype(f32)).astype(bf16)
    placed_by_token = jnp.any(hits_by_token, axis=2).astype(bf16)

    chip_acts = in_order(core, acts, core_swap(acts)).astype(f32)
    inverse_one = lax.rsqrt(jnp.mean(chip_acts * chip_acts, axis=-1, keepdims=True) + NORM_EPS)
    normed_one = (chip_acts * inverse_one * gain_one).astype(bf16)
    kv_lin = dot(normed_one, full_kv[:, : 2 * HEAD_SIZE])
    key_seq = rotate(kv_lin[:, :HEAD_SIZE], cosine, sine).astype(bf16)
    own_kv = jnp.concatenate([key_seq, kv_lin[:, HEAD_SIZE:].astype(bf16)], axis=1)
    before_kv = lax.ppermute(own_kv, ("xh", "xl"), [(p, p + 1) for p in range(planes - 1)])
    later = (block_at > spot)[:, None, None]
    seen_kv = exchange(jnp.where(later, own_kv[None], before_kv[None]), PLANE_CHIPS)
    query_lin = dot(normed_one, full_query)
    query_seq = rotate_heads(query_lin, cosine, sine).astype(bf16)
    attn_wide, attn, log_total = attend(meta, low_rows, query_seq, seen_kv, own_kv)

    branch = jnp.concatenate([dot(attn, full_out[0]), dot(attn, full_out[1])], axis=1)
    upper, lower = branch[:tok_rows], branch[tok_rows:]
    branch = jnp.where(core == 0, upper, lower) + core_swap(jnp.where(core == 0, lower, upper))
    values_in = acts.astype(f32)
    hidden_one = values_in + branch
    inverse_two = lax.rsqrt(jnp.mean(hidden_one * hidden_one, axis=-1, keepdims=True) + NORM_EPS)
    normed_two = (hidden_one * inverse_two * gain_two).astype(bf16)

    def to_experts(rows):
        mine = exchange(rows.reshape(experts, CAP, model_dim), HALF_CHIPS).reshape(all_slots, model_dim)
        return mine, core_swap(mine)

    def from_experts(mine, theirs):
        both = mine + core_swap(theirs.astype(bf16)).astype(f32)
        both = both.astype(bf16).reshape(experts, CAP, model_dim)
        return exchange(both, HALF_CHIPS).reshape(all_slots, model_dim)

    def expert_forward(rows):
        gate_pre, up_pre = dot(rows, w_gate), dot(rows, w_up)
        hidden = (jax.nn.silu(gate_pre) * up_pre).astype(bf16)
        return gate_pre, up_pre, hidden, dot(hidden, w_down)

    def expert_backward(kept, grad_rows):
        gate_pre, up_pre = kept[0], kept[1]
        grad_hidden = dot(grad_rows, w_down, NT)
        sigmoid = jax.nn.sigmoid(gate_pre)
        grad_gate = (grad_hidden * up_pre * sigmoid * (1.0 + gate_pre * (1.0 - sigmoid))).astype(bf16)
        grad_up = (grad_hidden * gate_pre * sigmoid).astype(bf16)
        return grad_gate, grad_up, dot(grad_gate, w_gate, NT) + dot(grad_up, w_up, NT)

    rows_mine, rows_theirs = to_experts(dot(placed, normed_two).astype(bf16))
    kept_theirs = expert_forward(rows_theirs)
    kept_mine = expert_forward(rows_mine)
    returned = from_experts(kept_mine[3], kept_theirs[3])
    mixture = dot(token_gate_high, returned) + dot(token_gate_low, returned)
    hidden_two = hidden_one + mixture

    valid_count = valid[0]
    own_pos = first_token + core * tok_rows + jnp.arange(tok_rows, dtype=jnp.int32)
    grad_two = jnp.where(
        (own_pos < valid_count)[:, None],
        total_tokens / valid_count.astype(f32) * (hidden_two - teacher.astype(f32)),
        0.0,
    )
    grad_two_high = grad_two.astype(bf16)
    grad_two_low = (grad_two - grad_two_high.astype(f32)).astype(bf16)
    grad_slots = (slot_gate * (dot(placed, grad_two_high) + dot(placed, grad_two_low))).astype(bf16)
    grads_mine, grads_theirs = to_experts(grad_slots)
    back_theirs = expert_backward(kept_theirs, grads_theirs)
    back_mine = expert_backward(kept_mine, grads_mine)
    grad_returned = from_experts(back_mine[2], back_theirs[2])

    def both_halves(partial):
        partial = partial.astype(bf16)
        return partial.astype(f32) + lax.ppermute(partial, "xh", SWAP).astype(f32)

    grad_w_down = both_halves(dot(kept_mine[2], grads_mine, TN) + dot(kept_theirs[2], grads_theirs, TN))
    grad_w_gate = both_halves(dot(rows_mine, back_mine[0], TN) + dot(rows_theirs, back_theirs[0], TN))
    grad_w_up = both_halves(dot(rows_mine, back_mine[1], TN) + dot(rows_theirs, back_theirs[1], TN))

    grad_normed_two = dot(placed_by_token, grad_returned)
    norm_two_grad, gain_two_grad = norm_backward(hidden_one, inverse_two, gain_two, grad_normed_two)
    grad_one = grad_two + norm_two_grad
    grad_branch = grad_one.astype(bf16)
    chip_branch = in_order(core, grad_branch, core_swap(grad_branch))
    left, right = chip_branch[:, :HALF_WIDTH], chip_branch[:, HALF_WIDTH:]
    grad_attn = (dot(left, full_out[0], NT) + dot(right, full_out[1], NT)).astype(bf16)

    def chip_sums(partial):
        pieces = partial.astype(bf16).reshape(chips, 2 * shard_rows, -1)
        return jnp.sum(exchange(pieces, CHIPS).astype(f32), axis=0)

    out_sums = chip_sums(jnp.stack([dot(attn, left, TN), dot(attn, right, TN)]))
    grad_w_out = from_column_halves(out_sums, half, core)

    every_kv = jnp.concatenate([seen_kv, own_kv[None]])
    query_grad, kv_grad = attend_back(
        meta, low_rows, query_seq, every_kv, attn_wide, grad_attn, log_total
    )
    query_lin_grad = rotate_heads(query_grad.astype(bf16).astype(f32), cosine, -sine).astype(bf16)
    came = exchange(kv_grad[:spots], PLANE_CHIPS).astype(f32)
    from_later = jnp.sum(jnp.where((block_at > spot)[:, None, None], came, 0.0), axis=0)
    from_before = jnp.sum(jnp.where((block_at <= spot)[:, None, None], came, 0.0), axis=0)
    from_next = lax.ppermute(from_before, ("xh", "xl"), [(p + 1, p) for p in range(planes - 1)])
    kv_sum = (from_later + from_next + kv_grad[spots].astype(f32)).astype(bf16)
    key_lin_grad = rotate(kv_sum[:, :HEAD_SIZE].astype(f32), cosine, -sine).astype(bf16)
    kv_lin_grad = jnp.concatenate([key_lin_grad, kv_sum[:, HEAD_SIZE:]], axis=1)

    normed_grad = dot(query_lin_grad, full_query, NT) + dot(kv_lin_grad, full_kv[:, : 2 * HEAD_SIZE], NT)
    upper, lower = normed_grad[:tok_rows], normed_grad[tok_rows:]
    normed_grad = jnp.where(core == 0, upper, lower) + core_swap(jnp.where(core == 0, lower, upper))
    own_inverse = jnp.where(core == 0, inverse_one[:tok_rows], inverse_one[tok_rows:])
    input_norm_grad, gain_one_grad = norm_backward(values_in, own_inverse, gain_one, normed_grad)
    grad_acts = grad_one + input_norm_grad

    query_sums = chip_sums(dot(normed_one, query_lin_grad, TN))
    gain_grads = jnp.concatenate([gain_one_grad, gain_two_grad]).astype(bf16)
    gain_columns = dot(gain_grads, jnp.asarray(np.eye(2, HEAD_SIZE), bf16), TN)
    kv_sums = chip_sums(jnp.concatenate([dot(normed_one, kv_lin_grad, TN), gain_columns], axis=1))
    sums = jnp.concatenate([kv_sums, query_sums], axis=1).reshape(2, shard_rows, -1)
    sums = exchange(sums, "c")

    def columns(begin_at, width):
        return jnp.concatenate([sums[k, :, begin_at : begin_at + width] for k in range(2)], axis=1)

    gain_sums = sums[0, :, 2 * HEAD_SIZE : 2 * HEAD_SIZE + 2] + sums[1, :, 2 * HEAD_SIZE : 2 * HEAD_SIZE + 2]
    return (
        hidden_two.astype(bf16),
        grad_acts,
        columns(kv_width, HALF_WIDTH),
        columns(0, HEAD_SIZE),
        columns(HEAD_SIZE, HEAD_SIZE),
        grad_w_out,
        gain_sums[:, 0],
        gain_sums[:, 1],
        grad_w_gate,
        grad_w_up,
        grad_w_down,
    )


def solution(mesh):
    fine_mesh = jax.sharding.Mesh(mesh.devices.reshape(2, 2, 4, 4, 2), ALL)
    rows, vector = P(ALL, None), P(ALL)
    wide, tall = P(None, ("xl", "y", "z", "c")), P(("xl", "y", "z", "c"), None)
    return jax.shard_map(
        body,
        mesh=fine_mesh,
        in_specs=(
            rows, rows, P(), P(), rows, rows, rows, rows, rows, rows, vector, vector, wide, wide, tall,
        ),
        out_specs=(rows, rows, rows, rows, rows, rows, vector, vector, wide, wide, tall),
        check_vma=False,
    )
```

time: 4020 us -> 579 us (0.14)
  starting transfers between devices: 2210 us -> 93.7 us
  blocking collectives: 706 us -> 78.5 us
  local copies, waits for them, and re-layouts: 436 us -> 31.1 us
  other arithmetic: 235 us -> 55 us
  matrix products: 204 us -> 69.5 us
  Pallas kernels: 0 us -> 67.3 us
  loops' own time: 54.5 us -> 0 us
    ppermute x198 -> x17, starting transfers between devices: 1790 us -> 34.5 us  [the longest x8 14 us: core_swap(): return lax.ppermute(value, 'c', SWAP)]
    unnamed x3 -> x0, blocking collectives: 502 us -> none
    unnamed x128 -> x0, starting transfers between devices: 370 us -> none
    unnamed x367 -> x164, local copies, waits for them, and re-layouts: 184 us -> 6.6 us
    dot_general x253 -> x37, matrix products: 204 us -> 69.5 us  [dot(): return lax.dot_general(a, b, (dims, ((), ())), preferred_element_type=f32)]
    convert_element_type x144 -> x8, other arithmetic: 108 us -> 7.29 us  [the longest x1 2.49 us: body(): query_seq = rotate_heads(query_lin, cosine, sine).astype(bf16)]
    all_gather x2 -> x0, blocking collectives: 71.1 us -> none  [the longest x1 36 us: body(): lax.all_gather(value_weight, ('head', 'blk'), axis=0, tiled=True)]
    another operation x70 -> x1, local copies, waits for them, and re-layouts: 69.7 us -> 0.01 us
  transfers between devices with their start and end apart: 339 -> 27, of which waited for: 11 -> 15; matrix products, arithmetic and copies ran while one was open for 27% -> 20% of each run, Pallas kernels for 0% -> 6%
where the time goes in v1:
time: 579 us; the launch traced here: 569 us
  waiting for transfers between devices  158 us (27%)
  starting transfers between devices  93.7 us (16%)
  blocking collectives  78.5 us (14%)
  matrix products  69.5 us (12%)
  Pallas kernels  67.3 us (12%)
  other arithmetic  55 us (9%)
  local copies, waits for them, and re-layouts  31.1 us (5%)
  between operations  16.4 us (3%)
    all_to_all x9, waiting for transfers between devices, exchange(): return lax.all_to_all(value, axes, 0, 0, tiled=True)  103 us
    all_to_all x3, blocking collectives, exchange(): return lax.all_to_all(value, axes, 0, 0, tiled=True)  78.5 us
    dot_general x37, matrix products, dot(): return lax.dot_general(a, b, (dims, ((), ())), preferred_element_type=f32)  69.5 us
    all_to_all x9, starting transfers between devices, exchange(): return lax.all_to_all(value, axes, 0, 0, tiled=True)  59.1 us
    all_gather x1, waiting for transfers between devices, body(): lax.all_gather(jnp.concatenate([query_part, out_part], axis=1), CHIPS)  43.2 us
    pallas_call x1, Pallas kernels, attend_back(): pl.pallas_call(attend_back_kernel, grid_spec=pltpu.PrefetchScalarGridSpec...  36 us
    pallas_call x1, Pallas kernels, attend(): pl.pallas_call(attend_kernel, grid_spec=pltpu.PrefetchScalarGridSpec(num_...  31.4 us
    ppermute x8, starting transfers between devices, core_swap(): return lax.ppermute(value, 'c', SWAP)  14 us
  transfers between devices with their start and end apart: 27, of which 15 were waited for; matrix products, arithmetic and copies ran while one was open for 20% of the time, Pallas kernels for 6%

profile of v1, /device:TPU:1, one launch (start us, length us, event | category | flops | bytes accessed | tf_op | source)
XLA Modules:
  0.0 569.3 jit_solution(8732493283653563558)
XLA Ops:
  8.1 6.0 %collective-permute-start.1 = (bf16[12,768]{1,0:T(8,128)(2,1)S(1)}, bf16[12,768]{1,0:T(8,128)(2,1)S(1)}, u32[]{:S(2)}, u32[]{:S(2)}) collective-permute-start(bf16[12,768]{1,0:T(8,128)(2,1)S(1)} %get-tuple-element.75), channel_id=1, source_target_pairs={{0,0},{1,64},{64,1},{65,65},{2,2},{3,66},{66,3},{67,67},{4,4},{5,6... | collective-permute-start | bytes 55304 | tf_op jit(solution)/shard_map/ppermute | solution.py:226
  24.2 11.1 %all-to-all-start.1 = ((bf16[64,24,384]{2,1,0:T(8,128)(2,1)}), bf16[64,24,384]{2,1,0:T(8,128)(2,1)S(1)}, u32[]{:S(2)}, u32[]{:S(2)}) async-start(bf16[64,24,384]{2,1,0:T(8,128)(2,1)} %broadcast_in_dim.151), calls=%async_computation.1 | async-start | bytes 2359296 | tf_op jit(solution)/shard_map/all_to_all | solution.py:46
  39.8 14.5 %all-to-all-done.1 = bf16[64,24,384]{2,1,0:T(8,128)(2,1)S(1)} async-done(((bf16[64,24,384]{2,1,0:T(8,128)(2,1)}), bf16[64,24,384]{2,1,0:T(8,128)(2,1)S(1)}, u32[]{:S(2)}, u32[]{:S(2)}) %all-to-all-start.1) | async-done | bytes 1179680 | tf_op jit(solution)/shard_map/all_to_all | solution.py:46
  75.6 43.2 %all-gather.3.cloned.1.call-done = bf16[1536,1536]{1,0:T(8,128)(2,1)} async-done(((bf16[24,1536]{1,0:T(8,128)(2,1)}), bf16[1536,1536]{1,0:T(8,128)(2,1)}) %all-gather.3.cloned.1.call-update) | async-done | bytes 4718608 | tf_op jit(solution)/shard_map/all_gather | solution.py:286
  132.7 31.4 %attend.1 = (f32[256,768]{1,0:T(8,128)S(1)}, bf16[256,768]{1,0:T(8,128)(2,1)S(1)}, f32[6,8,256]{2,1,0:T(8,128)S(1)}) custom-call(s32[2,18]{1,0:T(2,128)S(1)} %pad_add_fusion.meta_ref, s32[8,256]{1,0:T(8,128)S(1)} %broadcast_in_dim.150.low_ref, bf16[256,768]{1,0:T(8,128)(2,1)S(1)} %copy-done.4, bf16[16,256,256]{2,1,0:T(8,128)(2,1)S(1)} %all-to-all-done.2.keys_ref, ...), custom_call_target="tpu_custom_call" | custom-call | tf_op jit(solution)/shard_map/attend/pallas_call | solution.py:130
  177.4 34.0 %all_to_all.60 = bf16[32,24,1536]{2,1,0:T(8,128)(2,1)S(1)} all-to-all(bf16[32,24,1536]{2,1,0:T(8,128)(2,1)S(1)} %bitcast.138), channel_id=1, replica_groups=mesh['xh'=2,'xl'=2,'y'=4,'z'=4,'c'=2] {'xl','y','z'}, dimensions={0} | all-to-all | bytes 4718592 | tf_op jit(solution)/shard_map/all_to_all | solution.py:46
  213.1 4.2 collective-permute-done.5
  229.9 4.9 all-to-all-start.4
  236.8 28.1 %all-to-all-done.4 = bf16[32,24,1536]{2,1,0:T(8,128)(2,1)} async-done(((bf16[32,24,1536]{2,1,0:T(8,128)(2,1)}), bf16[32,24,1536]{2,1,0:T(8,128)(2,1)}, u32[]{:S(2)}, u32[]{:S(2)}) %all-to-all-start.4) | async-done | bytes 2359328 | tf_op jit(solution)/shard_map/all_to_all | solution.py:46
  271.4 37.1 %all_to_all.61 = bf16[32,24,1536]{2,1,0:T(8,128)(2,1)S(1)} all-to-all(bf16[32,24,1536]{2,1,0:T(8,128)(2,1)S(1)} %bitcast.143), channel_id=1, replica_groups=mesh['xh'=2,'xl'=2,'y'=4,'z'=4,'c'=2] {'xl','y','z'}, dimensions={0} | all-to-all | bytes 4718592 | tf_op jit(solution)/shard_map/all_to_all | solution.py:46
  328.2 4.9 all-to-all-start.6
  350.3 12.9 %all-to-all-done.6 = bf16[32,24,1536]{2,1,0:T(8,128)(2,1)} async-done(((bf16[32,24,1536]{2,1,0:T(8,128)(2,1)}), bf16[32,24,1536]{2,1,0:T(8,128)(2,1)}, u32[]{:S(2)}, u32[]{:S(2)}) %all-to-all-start.6) | async-done | bytes 2359328 | tf_op jit(solution)/shard_map/all_to_all | solution.py:46
  376.3 36.0 %attend_back.1 = (f32[256,768]{1,0:T(8,128)S(1)}, bf16[17,256,256]{2,1,0:T(8,128)(2,1)S(1)}) custom-call(s32[2,18]{1,0:T(2,128)S(1)} %pad_add_fusion.meta_ref, s32[8,256]{1,0:T(8,128)S(1)} %broadcast_in_dim.150.low_ref, bf16[256,768]{1,0:T(8,128)(2,1)S(1)} %copy-done.5, bf16[17,256,256]{2,1,0:T(8,128)(2,1)} %pad_maximum_fusion.1.keys_ref, ...), custom_call_target="tpu_custom_call" | custom-call | tf_op jit(solution)/shard_map/attend_back/pallas_call | solution.py:202
  413.8 4.6 all-to-all-start.7
  418.4 5.1 fusion.2
  433.0 14.7 %all-to-all-done.7 = bf16[16,256,256]{2,1,0:T(8,128)(2,1)} async-done(((bf16[16,256,256]{2,1,0:T(8,128)(2,1)}), bf16[16,256,256]{2,1,0:T(8,128)(2,1)}, u32[]{:S(2)}, u32[]{:S(2)}) %all-to-all-start.7) | async-done | bytes 2097184 | tf_op jit(solution)/shard_map/all_to_all | solution.py:46
  447.7 7.2 %all-to-all-start.11 = ((bf16[64,24,768]{2,1,0:T(8,128)(2,1)}), bf16[64,24,768]{2,1,0:T(8,128)(2,1)}, u32[]{:S(2)}, u32[]{:S(2)}) async-start(bf16[64,24,768]{2,1,0:T(8,128)(2,1)} %bitcast.137), calls=%async_computation.11 | async-start | bytes 4718592 | tf_op jit(solution)/shard_map/all_to_all | solution.py:46
  477.3 6.3 %all-to-all-done.11 = bf16[64,24,768]{2,1,0:T(8,128)(2,1)} async-done(((bf16[64,24,768]{2,1,0:T(8,128)(2,1)}), bf16[64,24,768]{2,1,0:T(8,128)(2,1)}, u32[]{:S(2)}, u32[]{:S(2)}) %all-to-all-start.11) | async-done | bytes 2359328 | tf_op jit(solution)/shard_map/all_to_all | solution.py:46
  483.6 8.8 %all-to-all-start.9 = ((bf16[64,24,768]{2,1,0:T(8,128)(2,1)}), bf16[64,24,768]{2,1,0:T(8,128)(2,1)}, u32[]{:S(2)}, u32[]{:S(2)}) async-start(bf16[64,24,768]{2,1,0:T(8,128)(2,1)} %bitcast.163), calls=%async_computation.9 | async-start | bytes 4718592 | tf_op jit(solution)/shard_map/all_to_all | solution.py:46
  503.7 4.8 collective-permute-start.12
  508.5 11.4 %all-to-all-done.9 = bf16[64,24,768]{2,1,0:T(8,128)(2,1)} async-done(((bf16[64,24,768]{2,1,0:T(8,128)(2,1)}), bf16[64,24,768]{2,1,0:T(8,128)(2,1)}, u32[]{:S(2)}, u32[]{:S(2)}) %all-to-all-start.9) | async-done | bytes 2359328 | tf_op jit(solution)/shard_map/all_to_all | solution.py:46
  524.7 10.1 %all-to-all-start.8 = ((bf16[64,24,384]{2,1,0:T(8,128)(2,1)}), bf16[64,24,384]{2,1,0:T(8,128)(2,1)S(1)}, u32[]{:S(2)}, u32[]{:S(2)}) async-start(bf16[64,24,384]{2,1,0:T(8,128)(2,1)} %pad_maximum_fusion.2), calls=%async_computation.8 | async-start | bytes 2359296 | tf_op jit(solution)/shard_map/all_to_all | solution.py:46
  538.1 13.9 %all-to-all-done.8 = bf16[64,24,384]{2,1,0:T(8,128)(2,1)S(1)} async-done(((bf16[64,24,384]{2,1,0:T(8,128)(2,1)}), bf16[64,24,384]{2,1,0:T(8,128)(2,1)S(1)}, u32[]{:S(2)}, u32[]{:S(2)}) %all-to-all-start.8) | async-done | bytes 1179680 | tf_op jit(solution)/shard_map/all_to_all | solution.py:46
  552.2 7.3 %all_to_all.62 = f32[2,12,1152]{2,1,0:T(8,128)S(1)} all-to-all(f32[2,12,1152]{2,1,0:T(8,128)S(1)} %reshape.255), channel_id=1, replica_groups=mesh['xh'=2,'xl'=2,'y'=4,'z'=4,'c'=2] {'c'}, dimensions={0} | all-to-all | bytes 221184 | tf_op jit(solution)/shard_map/all_to_all | solution.py:46
  (347 shorter events, 190.5 us)
Async XLA Ops:
  8.1 13.9 %collective-permute-start.1 = (bf16[12,768]{1,0:T(8,128)(2,1)S(1)}, bf16[12,768]{1,0:T(8,128)(2,1)S(1)}, u32[]{:S(2)}, u32[]{:S(2)}) collective-permute-start(bf16[12,768]{1,0:T(8,128)(2,1)S(1)} %get-tuple-element.75), channel_id=1, source_target_pairs={{0,0},{1,64},{64,1},{65,65},{2,2},{3,66},{66,3},{67,67},{4,4},{5,6... | collective-permute-start | bytes 55304 | tf_op jit(solution)/shard_map/ppermute | solution.py:226
  14.1 7.9 %collective-permute-start.2 = (bf16[12,768]{1,0:T(8,128)(2,1)S(1)}, bf16[12,768]{1,0:T(8,128)(2,1)S(1)}, u32[]{:S(2)}, u32[]{:S(2)}) collective-permute-start(bf16[12,768]{1,0:T(8,128)(2,1)S(1)} %get-tuple-element.76), channel_id=1, source_target_pairs={{0,64},{1,0},{64,65},{65,1},{2,66},{3,2},{66,67},{67,3},{4,68},{5,... | collective-permute-start | bytes 55304 | tf_op jit(solution)/shard_map/ppermute | solution.py:229
  17.1 4.8 all-to-all-start
  20.8 98.0 %all-gather.3.cloned.1.call-start = ((), (), s32[]{:S(2)}) async-start(), calls=%async_computation.12 | async-start | bytes 4792320 | tf_op jit(solution)/shard_map/all_gather | solution.py:286
  22.7 15.3 %collective-permute-start = (bf16[128,1536]{1,0:T(8,128)(2,1)}, bf16[128,1536]{1,0:T(8,128)(2,1)}, u32[]{:S(2)}, u32[]{:S(2)}) collective-permute-start(bf16[128,1536]{1,0:T(8,128)(2,1)} %param.17), channel_id=1, source_target_pairs={{0,1},{1,0},{2,3},{3,2},{4,5},{5,4},{6,7},{7,6},{8,9},{9,8},{10,11... | collective-permute-start | bytes 1179656 | tf_op jit(solution)/shard_map/ppermute | solution.py:42
  24.2 30.1 %all-to-all-start.1 = ((bf16[64,24,384]{2,1,0:T(8,128)(2,1)}), bf16[64,24,384]{2,1,0:T(8,128)(2,1)S(1)}, u32[]{:S(2)}, u32[]{:S(2)}) async-start(bf16[64,24,384]{2,1,0:T(8,128)(2,1)} %broadcast_in_dim.151), calls=%async_computation.1 | async-start | bytes 2359296 | tf_op jit(solution)/shard_map/all_to_all | solution.py:46
  63.3 68.4 %all-to-all-start.2 = ((bf16[16,256,256]{2,1,0:T(8,128)(2,1)}), bf16[16,256,256]{2,1,0:T(8,128)(2,1)S(1)}, u32[]{:S(2)}, u32[]{:S(2)}) async-start(bf16[16,256,256]{2,1,0:T(8,128)(2,1)} %broadcast_select_fusion), calls=%async_computation.2 | async-start | bytes 4194304 | tf_op jit(solution)/shard_map/all_to_all | solution.py:46
  169.4 5.0 collective-permute-start.4
  211.4 5.8 %collective-permute-start.5 = (bf16[768,1536]{1,0:T(8,128)(2,1)S(1)}, bf16[768,1536]{1,0:T(8,128)(2,1)S(1)}, u32[]{:S(2)}, u32[]{:S(2)}) collective-permute-start(bf16[768,1536]{1,0:T(8,128)(2,1)S(1)} %bitcast.158), channel_id=1, source_target_pairs={{0,1},{1,0},{2,3},{3,2},{4,5},{5,4},{6,7},{7,6},{8,9},{9,8},{10,11... | collective-permute-start | bytes 7077896 | tf_op jit(solution)/shard_map/ppermute | solution.py:42
  229.9 35.0 %all-to-all-start.4 = ((bf16[32,24,1536]{2,1,0:T(8,128)(2,1)}), bf16[32,24,1536]{2,1,0:T(8,128)(2,1)}, u32[]{:S(2)}, u32[]{:S(2)}) async-start(bf16[32,24,1536]{2,1,0:T(8,128)(2,1)} %bitcast.164), calls=%async_computation.4 | async-start | bytes 4718592 | tf_op jit(solution)/shard_map/all_to_all | solution.py:46
  308.6 7.1 %collective-permute-start.7 = (bf16[768,1536]{1,0:T(8,128)(2,1)S(1)}, bf16[768,1536]{1,0:T(8,128)(2,1)S(1)}, u32[]{:S(2)}, u32[]{:S(2)}) collective-permute-start(bf16[768,1536]{1,0:T(8,128)(2,1)S(1)} %bitcast.139), channel_id=1, source_target_pairs={{0,1},{1,0},{2,3},{3,2},{4,5},{5,4},{6,7},{7,6},{8,9},{9,8},{10,11... | collective-permute-start | bytes 7077896 | tf_op jit(solution)/shard_map/ppermute | solution.py:42
  328.2 35.0 %all-to-all-start.6 = ((bf16[32,24,1536]{2,1,0:T(8,128)(2,1)}), bf16[32,24,1536]{2,1,0:T(8,128)(2,1)}, u32[]{:S(2)}, u32[]{:S(2)}) async-start(bf16[32,24,1536]{2,1,0:T(8,128)(2,1)} %bitcast.142), calls=%async_computation.6 | async-start | bytes 4718592 | tf_op jit(solution)/shard_map/all_to_all | solution.py:46
  347.0 76.5 %collective-permute-start.16 = (bf16[384,1536]{1,0:T(8,128)(2,1)}, bf16[384,1536]{1,0:T(8,128)(2,1)}, u32[]{:S(2)}, u32[]{:S(2)}) collective-permute-start(bf16[384,1536]{1,0:T(8,128)(2,1)} %fusion.4), channel_id=1, source_target_pairs={{0,64},{64,0},{1,65},{65,1},{2,66},{66,2},{3,67},{67,3},{4,68},{68... | collective-permute-start | bytes 3538952 | tf_op jit(solution)/shard_map/ppermute | solution.py:393
  367.1 7.4 %collective-permute-start.9 = (bf16[128,1536]{1,0:T(8,128)(2,1)S(1)}, bf16[128,1536]{1,0:T(8,128)(2,1)S(1)}, u32[]{:S(2)}, u32[]{:S(2)}) collective-permute-start(bf16[128,1536]{1,0:T(8,128)(2,1)S(1)} %get-tuple-element.32), channel_id=1, source_target_pairs={{0,1},{1,0},{2,3},{3,2},{4,5},{5,4},{6,7},{7,6},{8,9},{9,8},{10,11... | collective-permute-start | bytes 1179656 | tf_op jit(solution)/shard_map/ppermute | solution.py:42
  371.4 55.5 %collective-permute-start.15 = (bf16[1536,384]{1,0:T(8,128)(2,1)}, bf16[1536,384]{1,0:T(8,128)(2,1)}, u32[]{:S(2)}, u32[]{:S(2)}) collective-permute-start(bf16[1536,384]{1,0:T(8,128)(2,1)} %fusion.3), channel_id=1, source_target_pairs={{0,64},{64,0},{1,65},{65,1},{2,66},{66,2},{3,67},{67,3},{4,68},{68... | collective-permute-start | bytes 3538952 | tf_op jit(solution)/shard_map/ppermute | solution.py:393
  413.8 33.9 %all-to-all-start.7 = ((bf16[16,256,256]{2,1,0:T(8,128)(2,1)}), bf16[16,256,256]{2,1,0:T(8,128)(2,1)}, u32[]{:S(2)}, u32[]{:S(2)}) async-start(bf16[16,256,256]{2,1,0:T(8,128)(2,1)} %slice.199), calls=%async_computation.7 | async-start | bytes 4194304 | tf_op jit(solution)/shard_map/all_to_all | solution.py:46
  423.4 31.5 %collective-permute-start.14 = (bf16[1536,384]{1,0:T(8,128)(2,1)}, bf16[1536,384]{1,0:T(8,128)(2,1)}, u32[]{:S(2)}, u32[]{:S(2)}) collective-permute-start(bf16[1536,384]{1,0:T(8,128)(2,1)} %fusion.2), channel_id=1, source_target_pairs={{0,64},{64,0},{1,65},{65,1},{2,66},{66,2},{3,67},{67,3},{4,68},{68... | collective-permute-start | bytes 3538952 | tf_op jit(solution)/shard_map/ppermute | solution.py:393
  447.7 35.9 %all-to-all-start.11 = ((bf16[64,24,768]{2,1,0:T(8,128)(2,1)}), bf16[64,24,768]{2,1,0:T(8,128)(2,1)}, u32[]{:S(2)}, u32[]{:S(2)}) async-start(bf16[64,24,768]{2,1,0:T(8,128)(2,1)} %bitcast.137), calls=%async_computation.11 | async-start | bytes 4718592 | tf_op jit(solution)/shard_map/all_to_all | solution.py:46
  473.7 18.8 %collective-permute-start.10 = (f32[256,256]{1,0:T(8,128)S(1)}, f32[256,256]{1,0:T(8,128)S(1)}, u32[]{:S(2)}, u32[]{:S(2)}) collective-permute-start(f32[256,256]{1,0:T(8,128)S(1)} %get-tuple-element.21), channel_id=1, source_target_pairs={{32,0},{64,32},{96,64},{33,1},{65,33},{97,65},{34,2},{66,34},{98,6... | collective-permute-start | bytes 786440 | tf_op jit(solution)/shard_map/ppermute | solution.py:422
  483.6 36.2 %all-to-all-start.9 = ((bf16[64,24,768]{2,1,0:T(8,128)(2,1)}), bf16[64,24,768]{2,1,0:T(8,128)(2,1)}, u32[]{:S(2)}, u32[]{:S(2)}) async-start(bf16[64,24,768]{2,1,0:T(8,128)(2,1)} %bitcast.163), calls=%async_computation.9 | async-start | bytes 4718592 | tf_op jit(solution)/shard_map/all_to_all | solution.py:46
  496.7 25.2 %collective-permute-start.11 = (f32[128,1536]{1,0:T(8,128)}, f32[128,1536]{1,0:T(8,128)S(1)}, u32[]{:S(2)}, u32[]{:S(2)}) collective-permute-start(f32[128,1536]{1,0:T(8,128)} %slice_select_fusion), channel_id=1, source_target_pairs={{0,1},{1,0},{2,3},{3,2},{4,5},{5,4},{6,7},{7,6},{8,9},{9,8},{10,11... | collective-permute-start | bytes 2359304 | tf_op jit(solution)/shard_map/ppermute | solution.py:42
  503.7 31.1 %collective-permute-start.12 = (f32[12,768]{1,0:T(8,128)S(1)}, f32[12,768]{1,0:T(8,128)S(1)}, u32[]{:S(2)}, u32[]{:S(2)}) collective-permute-start(f32[12,768]{1,0:T(8,128)S(1)} %get-tuple-element.69), channel_id=1, source_target_pairs={{0,0},{1,64},{64,1},{65,65},{2,2},{3,66},{66,3},{67,67},{4,4},{5,6... | collective-permute-start | bytes 110600 | tf_op jit(solution)/shard_map/ppermute | solution.py:238
  508.4 26.4 %collective-permute-start.13 = (f32[12,768]{1,0:T(8,128)S(1)}, f32[12,768]{1,0:T(8,128)S(1)}, u32[]{:S(2)}, u32[]{:S(2)}) collective-permute-start(f32[12,768]{1,0:T(8,128)S(1)} %get-tuple-element.70), channel_id=1, source_target_pairs={{0,1},{1,65},{64,0},{65,64},{2,3},{3,67},{66,2},{67,66},{4,5},{5,6... | collective-permute-start | bytes 110600 | tf_op jit(solution)/shard_map/ppermute | solution.py:241
  524.7 27.3 %all-to-all-start.8 = ((bf16[64,24,384]{2,1,0:T(8,128)(2,1)}), bf16[64,24,384]{2,1,0:T(8,128)(2,1)S(1)}, u32[]{:S(2)}, u32[]{:S(2)}) async-start(bf16[64,24,384]{2,1,0:T(8,128)(2,1)} %pad_maximum_fusion.2), calls=%async_computation.8 | async-start | bytes 2359296 | tf_op jit(solution)/shard_map/all_to_all | solution.py:46
  (84 other events, 805.7 us)
Sparse Core Ops, SparseCore 0:
  25.1 93.6 all-gather.2

commit v2 on v1

v2 whole, which is shorter than its diff:
```python
import math

import jax
import jax.numpy as jnp
import numpy as np
from jax import lax
from jax.experimental import pallas as pl
from jax.experimental.pallas import tpu as pltpu
from jax.sharding import PartitionSpec as P

HEAD_SIZE = 128
GROUP = 6
HALF_WIDTH = GROUP * HEAD_SIZE
WINDOW = 4096
CAP = 24
EXPERTS = 32

NORM_EPS = 1e-06
ROPE_BASE = 1000000.0
MASKED = -1e30
SCALE = HEAD_SIZE ** (-0.5)
SCALE_LOG2 = SCALE * math.log2(math.e)

ALL = ("xh", "xl", "y", "z", "c")
CHIPS = ("xh", "xl", "y", "z")
HALF_CHIPS = ("xl", "y", "z")
PLANE_CHIPS = ("y", "z")
SWAP = [(0, 1), (1, 0)]
PAIR = [(0, 1), (1, 0), (2, 3), (3, 2)]

f32 = jnp.float32
bf16 = jnp.bfloat16


def dot(a, b, dims=((1,), (0,))):
    return lax.dot_general(a, b, (dims, ((), ())), preferred_element_type=f32)


NT = ((1,), (1,))
TN = ((0,), (0,))


def core_swap(value):
    return lax.ppermute(value, "c", SWAP)


def exchange(value, axes):
    return lax.all_to_all(value, axes, 0, 0, tiled=True)


def gather_ring(value, axes, size):
    pieces = [value] + [
        lax.ppermute(value, axes, [((i + k) % size, i) for i in range(size)]) for k in range(1, size)
    ]
    return pieces


def in_ring_order(pieces, place):
    size = len(pieces)
    ordered = jnp.zeros((size,) + pieces[0].shape, pieces[0].dtype)
    for k, piece in enumerate(pieces):
        ordered = lax.dynamic_update_index_in_dim(ordered, piece, (place + k) % size, 0)
    return ordered


def in_order(core, own, other):
    return jnp.concatenate([jnp.where(core == 0, own, other), jnp.where(core == 0, other, own)])


def of_core(core, rows, own):
    upper, lower = jnp.split(rows, 2)
    return jnp.where((core == 0) == own, upper, lower)


def doc_begin(positions, doc_starts):
    before = doc_starts[None, :] <= positions[:, None]
    return jnp.max(jnp.where(before, doc_starts[None, :], 0), axis=-1)


def rope_tables(offset):
    column = jnp.arange(HEAD_SIZE, dtype=jnp.int32)
    half = HEAD_SIZE // 2
    inv_freq = jnp.exp((column % half).astype(f32) * (-2.0 * math.log(ROPE_BASE) / HEAD_SIZE))
    angle = offset.astype(f32)[:, None] * inv_freq[None, :]
    return jnp.cos(angle), jnp.where(column[None, :] < half, -1.0, 1.0) * jnp.sin(angle)


def rotate(values, cosine, sine):
    half = HEAD_SIZE // 2
    turned = jnp.concatenate([values[..., half:], values[..., :half]], axis=-1)
    return values * cosine + turned * sine


def norm_backward(values, inverse, gain_row, incoming_grad):
    scaled = incoming_grad * gain_row
    input_grad = inverse * scaled - values * inverse * inverse * inverse * jnp.mean(
        scaled * values, axis=-1, keepdims=True
    )
    gain_grad = jnp.sum(incoming_grad * values * inverse, axis=0, keepdims=True)
    return (input_grad, gain_grad)


def block_mask(low, t, blocks, rows, key_axis):
    key_at = lax.broadcasted_iota(jnp.int32, (rows, rows), key_axis)
    allowed = key_at >= low - t * rows
    if t == blocks - 1:
        allowed = allowed & (key_at <= lax.broadcasted_iota(jnp.int32, (rows, rows), 1 - key_axis))
    return allowed


def seen_block(spot, keys_ref, own_ref, t):
    spots = keys_ref.shape[0]
    return own_ref if t == spots else keys_ref.at[lax.rem(spot + t, spots)]


def attend_kernel(
    spot_ref, low_ref, query_ref, keys_ref, own_ref, out_ref, low_out_ref, log_ref, score_ref
):
    blocks, rows = keys_ref.shape[0] + 1, query_ref.shape[0]
    query = query_ref[...]
    low = low_ref[:, 0:1]
    top = None
    for t in range(blocks):
        score = dot(query, seen_block(spot_ref[0], keys_ref, own_ref, t)[:, :HEAD_SIZE], NT)
        score = jnp.where(block_mask(low, t, blocks, rows, 1), score, MASKED)
        score_ref[t] = score
        part = jnp.maximum(score[:, :HEAD_SIZE], score[:, HEAD_SIZE:])
        top = part if top is None else jnp.maximum(top, part)
    top = jnp.max(top, axis=1, keepdims=True) * SCALE_LOG2
    total = jnp.zeros((rows, HEAD_SIZE), f32)
    mixed = jnp.zeros((rows, HEAD_SIZE), f32)
    for t in range(blocks):
        weights = jnp.exp2(score_ref[t] * SCALE_LOG2 - top)
        total = total + weights[:, :HEAD_SIZE] + weights[:, HEAD_SIZE:]
        value = seen_block(spot_ref[0], keys_ref, own_ref, t)[:, HEAD_SIZE:]
        mixed = mixed + dot(weights.astype(bf16), value)
    total = jnp.sum(total, axis=1, keepdims=True)
    log_ref[0] = jnp.broadcast_to(top + jnp.log2(total), (rows, HEAD_SIZE)).T[:8]
    mixed = mixed / total
    out_ref[...] = mixed
    low_out_ref[...] = mixed.astype(bf16)


def attend(spot, low, query, keys, own):
    blocks, rows = keys.shape[0] + 1, query.shape[0]
    whole = lambda *shape: pl.BlockSpec(shape, lambda h, spot: (0,) * len(shape))
    by_head = pl.BlockSpec((rows, HEAD_SIZE), lambda h, spot: (0, h))
    return pl.pallas_call(
        attend_kernel,
        grid_spec=pltpu.PrefetchScalarGridSpec(
            num_scalar_prefetch=1,
            grid=(GROUP,),
            in_specs=[whole(rows, HEAD_SIZE), by_head, whole(*keys.shape), whole(*own.shape)],
            out_specs=[by_head, by_head, pl.BlockSpec((1, 8, rows), lambda h, spot: (h, 0, 0))],
            scratch_shapes=[pltpu.VMEM((blocks, rows, rows), f32)],
        ),
        out_shape=[
            jax.ShapeDtypeStruct((rows, HALF_WIDTH), f32),
            jax.ShapeDtypeStruct((rows, HALF_WIDTH), bf16),
            jax.ShapeDtypeStruct((GROUP, 8, rows), f32),
        ],
        compiler_params=pltpu.CompilerParams(vmem_limit_bytes=56 * 1024 * 1024),
        cost_estimate=pl.CostEstimate(flops=20_000_000_000, bytes_accessed=4_000_000, transcendentals=7_000_000),
        name="attend",
    )(spot, low, query, keys, own)


def place_rows_kernel(route_ref, gate_ref, placed_ref, placed_by_token_ref, gate_high_ref, gate_low_ref, slot_gate_ref):
    tokens, top = route_ref.shape
    slots = EXPERTS * CAP
    expert = lax.broadcasted_iota(jnp.int32, (tokens, HEAD_SIZE), 1)
    chosen = jnp.zeros((tokens, HEAD_SIZE), f32)
    gate = jnp.zeros((tokens, HEAD_SIZE), f32)
    for k in range(top):
        hit = route_ref[:, k : k + 1] == expert
        chosen = chosen + jnp.where(hit, 1.0, 0.0)
        gate = gate + jnp.where(hit, gate_ref[:, k : k + 1], 0.0)
    square = (tokens, tokens)
    earlier = lax.broadcasted_iota(jnp.int32, square, 1) < lax.broadcasted_iota(jnp.int32, square, 0)
    chosen = chosen.astype(bf16)
    before = dot(jnp.where(earlier, 1.0, 0.0).astype(bf16), chosen)
    first = lax.broadcasted_iota(jnp.int32, (HEAD_SIZE, slots), 0) * CAP
    slot = lax.broadcasted_iota(jnp.int32, (HEAD_SIZE, slots), 1)
    within = (slot >= first) & (slot < first + CAP)
    spread = jnp.where(within, 1.0, 0.0).astype(bf16)
    slot_in = jnp.sum(jnp.where(within, slot - first, 0).astype(f32), axis=0, keepdims=True)
    here = (dot(chosen, spread) > 0.5) & (jnp.abs(dot(before.astype(bf16), spread) - slot_in) < 0.5)
    high = gate.astype(bf16)
    low = (gate - high.astype(f32)).astype(bf16)
    high_at = jnp.where(here, dot(high, spread), 0.0)
    low_at = jnp.where(here, dot(low, spread), 0.0)
    placed = jnp.where(here, 1.0, 0.0)
    placed_by_token_ref[...] = placed.astype(bf16)
    placed_ref[...] = placed.T.astype(bf16)
    gate_high_ref[...] = high_at.astype(bf16)
    gate_low_ref[...] = low_at.astype(bf16)
    total = jnp.sum((high_at + low_at).T, axis=1, keepdims=True)
    slot_gate_ref[...] = jnp.broadcast_to(total, (slots, HEAD_SIZE))


def place_rows(routes, gates):
    tokens, slots = routes.shape[0], EXPERTS * CAP
    by_token = jax.ShapeDtypeStruct((tokens, slots), bf16)
    return pl.pallas_call(
        place_rows_kernel,
        out_shape=[
            jax.ShapeDtypeStruct((slots, tokens), bf16),
            by_token,
            by_token,
            by_token,
            jax.ShapeDtypeStruct((slots, HEAD_SIZE), f32),
        ],
        name="place_rows",
    )(routes, gates)


def normed_rows(values, gain_row):
    inverse = lax.rsqrt(jnp.mean(values * values, axis=-1, keepdims=True) + NORM_EPS)
    return (values * inverse * gain_row).astype(bf16)


def project_keys_kernel(acts_ref, weight_ref, cosine_ref, sine_ref, normed_ref, kv_ref, gain_ref):
    pick = lax.broadcasted_iota(jnp.int32, (16, HEAD_SIZE), 0) == lax.broadcasted_iota(jnp.int32, (16, HEAD_SIZE), 1)
    gains = dot(pick.astype(bf16), weight_ref[:, 2 * HEAD_SIZE :], NT)
    gain_ref[...] = gains[:8]
    normed = normed_rows(acts_ref[...].astype(f32), gains[0:1])
    normed_ref[...] = normed
    linear = dot(normed, weight_ref[:, : 2 * HEAD_SIZE])
    key = linear[:, :HEAD_SIZE]
    turned = key * cosine_ref[...] + pltpu.roll(key, HEAD_SIZE // 2, 1) * sine_ref[...]
    kv_ref[:, :HEAD_SIZE] = turned.astype(bf16)
    kv_ref[:, HEAD_SIZE:] = linear[:, HEAD_SIZE:].astype(bf16)


def project_keys(acts, weights, tables):
    rows, width = acts.shape
    whole = lambda *shape: pl.BlockSpec(shape, lambda i: (0,) * len(shape))
    return pl.pallas_call(
        project_keys_kernel,
        grid=(1,),
        in_specs=[whole(rows, width), whole(width, 3 * HEAD_SIZE)] + [whole(rows, HEAD_SIZE)] * 2,
        out_specs=[whole(rows, width), whole(rows, 2 * HEAD_SIZE), whole(8, width)],
        out_shape=[
            jax.ShapeDtypeStruct((rows, width), bf16),
            jax.ShapeDtypeStruct((rows, 2 * HEAD_SIZE), bf16),
            jax.ShapeDtypeStruct((8, width), f32),
        ],
        compiler_params=pltpu.CompilerParams(vmem_limit_bytes=32 * 1024 * 1024),
        name="project_keys",
    )(acts, weights, *tables)


def project_kernel(
    own_ref, acts_ref, gain_ref, weight_ref, own_cosine_ref, own_sine_ref, cosine_ref, sine_ref,
    normed_ref, own_out_ref, out_ref,
):
    normed_ref[...] = normed_rows(acts_ref[...].astype(f32), gain_ref[0:1, :])
    for rows_ref, cos_ref, sin_ref, target in (
        (own_ref, own_cosine_ref, own_sine_ref, own_out_ref),
        (normed_ref, cosine_ref, sine_ref, out_ref),
    ):
        linear = dot(rows_ref[...], weight_ref[...])
        for h in range(GROUP // 2):
            at = slice(h * HEAD_SIZE, (h + 1) * HEAD_SIZE)
            head = linear[:, at]
            turned = head * cos_ref[...] + pltpu.roll(head, HEAD_SIZE // 2, 1) * sin_ref[...]
            target[:, at] = turned.astype(bf16)


def project(own_rows, pair_acts, gains, weight, own_tables, pair_tables):
    shape = jax.ShapeDtypeStruct((own_rows.shape[0], weight.shape[1]), bf16)
    return pl.pallas_call(
        project_kernel,
        out_shape=[jax.ShapeDtypeStruct(own_rows.shape, bf16), shape, shape],
        compiler_params=pltpu.CompilerParams(vmem_limit_bytes=32 * 1024 * 1024),
        name="project",
    )(own_rows, pair_acts, gains, weight, *own_tables, *pair_tables)


def piece_at(place_ref, k, shape):
    depth, width = shape
    row_half = lax.rem(place_ref[1] + k % 2, 2)
    column_half = lax.rem(place_ref[0] + k // 2, 2)
    return (
        pl.ds(pl.multiple_of(row_half * depth, HEAD_SIZE), depth),
        pl.ds(pl.multiple_of(column_half * width, HEAD_SIZE), width),
    )


def out_project_kernel(place_ref, attn_ref, *refs):
    pieces, (own_ref, other_ref, sum_ref) = refs[:-3], refs[-3:]
    rows = own_ref.shape[0]
    sum_ref[...] = jnp.zeros_like(sum_ref)
    for k, piece in enumerate(pieces):
        features, columns = piece_at(place_ref, k, piece.shape)
        sum_ref[:, columns] += dot(attn_ref[:, features], piece[...])
    core = place_ref[2]
    own_ref[...] = sum_ref[pl.ds(pl.multiple_of(core * rows, rows), rows), :]
    other_ref[...] = sum_ref[pl.ds(pl.multiple_of((1 - core) * rows, rows), rows), :]


def out_project(place, attn, pieces):
    rows, width = attn.shape[0], 2 * pieces[0].shape[1]
    shape = jax.ShapeDtypeStruct((rows // 2, width), f32)
    vmem = pl.BlockSpec(memory_space=pltpu.VMEM)
    return pl.pallas_call(
        out_project_kernel,
        in_specs=[pl.BlockSpec(memory_space=pltpu.SMEM)] + [vmem] * (1 + len(pieces)),
        out_specs=[vmem, vmem],
        out_shape=[shape, shape],
        scratch_shapes=[pltpu.VMEM((rows, width), f32)],
        compiler_params=pltpu.CompilerParams(vmem_limit_bytes=32 * 1024 * 1024),
        name="out_project",
    )(place, attn, *pieces)


def out_project_back_kernel(place_ref, grad_ref, *refs):
    pieces, (out_ref, sum_ref) = refs[:-2], refs[-2:]
    sum_ref[...] = jnp.zeros_like(sum_ref)
    for k, piece in enumerate(pieces):
        features, columns = piece_at(place_ref, k, piece.shape)
        sum_ref[:, features] += dot(grad_ref[:, columns], piece[...], NT)
    out_ref[...] = sum_ref[...].astype(bf16)


def out_project_back(place, grad, pieces):
    rows, width = grad.shape[0], 2 * pieces[0].shape[0]
    vmem = pl.BlockSpec(memory_space=pltpu.VMEM)
    return pl.pallas_call(
        out_project_back_kernel,
        in_specs=[pl.BlockSpec(memory_space=pltpu.SMEM)] + [vmem] * (1 + len(pieces)),
        out_specs=vmem,
        out_shape=jax.ShapeDtypeStruct((rows, width), bf16),
        scratch_shapes=[pltpu.VMEM((rows, width), f32)],
        compiler_params=pltpu.CompilerParams(vmem_limit_bytes=32 * 1024 * 1024),
        name="out_project_back",
    )(place, grad, *pieces)


def attend_back_kernel(
    spot_ref, low_ref, query_ref, cosine_ref, sine_ref, keys_ref, own_ref, out_ref, grad_ref, log_ref,
    query_grad_ref, keys_grad_ref, own_grad_ref, sum_ref, turned_key_ref, weight_ref, score_ref,
):
    h, heads = pl.program_id(0), pl.num_programs(0)
    blocks, rows = keys_ref.shape[0] + 1, query_ref.shape[0]
    spot = spot_ref[0]

    @pl.when(h == 0)
    def _():
        sum_ref[...] = jnp.zeros_like(sum_ref)
        for t in range(blocks):
            turned_key_ref[t] = seen_block(spot, keys_ref, own_ref, t)[:, :HEAD_SIZE].T

    query, out_grad = query_ref[...], grad_ref[...]
    delta = jnp.sum((out_grad.astype(f32) * out_ref[...]).T, axis=0, keepdims=True)
    log_total, low = log_ref[0, 0:1, :], low_ref[0:1, :]
    for t in range(blocks):
        block = seen_block(spot, keys_ref, own_ref, t)
        key, value = block[:, :HEAD_SIZE], block[:, HEAD_SIZE:]
        weights = jnp.exp2(dot(key, query, NT) * SCALE_LOG2 - log_total)
        weights = jnp.where(block_mask(low, t, blocks, rows, 0), weights, 0.0)
        weight_ref[t] = weights.astype(bf16)
        score_ref[t] = (weights * (dot(value, out_grad, NT) - delta)).astype(bf16)
    query_grad = jnp.zeros((HEAD_SIZE, rows), f32)
    for t in range(blocks):
        query_grad = query_grad + dot(turned_key_ref[t], score_ref[t])
    query_grad = (query_grad * SCALE).T.astype(bf16).astype(f32)
    turned = query_grad * cosine_ref[...] - pltpu.roll(query_grad, HEAD_SIZE // 2, 1) * sine_ref[...]
    query_grad_ref[...] = turned.astype(bf16)
    for t in range(blocks):
        sum_ref[t, :, :HEAD_SIZE] += dot(score_ref[t], query)
        sum_ref[t, :, HEAD_SIZE:] += dot(weight_ref[t], out_grad)

    @pl.when(h == heads - 1)
    def _():
        for t in range(blocks):
            target = seen_block(spot, keys_grad_ref, own_grad_ref, t)
            target[:, :HEAD_SIZE] = (sum_ref[t, :, :HEAD_SIZE] * SCALE).astype(bf16)
            target[:, HEAD_SIZE:] = sum_ref[t, :, HEAD_SIZE:].astype(bf16)


def attend_back(spot, low, query, cosine, sine, keys, own, out, out_grad, log_total):
    blocks, rows = keys.shape[0] + 1, query.shape[0]
    whole = lambda *shape: pl.BlockSpec(shape, lambda h, spot: (0,) * len(shape))
    by_head = pl.BlockSpec((rows, HEAD_SIZE), lambda h, spot: (0, h))
    table = whole(rows, HEAD_SIZE)
    return pl.pallas_call(
        attend_back_kernel,
        grid_spec=pltpu.PrefetchScalarGridSpec(
            num_scalar_prefetch=1,
            grid=(GROUP,),
            in_specs=[
                whole(8, rows), by_head, table, table, whole(*keys.shape), whole(*own.shape), by_head, by_head,
                pl.BlockSpec((1, 8, rows), lambda h, spot: (h, 0, 0)),
            ],
            out_specs=[by_head, whole(*keys.shape), whole(*own.shape)],
            scratch_shapes=[
                pltpu.VMEM((blocks, rows, 2 * HEAD_SIZE), f32),
                pltpu.VMEM((blocks, HEAD_SIZE, rows), bf16),
                pltpu.VMEM((blocks, rows, rows), bf16),
                pltpu.VMEM((blocks, rows, rows), bf16),
            ],
        ),
        out_shape=[
            jax.ShapeDtypeStruct((rows, HALF_WIDTH), bf16),
            jax.ShapeDtypeStruct(keys.shape, bf16),
            jax.ShapeDtypeStruct(own.shape, bf16),
        ],
        compiler_params=pltpu.CompilerParams(vmem_limit_bytes=56 * 1024 * 1024),
        cost_estimate=pl.CostEstimate(flops=28_000_000_000, bytes_accessed=8_000_000, transcendentals=7_000_000),
        name="attend_back",
    )(spot, low, query, cosine, sine, keys, own, out, out_grad, log_total)


def body(
    acts, teacher, valid, doc_starts, routes, gates,
    w_query, key_weight, value_weight, w_out, gain_attn, gain_ffn, w_gate, w_up, w_down,
):
    half, core = lax.axis_index("xh"), lax.axis_index("c")
    plane, spot = lax.axis_index(("xh", "xl")), lax.axis_index(PLANE_CHIPS)
    chip = lax.axis_index(CHIPS)
    tok_rows, model_dim = acts.shape
    chip_rows = 2 * tok_rows
    spots = lax.axis_size(PLANE_CHIPS)
    planes = lax.axis_size(("xh", "xl"))
    chips = spots * planes
    total_tokens = chips * chip_rows
    shard_rows = w_query.shape[0]

    chip_acts = in_order(core, acts, core_swap(acts))
    pair_acts = lax.ppermute(acts, "z", PAIR)
    pair_acts = in_order(core, pair_acts, core_swap(pair_acts))

    gain_pair = jnp.pad(jnp.stack([gain_attn, gain_ffn], axis=1), ((0, 0), (0, HEAD_SIZE - 2)))
    by_core = jnp.stack(
        [
            jnp.concatenate(
                [
                    key_weight[:, k * HEAD_SIZE : (k + 1) * HEAD_SIZE],
                    value_weight[:, k * HEAD_SIZE : (k + 1) * HEAD_SIZE],
                    gain_pair,
                    w_query[:, k * HALF_WIDTH : (k + 1) * HALF_WIDTH],
                    w_out[:, k * HALF_WIDTH : (k + 1) * HALF_WIDTH],
                ],
                axis=1,
            )
            for k in range(2)
        ]
    )
    own_weights = exchange(by_core, "c").reshape(2 * shard_rows, -1)
    kv_width = 3 * HEAD_SIZE
    kv_part, query_part = own_weights[:, :kv_width], own_weights[:, kv_width : kv_width + HALF_WIDTH]
    side = chip % 2
    quarter = HALF_WIDTH // 2
    by_side = jnp.stack(
        [jnp.concatenate([kv_part, query_part[:, k * quarter : (k + 1) * quarter]], axis=1) for k in range(2)]
    )
    out_pieces = gather_ring(own_weights[:, kv_width + HALF_WIDTH :], "z", 4)
    by_side, out_pieces = lax.optimization_barrier((by_side, out_pieces))
    weights = exchange(
        jnp.broadcast_to(by_side[None], (chips // 2,) + by_side.shape).reshape((chips,) + by_side.shape[1:]), CHIPS
    )
    out_pieces = gather_ring(in_ring_order(out_pieces, lax.axis_index("z")), "y", 4)
    out_pieces = in_ring_order(out_pieces, lax.axis_index("y"))

    first_token = chip * chip_rows
    chip_pos = first_token + jnp.arange(chip_rows, dtype=jnp.int32)
    begin = doc_begin(chip_pos, doc_starts)
    cosine, sine = rope_tables(chip_pos - begin)
    pair_pos = chip_pos + (1 - 2 * side) * chip_rows
    pair_tables = rope_tables(pair_pos - doc_begin(pair_pos, doc_starts))
    low = jnp.maximum(begin, chip_pos - (WINDOW - 1)) - (first_token - WINDOW)
    low_rows = jnp.broadcast_to(low[None, :], (8, chip_rows))
    low_columns = jnp.broadcast_to(low[:, None], (chip_rows, HEAD_SIZE))
    block_at = jnp.arange(spots, dtype=jnp.int32)

    weights, out_pieces, chip_acts, pair_acts = lax.optimization_barrier((weights, out_pieces, chip_acts, pair_acts))
    weights = weights.reshape(model_dim, -1)
    full_kv, half_query = weights[:, :kv_width], weights[:, kv_width:]

    normed_one, own_kv, gain_rows = project_keys(chip_acts, weights, (cosine, sine))
    gain_one, gain_two = gain_rows[0:1], gain_rows[1:2]
    before_kv = lax.ppermute(own_kv, ("xh", "xl"), [(p, p + 1) for p in range(planes - 1)])
    later = (block_at > spot)[:, None, None]
    kv_sent, out_pieces = lax.optimization_barrier(
        (jnp.where(later, own_kv[None], before_kv[None]), out_pieces)
    )
    seen_kv = exchange(kv_sent, PLANE_CHIPS)
    all_slots = EXPERTS * CAP
    placed, placed_by_token, token_gate_high, token_gate_low, slot_gate = place_rows(routes, gates)

    out_pieces = out_pieces.reshape(-1, HALF_WIDTH)
    out_pieces = [
        lax.ppermute(
            out_pieces,
            ("xh", "xl", "c"),
            [
                (c * 4 + (l ^ k % 2) * 2 + (h ^ k // 2), h * 4 + l * 2 + c)
                for h in range(2)
                for l in range(2)
                for c in range(2)
            ],
        )
        for k in range(4)
    ]
    seen_kv, out_pieces = lax.optimization_barrier((seen_kv, out_pieces))

    pair_normed, query_mine, query_theirs = project(
        normed_one, pair_acts, gain_rows, half_query, (cosine, sine), pair_tables
    )
    query_theirs = lax.ppermute(query_theirs, "z", PAIR)
    query_seq = jnp.concatenate(
        [jnp.where(side == 0, query_mine, query_theirs), jnp.where(side == 0, query_theirs, query_mine)], axis=1
    )
    query_seq, placed, slot_gate, token_gate_high, token_gate_low, placed_by_token = lax.optimization_barrier(
        (query_seq, placed, slot_gate, token_gate_high, token_gate_low, placed_by_token)
    )
    spot_word = spot.astype(jnp.int32).reshape(1)
    attn_wide, attn, log_total = attend(spot_word, low_columns, query_seq, seen_kv, own_kv)

    place = jnp.stack([half, lax.axis_index("xl"), core]).astype(jnp.int32)
    branch, other_branch = out_project(place, attn, out_pieces)
    branch = branch + core_swap(other_branch)
    values_in = acts.astype(f32)
    hidden_one = values_in + branch
    inverse_two = lax.rsqrt(jnp.mean(hidden_one * hidden_one, axis=-1, keepdims=True) + NORM_EPS)
    normed_two = (hidden_one * inverse_two * gain_two).astype(bf16)

    def to_experts(rows):
        mine = exchange(rows.reshape(EXPERTS, CAP, model_dim), HALF_CHIPS).reshape(all_slots, model_dim)
        return mine, core_swap(mine)

    def from_experts(mine, theirs):
        both = mine + core_swap(theirs.astype(bf16)).astype(f32)
        both = both.astype(bf16).reshape(EXPERTS, CAP, model_dim)
        return exchange(both, HALF_CHIPS).reshape(all_slots, model_dim)

    units = w_gate.shape[1]
    gate_up = jnp.concatenate([w_gate, w_up], axis=1)

    def expert_hidden(rows):
        both = dot(rows, gate_up)
        gate_pre, up_pre = both[:, :units], both[:, units:]
        return gate_pre, up_pre, (jax.nn.silu(gate_pre) * up_pre).astype(bf16)

    def hidden_backward(kept, grad_rows):
        gate_pre, up_pre = kept[0], kept[1]
        grad_hidden = dot(grad_rows, w_down, NT)
        sigmoid = jax.nn.sigmoid(gate_pre)
        grad_gate = (grad_hidden * up_pre * sigmoid * (1.0 + gate_pre * (1.0 - sigmoid))).astype(bf16)
        grad_up = (grad_hidden * gate_pre * sigmoid).astype(bf16)
        return jnp.concatenate([grad_gate, grad_up], axis=1)

    def rows_backward(back):
        return dot(back, gate_up, NT)

    rows_mine, rows_theirs = to_experts(dot(placed, normed_two).astype(bf16))
    kept_mine = expert_hidden(rows_mine)
    kept_mine, rows_theirs = lax.optimization_barrier((kept_mine, rows_theirs))
    kept_theirs = expert_hidden(rows_theirs)
    returned = from_experts(dot(kept_mine[2], w_down), dot(kept_theirs[2], w_down))
    mixture = dot(token_gate_high, returned) + dot(token_gate_low, returned)
    hidden_two = hidden_one + mixture

    valid_count = valid[0]
    own_pos = first_token + core * tok_rows + jnp.arange(tok_rows, dtype=jnp.int32)
    grad_two = jnp.where(
        (own_pos < valid_count)[:, None],
        total_tokens / valid_count.astype(f32) * (hidden_two - teacher.astype(f32)),
        0.0,
    )
    grad_two_high = grad_two.astype(bf16)
    grad_two_low = (grad_two - grad_two_high.astype(f32)).astype(bf16)
    grad_slots = (slot_gate[:, :1] * (dot(placed, grad_two_high) + dot(placed, grad_two_low))).astype(bf16)
    grads_mine, grads_theirs = to_experts(grad_slots)
    back_mine = hidden_backward(kept_mine, grads_mine)
    back_mine, grads_theirs = lax.optimization_barrier((back_mine, grads_theirs))
    back_theirs = hidden_backward(kept_theirs, grads_theirs)
    grad_returned = from_experts(rows_backward(back_mine), rows_backward(back_theirs))

    expert_parts = (
        (dot(rows_mine, back_mine, TN) + dot(rows_theirs, back_theirs, TN)).astype(bf16),
        (dot(kept_mine[2], grads_mine, TN) + dot(kept_theirs[2], grads_theirs, TN)).astype(bf16),
    )
    expert_parts, grad_returned = lax.optimization_barrier((expert_parts, grad_returned))

    grad_normed_two = dot(placed_by_token, grad_returned)
    norm_two_grad, gain_two_grad = norm_backward(hidden_one, inverse_two, gain_two, grad_normed_two)
    grad_one = grad_two + norm_two_grad
    grad_branch = grad_one.astype(bf16)
    chip_branch = in_order(core, grad_branch, core_swap(grad_branch))
    left, right = chip_branch[:, :HALF_WIDTH], chip_branch[:, HALF_WIDTH:]
    grad_attn = out_project_back(place, chip_branch, out_pieces)

    def send_to_chips(partial):
        return exchange(partial.astype(bf16).reshape(chips, 2 * shard_rows, -1), CHIPS)

    gate_up_other = lax.ppermute(expert_parts[0], "xh", SWAP)
    down_other = lax.ppermute(expert_parts[1], "xh", SWAP)
    out_partial = jnp.stack([dot(attn, left, TN), dot(attn, right, TN)]).astype(bf16)
    out_partial = out_partial.reshape(planes, spots, 2 * shard_rows, -1).transpose(1, 0, 2, 3)
    out_received = exchange(out_partial, PLANE_CHIPS)

    query_lin_grad, kv_grad, own_kv_grad = attend_back(
        spot_word, low_rows, query_seq, cosine, sine, seen_kv, own_kv, attn_wide, grad_attn, log_total
    )
    query_left, query_right = query_lin_grad[:, :quarter], query_lin_grad[:, quarter:]
    pair_query_grad = lax.ppermute(jnp.where(side == 0, query_right, query_left), "z", PAIR)
    kv_grad, out_received, gate_up_other, pair_query_grad = lax.optimization_barrier(
        (kv_grad, out_received, gate_up_other, pair_query_grad)
    )
    came = exchange(kv_grad, PLANE_CHIPS)
    side_query_grad = jnp.where(side == 0, query_left, query_right)
    pair_normed_grad = dot(pair_query_grad, half_query, NT)
    pair_normed_grad = of_core(core, pair_normed_grad, True) + core_swap(of_core(core, pair_normed_grad, False))
    back_normed_grad = lax.ppermute(pair_normed_grad.astype(bf16), "z", PAIR)
    query_partial = (dot(normed_one, side_query_grad, TN) + dot(pair_normed, pair_query_grad, TN)).astype(bf16)
    side_normed_grad = dot(side_query_grad, half_query, NT)
    came, down_other, query_partial, side_normed_grad, back_normed_grad = lax.optimization_barrier(
        (came, down_other, query_partial, side_normed_grad, back_normed_grad)
    )
    came = came.astype(f32)
    from_later = jnp.sum(jnp.where((block_at > spot)[:, None, None], came, 0.0), axis=0)
    from_before = jnp.sum(jnp.where((block_at <= spot)[:, None, None], came, 0.0), axis=0)
    from_next = lax.ppermute(from_before.astype(bf16), ("xh", "xl"), [(p + 1, p) for p in range(planes - 1)])
    kv_sum = (from_later + from_next.astype(f32) + own_kv_grad.astype(f32)).astype(bf16)
    key_lin_grad = rotate(kv_sum[:, :HEAD_SIZE].astype(f32), cosine, -sine).astype(bf16)
    kv_lin_grad = jnp.concatenate([key_lin_grad, kv_sum[:, HEAD_SIZE:]], axis=1)

    normed_grad = side_normed_grad + dot(kv_lin_grad, full_kv[:, : 2 * HEAD_SIZE], NT)
    normed_grad = of_core(core, normed_grad, True) + core_swap(of_core(core, normed_grad, False))
    normed_grad = normed_grad + back_normed_grad.astype(f32)
    own_inverse = lax.rsqrt(jnp.mean(values_in * values_in, axis=-1, keepdims=True) + NORM_EPS)
    input_norm_grad, gain_one_grad = norm_backward(values_in, own_inverse, gain_one, normed_grad)
    grad_acts = grad_one + input_norm_grad

    gain_grads = jnp.concatenate([gain_one_grad, gain_two_grad]).astype(bf16)
    gain_columns = dot(gain_grads, jnp.asarray(np.eye(2, HEAD_SIZE), bf16), TN)
    kv_partial = jnp.concatenate([dot(normed_one, kv_lin_grad, TN), gain_columns], axis=1).astype(bf16)
    partial = jnp.concatenate([kv_partial, query_partial], axis=1)
    partial, gate_up_other, down_other, out_received = lax.optimization_barrier(
        (partial, gate_up_other, down_other, out_received)
    )
    received = send_to_chips(partial)
    gate_up_grad = expert_parts[0].astype(f32) + gate_up_other.astype(f32)
    expert_grads = (
        gate_up_grad[:, :units],
        gate_up_grad[:, units:],
        expert_parts[1].astype(f32) + down_other.astype(f32),
    )
    plane_sums = jnp.sum(out_received.astype(f32), axis=0).astype(bf16)
    plane_sums = plane_sums.reshape(2, 2, 2, shard_rows, -1)
    grad_w_out = 0.0
    for k in range(4):
        piece = lax.dynamic_index_in_dim(plane_sums, (lax.axis_index("xl") + k) % 2, 1, False)
        piece = lax.dynamic_index_in_dim(piece, (half + k // 2) % 2, 1, False)
        piece = lax.ppermute(
            piece,
            ("xh", "xl", "c"),
            [
                (h * 4 + l * 2 + c, c * 4 + (l ^ k % 2) * 2 + (h ^ k // 2))
                for h in range(2)
                for l in range(2)
                for c in range(2)
            ],
        )
        grad_w_out = grad_w_out + piece.astype(f32)
    grad_w_out = jnp.concatenate([grad_w_out[0], grad_w_out[1]], axis=1)
    received = received.astype(f32).reshape(chips // 2, 2, 2 * shard_rows, -1)
    sums = jnp.sum(received, axis=0)
    sums = jnp.concatenate(
        [sums[0, :, :kv_width] + sums[1, :, :kv_width], sums[0, :, kv_width:], sums[1, :, kv_width:]], axis=1
    ).reshape(2, shard_rows, -1)
    sums = exchange(sums, "c")

    def columns(begin_at, width):
        return jnp.concatenate([sums[k, :, begin_at : begin_at + width] for k in range(2)], axis=1)

    gain_sums = sums[0, :, 2 * HEAD_SIZE : 2 * HEAD_SIZE + 2] + sums[1, :, 2 * HEAD_SIZE : 2 * HEAD_SIZE + 2]
    return (
        hidden_two.astype(bf16),
        grad_acts,
        columns(kv_width, HALF_WIDTH),
        columns(0, HEAD_SIZE),
        columns(HEAD_SIZE, HEAD_SIZE),
        grad_w_out,
        gain_sums[:, 0],
        gain_sums[:, 1],
        *expert_grads,
    )


def solution(mesh):
    fine_mesh = jax.sharding.Mesh(mesh.devices.reshape(2, 2, 4, 4, 2), ALL)
    rows, vector = P(ALL, None), P(ALL)
    wide, tall = P(None, ("xl", "y", "z", "c")), P(("xl", "y", "z", "c"), None)
    return jax.shard_map(
        body,
        mesh=fine_mesh,
        in_specs=(
            rows, rows, P(), P(), rows, rows, rows, rows, rows, rows, vector, vector, wide, wide, tall,
        ),
        out_specs=(rows, rows, rows, rows, rows, rows, vector, vector, wide, wide, tall),
        check_vma=False,
    )
```

time: 579 us -> 517 us (0.89)
  matrix products: 69.5 us -> 45.2 us
  Pallas kernels: 67.3 us -> 51.2 us
  other arithmetic: 55 us -> 39.1 us
  between operations: 16.4 us -> 3.45 us
  starting transfers between devices: 93.7 us -> 104 us
  waiting for transfers between devices: 158 us -> 150 us
  blocking collectives: 78.5 us -> 86 us
    ppermute x8 -> x21, waiting for transfers between devices: 0.02 us -> 89 us  [the longest x6 27.8 us: gather_ring(): lax.ppermute(value, axes, [((i + k) % size, i) for i in range(size)])]
    all_to_all x9 -> x7, waiting for transfers between devices: 103 us -> 47 us  [exchange(): return lax.all_to_all(value, axes, 0, 0, tiled=True)]
    all_gather x1 -> x0, waiting for transfers between devices: 43.2 us -> none  [body(): lax.all_gather(jnp.concatenate([query_part, out_part], axis=1), CHIPS)]
    dot_general x37 -> x26, matrix products: 69.5 us -> 45.2 us  [dot(): return lax.dot_general(a, b, (dims, ((), ())), preferred_element_type=f32)]
    ppermute x8 -> x21, starting transfers between devices: 18.6 us -> 42 us  [the longest x4 10.5 us: body(): lax.ppermute(out_pieces, ('xh', 'xl', 'c'), [(c * 4 + (l ^ k % 2) * 2 + (...]
    all_to_all x9 -> x7, starting transfers between devices: 59.1 us -> 44.1 us  [exchange(): return lax.all_to_all(value, axes, 0, 0, tiled=True)]
    pallas_call x1, Pallas kernels: 31.4 us -> 16.4 us  [attend(): pl.pallas_call(attend_kernel, grid_spec=pltpu.PrefetchScalarGridSpec(num_...]
    pallas_call x1, Pallas kernels: 36 us -> 23.9 us  [attend_back(): pl.pallas_call(attend_back_kernel, grid_spec=pltpu.PrefetchScalarGridSpec...]
  transfers between devices with their start and end apart: 27 -> 39, of which waited for: 15 -> 20; matrix products, arithmetic and copies ran while one was open for 20% -> 12% of each run, Pallas kernels for 6% -> 6%
where the time goes in v2:
time: 517 us; the launch traced here: 508 us
  waiting for transfers between devices  150 us (29%)
  starting transfers between devices  104 us (20%)
  blocking collectives  86 us (17%)
  Pallas kernels  51.2 us (10%)
  matrix products  45.2 us (9%)
  other arithmetic  39.1 us (8%)
  local copies, waits for them, and re-layouts  29.1 us (6%)
    all_to_all x4, blocking collectives, exchange(): return lax.all_to_all(value, axes, 0, 0, tiled=True)  86 us
    all_to_all x7, waiting for transfers between devices, exchange(): return lax.all_to_all(value, axes, 0, 0, tiled=True)  47 us
    dot_general x26, matrix products, dot(): return lax.dot_general(a, b, (dims, ((), ())), preferred_element_type=f32)  45.2 us
    all_to_all x7, starting transfers between devices, exchange(): return lax.all_to_all(value, axes, 0, 0, tiled=True)  44.1 us
    ppermute x6, waiting for transfers between devices, gather_ring(): lax.ppermute(value, axes, [((i + k) % size, i) for i in range(size)])  27.8 us
    pallas_call x1, Pallas kernels, attend_back(): pl.pallas_call(attend_back_kernel, grid_spec=pltpu.PrefetchScalarGridSpec...  23.9 us
    ppermute x1, waiting for transfers between devices, body(): down_other = lax.ppermute(expert_parts[1], 'xh', SWAP)  20.2 us
    pallas_call x1, Pallas kernels, attend(): pl.pallas_call(attend_kernel, grid_spec=pltpu.PrefetchScalarGridSpec(num_...  16.4 us
  transfers between devices with their start and end apart: 39, of which 20 were waited for; matrix products, arithmetic and copies ran while one was open for 12% of the time, Pallas kernels for 6%

profile of v2, /device:TPU:1, one launch (start us, length us, event | category | flops | bytes accessed | tf_op | source)
XLA Modules:
  0.0 507.9 jit_solution(16336966610174374178)
XLA Ops:
  4.5 4.9 all_to_all.55
  21.7 8.3 %all-to-all-start.1 = ((bf16[64,24,768]{2,1,0:T(8,128)(2,1)}), bf16[64,24,768]{2,1,0:T(8,128)(2,1)S(1)}, u32[]{:S(2)}, u32[]{:S(2)}) async-start(bf16[64,24,768]{2,1,0:T(8,128)(2,1)} %bitcast.140), calls=%async_computation.1 | async-start | bytes 4718592 | tf_op jit(solution)/shard_map/all_to_all | solution.py:48
  36.6 23.0 %collective-permute-done.3 = bf16[4,24,768]{2,1,0:T(8,128)(2,1)S(1)} collective-permute-done((bf16[4,24,768]{2,1,0:T(8,128)(2,1)S(1)}, bf16[4,24,768]{2,1,0:T(8,128)(2,1)S(1)}, u32[]{:S(2)}, u32[]{:S(2)}) %collective-permute-start.3) | collective-permute-done | bytes 147488 | tf_op jit(solution)/shard_map/ppermute | solution.py:53
  81.6 5.7 %all-to-all-start.2 = ((bf16[16,256,256]{2,1,0:T(8,128)(2,1)}), bf16[16,256,256]{2,1,0:T(8,128)(2,1)}, u32[]{:S(2)}, u32[]{:S(2)}) async-start(bf16[16,256,256]{2,1,0:T(8,128)(2,1)} %broadcast_select_fusion), calls=%async_computation.2 | async-start | bytes 4194304 | tf_op jit(solution)/shard_map/all_to_all | solution.py:48
  87.4 6.6 %collective-permute-start.11 = (bf16[384,768]{1,0:T(8,128)(2,1)}, bf16[384,768]{1,0:T(8,128)(2,1)}, u32[]{:S(2)}, u32[]{:S(2)}) collective-permute-start(bf16[384,768]{1,0:T(8,128)(2,1)} %bitcast.153), channel_id=1, source_target_pairs={{0,0},{64,1},{32,32},{96,33},{1,64},{65,65},{33,96},{97,97},{2,2},... | collective-permute-start | bytes 1769480 | tf_op jit(solution)/shard_map/ppermute | solution.py:494
  107.4 9.5 %collective-permute-done.9 = bf16[256,384]{1,0:T(8,128)(2,1)} collective-permute-done((bf16[256,384]{1,0:T(8,128)(2,1)}, bf16[256,384]{1,0:T(8,128)(2,1)}, u32[]{:S(2)}, u32[]{:S(2)}) %collective-permute-start.9) | collective-permute-done | bytes 196640 | tf_op jit(solution)/shard_map/ppermute | solution.py:511
  121.6 16.4 %attend.1 = (f32[256,768]{1,0:T(8,128)}, bf16[256,768]{1,0:T(8,128)(2,1)}, f32[6,8,256]{2,1,0:T(8,128)}) custom-call(s32[1]{0:T(128)} %bitcast.3.spot_ref, s32[256,128]{1,0:T(8,128)} %broadcast_in_dim.157.low_ref, bf16[256,768]{1,0:T(8,128)(2,1)} %pad_maximum_fusion.9.query_ref, bf16[16,256,256]{2,1,0:T(8,128)(2,1)} %all-to-all-done.2.keys_ref, ...), custom_call_target="tpu_custom_call" | custom-call | flops 20000000000 | bytes 4000000 | tf_op jit(solution)/shard_map/attend/pallas_call | solution.py:148
  146.1 38.8 %all_to_all.56 = bf16[32,24,1536]{2,1,0:T(8,128)(2,1)S(1)} all-to-all(bf16[32,24,1536]{2,1,0:T(8,128)(2,1)S(1)} %bitcast.143), channel_id=1, replica_groups=mesh['xh'=2,'xl'=2,'y'=4,'z'=4,'c'=2] {'xl','y','z'}, dimensions={0} | all-to-all | bytes 4718592 | tf_op jit(solution)/shard_map/all_to_all | solution.py:48
  197.2 4.2 collective-permute-done.17
  204.1 4.8 all-to-all-start.4
  211.3 27.7 %all-to-all-done.4 = bf16[32,24,1536]{2,1,0:T(8,128)(2,1)} async-done(((bf16[32,24,1536]{2,1,0:T(8,128)(2,1)}), bf16[32,24,1536]{2,1,0:T(8,128)(2,1)}, u32[]{:S(2)}, u32[]{:S(2)}) %all-to-all-start.4) | async-done | bytes 2359328 | tf_op jit(solution)/shard_map/all_to_all | solution.py:48
  245.4 36.9 %all_to_all.57 = bf16[32,24,1536]{2,1,0:T(8,128)(2,1)S(1)} all-to-all(bf16[32,24,1536]{2,1,0:T(8,128)(2,1)S(1)} %bitcast.144), channel_id=1, replica_groups=mesh['xh'=2,'xl'=2,'y'=4,'z'=4,'c'=2] {'xl','y','z'}, dimensions={0} | all-to-all | bytes 4718592 | tf_op jit(solution)/shard_map/all_to_all | solution.py:48
  302.1 5.1 %all-to-all-start.6 = ((bf16[32,24,1536]{2,1,0:T(8,128)(2,1)}), bf16[32,24,1536]{2,1,0:T(8,128)(2,1)}, u32[]{:S(2)}, u32[]{:S(2)}) async-start(bf16[32,24,1536]{2,1,0:T(8,128)(2,1)} %bitcast.152), calls=%async_computation.6 | async-start | bytes 4718592 | tf_op jit(solution)/shard_map/all_to_all | solution.py:48
  317.9 19.3 %all-to-all-done.6 = bf16[32,24,1536]{2,1,0:T(8,128)(2,1)} async-done(((bf16[32,24,1536]{2,1,0:T(8,128)(2,1)}), bf16[32,24,1536]{2,1,0:T(8,128)(2,1)}, u32[]{:S(2)}, u32[]{:S(2)}) %all-to-all-start.6) | async-done | bytes 2359328 | tf_op jit(solution)/shard_map/all_to_all | solution.py:48
  352.8 5.1 %all-to-all-start.7 = ((bf16[16,4,24,768]{3,2,1,0:T(8,128)(2,1)}), bf16[16,4,24,768]{3,2,1,0:T(8,128)(2,1)}, u32[]{:S(2)}, u32[]{:S(2)}) async-start(bf16[16,4,24,768]{3,2,1,0:T(8,128)(2,1)} %bitcast.141), calls=%async_computation.7 | async-start | bytes 4718592 | tf_op jit(solution)/shard_map/all_to_all | solution.py:48
  358.5 23.9 %attend_back.1 = (bf16[256,768]{1,0:T(8,128)(2,1)}, bf16[16,256,256]{2,1,0:T(8,128)(2,1)}, bf16[256,256]{1,0:T(8,128)(2,1)}) custom-call(s32[1]{0:T(128)} %bitcast.3.spot_ref, s32[8,256]{1,0:T(8,128)} %broadcast_in_dim.176.low_ref, bf16[256,768]{1,0:T(8,128)(2,1)} %pad_maximum_fusion.9.query_ref, f32[256,128]{1,0:T(8,128)} %get-tuple-element.210.cosine_ref.own_cosine_ref, ...), custom_call_target="tpu_custom_call" | custom-call | flops 28000000000 | bytes 8000000 | tf_op jit(solution)/shard_map/attend_back/pallas_call | solution.py:387
  385.0 6.5 %collective-permute-done.22 = bf16[256,384]{1,0:T(8,128)(2,1)S(1)} collective-permute-done((bf16[256,384]{1,0:T(8,128)(2,1)S(1)}, bf16[256,384]{1,0:T(8,128)(2,1)S(1)}, u32[]{:S(2)}, u32[]{:S(2)}) %collective-permute-start.22) | collective-permute-done | bytes 196640 | tf_op jit(solution)/shard_map/ppermute | solution.py:608
  391.6 6.8 %collective-permute-done.21 = bf16[1536,768]{1,0:T(8,128)(2,1)} collective-permute-done((bf16[1536,768]{1,0:T(8,128)(2,1)}, bf16[1536,768]{1,0:T(8,128)(2,1)}, u32[]{:S(2)}, u32[]{:S(2)}) %collective-permute-start.21) | collective-permute-done | bytes 2359328 | tf_op jit(solution)/shard_map/ppermute | solution.py:598
  398.3 4.7 all-to-all-start.8
  415.3 20.2 %collective-permute-done.23 = bf16[384,1536]{1,0:T(8,128)(2,1)S(1)} collective-permute-done((bf16[384,1536]{1,0:T(8,128)(2,1)S(1)}, bf16[384,1536]{1,0:T(8,128)(2,1)S(1)}, u32[]{:S(2)}, u32[]{:S(2)}) %collective-permute-start.23) | collective-permute-done | bytes 1179680 | tf_op jit(solution)/shard_map/ppermute | solution.py:599
  440.5 5.1 %collective-permute-done.26 = bf16[256,256]{1,0:T(8,128)(2,1)S(1)} collective-permute-done((bf16[256,256]{1,0:T(8,128)(2,1)S(1)}, bf16[256,256]{1,0:T(8,128)(2,1)S(1)}, u32[]{:S(2)}, u32[]{:S(2)}) %collective-permute-start.26) | collective-permute-done | bytes 131104 | tf_op jit(solution)/shard_map/ppermute | solution.py:625
  457.4 10.4 %all-to-all-start.9 = ((bf16[64,24,768]{2,1,0:T(8,128)(2,1)}), bf16[64,24,768]{2,1,0:T(8,128)(2,1)S(1)}, u32[]{:S(2)}, u32[]{:S(2)}) async-start(bf16[64,24,768]{2,1,0:T(8,128)(2,1)} %bitcast.139), calls=%async_computation.9 | async-start | bytes 4718592 | tf_op jit(solution)/shard_map/all_to_all | solution.py:48
  487.4 9.0 %collective-permute-done.31 = bf16[2,12,768]{2,0,1:T(2,128)(2,1)S(1)} collective-permute-done((bf16[2,12,768]{2,0,1:T(2,128)(2,1)S(1)}, bf16[2,12,768]{2,0,1:T(2,128)(2,1)S(1)}, u32[]{:S(2)}, u32[]{:S(2)}) %collective-permute-start.31) | collective-permute-done | bytes 36896 | tf_op jit(solution)/shard_map/ppermute | solution.py:657
  499.6 5.4 %all_to_all.58 = f32[2,12,1152]{2,1,0:T(8,128)S(1)} all-to-all(f32[2,12,1152]{2,1,0:T(8,128)S(1)} %pad_maximum_fusion.10), channel_id=1, replica_groups=mesh['xh'=2,'xl'=2,'y'=4,'z'=4,'c'=2] {'c'}, dimensions={0} | all-to-all | bytes 221184 | tf_op jit(solution)/shard_map/all_to_all | solution.py:48
  (392 shorter events, 196.1 us)
Async XLA Ops:
  14.1 51.5 %collective-permute-start.6 = (bf16[128,1536]{1,0:T(8,128)(2,1)}, bf16[128,1536]{1,0:T(8,128)(2,1)}, u32[]{:S(2)}, u32[]{:S(2)}) collective-permute-start(bf16[128,1536]{1,0:T(8,128)(2,1)} %param.16), channel_id=1, source_target_pairs={{0,1},{1,0},{2,3},{3,2},{4,5},{5,4},{6,7},{7,6},{8,9},{9,8},{10,11... | collective-permute-start | bytes 1179656 | tf_op jit(solution)/shard_map/ppermute | solution.py:44
  15.3 49.2 %collective-permute-start.7 = (bf16[128,1536]{1,0:T(8,128)(2,1)}, bf16[128,1536]{1,0:T(8,128)(2,1)}, u32[]{:S(2)}, u32[]{:S(2)}) collective-permute-start(bf16[128,1536]{1,0:T(8,128)(2,1)} %param.16), channel_id=1, source_target_pairs={{0,2},{2,0},{4,6},{6,4},{1,3},{3,1},{5,7},{7,5},{8,10},{10,8},{12,... | collective-permute-start | bytes 1179656 | tf_op jit(solution)/shard_map/ppermute | solution.py:431
  21.7 47.8 %all-to-all-start.1 = ((bf16[64,24,768]{2,1,0:T(8,128)(2,1)}), bf16[64,24,768]{2,1,0:T(8,128)(2,1)S(1)}, u32[]{:S(2)}, u32[]{:S(2)}) async-start(bf16[64,24,768]{2,1,0:T(8,128)(2,1)} %bitcast.140), calls=%async_computation.1 | async-start | bytes 4718592 | tf_op jit(solution)/shard_map/all_to_all | solution.py:48
  33.2 26.5 %collective-permute-start.3 = (bf16[4,24,768]{2,1,0:T(8,128)(2,1)S(1)}, bf16[4,24,768]{2,1,0:T(8,128)(2,1)S(1)}, u32[]{:S(2)}, u32[]{:S(2)}) collective-permute-start(bf16[4,24,768]{2,1,0:T(8,128)(2,1)S(1)} %bitcast_dynamic-update-slice_fusion.4), channel_id=1, source_target_pairs={{8,0},{16,8},{24,16},{0,24},{9,1},{17,9},{25,17},{1,25},{10,2},{18... | collective-permute-start | bytes 442376 | tf_op jit(solution)/shard_map/ppermute | solution.py:53
  35.4 26.2 %collective-permute-start.4 = (bf16[4,24,768]{2,1,0:T(8,128)(2,1)S(1)}, bf16[4,24,768]{2,1,0:T(8,128)(2,1)S(1)}, u32[]{:S(2)}, u32[]{:S(2)}) collective-permute-start(bf16[4,24,768]{2,1,0:T(8,128)(2,1)S(1)} %bitcast_dynamic-update-slice_fusion.4), channel_id=1, source_target_pairs={{16,0},{24,8},{0,16},{8,24},{17,1},{25,9},{1,17},{9,25},{18,2},{26... | collective-permute-start | bytes 442376 | tf_op jit(solution)/shard_map/ppermute | solution.py:53
  36.0 28.5 %collective-permute-start.5 = (bf16[4,24,768]{2,1,0:T(8,128)(2,1)S(1)}, bf16[4,24,768]{2,1,0:T(8,128)(2,1)S(1)}, u32[]{:S(2)}, u32[]{:S(2)}) collective-permute-start(bf16[4,24,768]{2,1,0:T(8,128)(2,1)S(1)} %bitcast_dynamic-update-slice_fusion.4), channel_id=1, source_target_pairs={{24,0},{0,8},{8,16},{16,24},{25,1},{1,9},{9,17},{17,25},{26,2},{2,... | collective-permute-start | bytes 442376 | tf_op jit(solution)/shard_map/ppermute | solution.py:53
  81.6 39.3 %all-to-all-start.2 = ((bf16[16,256,256]{2,1,0:T(8,128)(2,1)}), bf16[16,256,256]{2,1,0:T(8,128)(2,1)}, u32[]{:S(2)}, u32[]{:S(2)}) async-start(bf16[16,256,256]{2,1,0:T(8,128)(2,1)} %broadcast_select_fusion), calls=%async_computation.2 | async-start | bytes 4194304 | tf_op jit(solution)/shard_map/all_to_all | solution.py:48
  87.4 31.4 %collective-permute-start.11 = (bf16[384,768]{1,0:T(8,128)(2,1)}, bf16[384,768]{1,0:T(8,128)(2,1)}, u32[]{:S(2)}, u32[]{:S(2)}) collective-permute-start(bf16[384,768]{1,0:T(8,128)(2,1)} %bitcast.153), channel_id=1, source_target_pairs={{0,0},{64,1},{32,32},{96,33},{1,64},{65,65},{33,96},{97,97},{2,2},... | collective-permute-start | bytes 1769480 | tf_op jit(solution)/shard_map/ppermute | solution.py:494
  94.0 24.8 %collective-permute-start.12 = (bf16[384,768]{1,0:T(8,128)(2,1)}, bf16[384,768]{1,0:T(8,128)(2,1)}, u32[]{:S(2)}, u32[]{:S(2)}) collective-permute-start(bf16[384,768]{1,0:T(8,128)(2,1)} %bitcast.154), channel_id=1, source_target_pairs={{32,0},{96,1},{0,32},{64,33},{33,64},{97,65},{1,96},{65,97},{34,2}... | collective-permute-start | bytes 1769480 | tf_op jit(solution)/shard_map/ppermute | solution.py:494
  94.7 26.2 %collective-permute-start.13 = (bf16[384,768]{1,0:T(8,128)(2,1)}, bf16[384,768]{1,0:T(8,128)(2,1)}, u32[]{:S(2)}, u32[]{:S(2)}) collective-permute-start(bf16[384,768]{1,0:T(8,128)(2,1)} %bitcast.155), channel_id=1, source_target_pairs={{1,0},{65,1},{33,32},{97,33},{0,64},{64,65},{32,96},{96,97},{3,2},... | collective-permute-start | bytes 1769480 | tf_op jit(solution)/shard_map/ppermute | solution.py:494
  97.4 23.4 %collective-permute-start.14 = (bf16[384,768]{1,0:T(8,128)(2,1)}, bf16[384,768]{1,0:T(8,128)(2,1)}, u32[]{:S(2)}, u32[]{:S(2)}) collective-permute-start(bf16[384,768]{1,0:T(8,128)(2,1)} %bitcast.156), channel_id=1, source_target_pairs={{33,0},{97,1},{1,32},{65,33},{32,64},{96,65},{0,96},{64,97},{35,2}... | collective-permute-start | bytes 1769480 | tf_op jit(solution)/shard_map/ppermute | solution.py:494
  101.5 15.5 %collective-permute-start.9 = (bf16[256,384]{1,0:T(8,128)(2,1)}, bf16[256,384]{1,0:T(8,128)(2,1)}, u32[]{:S(2)}, u32[]{:S(2)}) collective-permute-start(bf16[256,384]{1,0:T(8,128)(2,1)} %get-tuple-element.85), channel_id=1, source_target_pairs={{0,2},{2,0},{4,6},{6,4},{1,3},{3,1},{5,7},{7,5},{8,10},{10,8},{12,... | collective-permute-start | bytes 589832 | tf_op jit(solution)/shard_map/ppermute | solution.py:511
  204.1 34.8 %all-to-all-start.4 = ((bf16[32,24,1536]{2,1,0:T(8,128)(2,1)}), bf16[32,24,1536]{2,1,0:T(8,128)(2,1)}, u32[]{:S(2)}, u32[]{:S(2)}) async-start(bf16[32,24,1536]{2,1,0:T(8,128)(2,1)} %bitcast.151), calls=%async_computation.4 | async-start | bytes 4718592 | tf_op jit(solution)/shard_map/all_to_all | solution.py:48
  302.1 35.1 %all-to-all-start.6 = ((bf16[32,24,1536]{2,1,0:T(8,128)(2,1)}), bf16[32,24,1536]{2,1,0:T(8,128)(2,1)}, u32[]{:S(2)}, u32[]{:S(2)}) async-start(bf16[32,24,1536]{2,1,0:T(8,128)(2,1)} %bitcast.152), calls=%async_computation.6 | async-start | bytes 4718592 | tf_op jit(solution)/shard_map/all_to_all | solution.py:48
  342.8 55.5 %collective-permute-start.21 = (bf16[1536,768]{1,0:T(8,128)(2,1)}, bf16[1536,768]{1,0:T(8,128)(2,1)}, u32[]{:S(2)}, u32[]{:S(2)}) collective-permute-start(bf16[1536,768]{1,0:T(8,128)(2,1)} %add_convert_fusion.1), channel_id=1, source_target_pairs={{0,64},{64,0},{1,65},{65,1},{2,66},{66,2},{3,67},{67,3},{4,68},{68... | collective-permute-start | bytes 7077896 | tf_op jit(solution)/shard_map/ppermute | solution.py:598
  352.8 45.5 %all-to-all-start.7 = ((bf16[16,4,24,768]{3,2,1,0:T(8,128)(2,1)}), bf16[16,4,24,768]{3,2,1,0:T(8,128)(2,1)}, u32[]{:S(2)}, u32[]{:S(2)}) async-start(bf16[16,4,24,768]{3,2,1,0:T(8,128)(2,1)} %bitcast.141), calls=%async_computation.7 | async-start | bytes 4718592 | tf_op jit(solution)/shard_map/all_to_all | solution.py:48
  398.3 38.2 %all-to-all-start.8 = ((bf16[16,256,256]{2,1,0:T(8,128)(2,1)}), bf16[16,256,256]{2,1,0:T(8,128)(2,1)}, u32[]{:S(2)}, u32[]{:S(2)}) async-start(bf16[16,256,256]{2,1,0:T(8,128)(2,1)} %get-tuple-element.121), calls=%async_computation.8 | async-start | bytes 4194304 | tf_op jit(solution)/shard_map/all_to_all | solution.py:48
  406.4 29.1 %collective-permute-start.23 = (bf16[384,1536]{1,0:T(8,128)(2,1)S(1)}, bf16[384,1536]{1,0:T(8,128)(2,1)S(1)}, u32[]{:S(2)}, u32[]{:S(2)}) collective-permute-start(bf16[384,1536]{1,0:T(8,128)(2,1)S(1)} %copy-done.54), channel_id=1, source_target_pairs={{0,64},{64,0},{1,65},{65,1},{2,66},{66,2},{3,67},{67,3},{4,68},{68... | collective-permute-start | bytes 3538952 | tf_op jit(solution)/shard_map/ppermute | solution.py:599
  410.1 26.4 %collective-permute-start.25 = (bf16[128,1536]{1,0:T(8,128)(2,1)S(1)}, bf16[128,1536]{1,0:T(8,128)(2,1)}, u32[]{:S(2)}, u32[]{:S(2)}) collective-permute-start(bf16[128,1536]{1,0:T(8,128)(2,1)S(1)} %add_convert_fusion.3), channel_id=1, source_target_pairs={{0,2},{2,0},{4,6},{6,4},{1,3},{3,1},{5,7},{7,5},{8,10},{10,8},{12,... | collective-permute-start | bytes 1179656 | tf_op jit(solution)/shard_map/ppermute | solution.py:616
  457.4 41.8 %all-to-all-start.9 = ((bf16[64,24,768]{2,1,0:T(8,128)(2,1)}), bf16[64,24,768]{2,1,0:T(8,128)(2,1)S(1)}, u32[]{:S(2)}, u32[]{:S(2)}) async-start(bf16[64,24,768]{2,1,0:T(8,128)(2,1)} %bitcast.139), calls=%async_computation.9 | async-start | bytes 4718592 | tf_op jit(solution)/shard_map/all_to_all | solution.py:48
  470.3 26.1 %collective-permute-start.31 = (bf16[2,12,768]{2,0,1:T(2,128)(2,1)S(1)}, bf16[2,12,768]{2,0,1:T(2,128)(2,1)S(1)}, u32[]{:S(2)}, u32[]{:S(2)}) collective-permute-start(bf16[2,12,768]{2,0,1:T(2,128)(2,1)S(1)} %bitcast.165), channel_id=1, source_target_pairs={{0,33},{1,97},{32,1},{33,65},{64,32},{65,96},{96,0},{97,64},{2,35}... | collective-permute-start | bytes 110600 | tf_op jit(solution)/shard_map/ppermute | solution.py:657
  472.9 23.5 %collective-permute-start.30 = (bf16[2,12,768]{2,0,1:T(2,128)(2,1)S(1)}, bf16[2,12,768]{2,0,1:T(2,128)(2,1)S(1)}, u32[]{:S(2)}, u32[]{:S(2)}) collective-permute-start(bf16[2,12,768]{2,0,1:T(2,128)(2,1)S(1)} %bitcast.166), channel_id=1, source_target_pairs={{0,1},{1,65},{32,33},{33,97},{64,0},{65,64},{96,32},{97,96},{2,3},... | collective-permute-start | bytes 110600 | tf_op jit(solution)/shard_map/ppermute | solution.py:657
  475.0 22.0 %collective-permute-start.29 = (bf16[2,12,768]{2,0,1:T(2,128)(2,1)S(1)}, bf16[2,12,768]{2,0,1:T(2,128)(2,1)S(1)}, u32[]{:S(2)}, u32[]{:S(2)}) collective-permute-start(bf16[2,12,768]{2,0,1:T(2,128)(2,1)S(1)} %bitcast.167), channel_id=1, source_target_pairs={{0,32},{1,96},{32,0},{33,64},{64,33},{65,97},{96,1},{97,65},{2,34}... | collective-permute-start | bytes 110600 | tf_op jit(solution)/shard_map/ppermute | solution.py:657
  475.2 23.2 %collective-permute-start.28 = (bf16[2,12,768]{2,0,1:T(2,128)(2,1)S(1)}, bf16[2,12,768]{2,0,1:T(2,128)(2,1)S(1)}, u32[]{:S(2)}, u32[]{:S(2)}) collective-permute-start(bf16[2,12,768]{2,0,1:T(2,128)(2,1)S(1)} %bitcast.169), channel_id=1, source_target_pairs={{0,0},{1,64},{32,32},{33,96},{64,1},{65,65},{96,33},{97,97},{2,2},... | collective-permute-start | bytes 110600 | tf_op jit(solution)/shard_map/ppermute | solution.py:657
  (111 other events, 992.4 us)

commit v3 on v2

v3 whole, which is shorter than its diff:
```python
import math

import jax
import jax.numpy as jnp
import numpy as np
from jax import lax
from jax.experimental import pallas as pl
from jax.experimental.pallas import tpu as pltpu
from jax.sharding import PartitionSpec as P

HEAD_SIZE = 128
GROUP = 6
HALF_WIDTH = GROUP * HEAD_SIZE
WINDOW = 4096
CAP = 24
EXPERTS = 32
FAR_BYTES = 60 * 1024 * 1024
NEAR_BYTES = 24 * 1024 * 1024

NORM_EPS = 1e-06
ROPE_BASE = 1000000.0
MASKED = -1e30
SCALE = HEAD_SIZE ** (-0.5)
SCALE_LOG2 = SCALE * math.log2(math.e)

ALL = ("xh", "xl", "y", "z", "c")
CHIPS = ("xh", "xl", "y", "z")
HALF_CHIPS = ("xl", "y", "z")
PLANE_CHIPS = ("y", "z")
SWAP = [(0, 1), (1, 0)]
PAIR = [(0, 1), (1, 0), (2, 3), (3, 2)]

f32 = jnp.float32
bf16 = jnp.bfloat16


def dot(a, b, dims=((1,), (0,))):
    return lax.dot_general(a, b, (dims, ((), ())), preferred_element_type=f32)


NT = ((1,), (1,))
TN = ((0,), (0,))


def core_swap(value):
    return lax.ppermute(value, "c", SWAP)


def exchange(value, axes):
    return lax.all_to_all(value, axes, 0, 0, tiled=True)


def of_core(core, rows, own):
    upper, lower = jnp.split(rows, 2)
    return jnp.where((core == 0) == own, upper, lower)


def doc_begin(positions, doc_starts):
    before = doc_starts[None, :] <= positions[:, None]
    return jnp.max(jnp.where(before, doc_starts[None, :], 0), axis=-1)


def rope_tables(offset):
    column = jnp.arange(HEAD_SIZE, dtype=jnp.int32)
    half = HEAD_SIZE // 2
    inv_freq = jnp.exp((column % half).astype(f32) * (-2.0 * math.log(ROPE_BASE) / HEAD_SIZE))
    angle = offset.astype(f32)[:, None] * inv_freq[None, :]
    return jnp.cos(angle), jnp.where(column[None, :] < half, -1.0, 1.0) * jnp.sin(angle)


def norm_backward(values, inverse, gain_row, incoming_grad):
    scaled = incoming_grad * gain_row
    input_grad = inverse * scaled - values * inverse * inverse * inverse * jnp.mean(
        scaled * values, axis=-1, keepdims=True
    )
    gain_grad = jnp.sum(incoming_grad * values * inverse, axis=0, keepdims=True)
    return (input_grad, gain_grad)


def block_mask(low, t, blocks, rows, key_axis):
    key_at = lax.broadcasted_iota(jnp.int32, (rows, rows), key_axis)
    allowed = key_at >= low - t * rows
    if t == blocks - 1:
        allowed = allowed & (key_at <= lax.broadcasted_iota(jnp.int32, (rows, rows), 1 - key_axis))
    return allowed


def seen_block(spot, keys_ref, own_ref, t):
    spots = keys_ref.shape[0]
    return own_ref if t == spots else keys_ref.at[lax.rem(spot + t, spots)]


def side_block(place_ref, mine_ref, theirs_ref):
    mine = pl.program_id(0) // (GROUP // 2) == place_ref[2]
    return jnp.where(mine, mine_ref[...], theirs_ref[...])


def attend_kernel(
    place_ref, low_ref, mine_ref, theirs_ref, keys_ref, own_ref, out_ref, low_out_ref, log_ref, score_ref
):
    blocks, rows = keys_ref.shape[0] + 1, mine_ref.shape[0]
    query = side_block(place_ref, mine_ref, theirs_ref)
    spot = place_ref[1]
    low = low_ref[:, 0:1]
    top = None
    for t in range(blocks):
        score = dot(query, seen_block(spot, keys_ref, own_ref, t)[:, :HEAD_SIZE], NT)
        score = jnp.where(block_mask(low, t, blocks, rows, 1), score, MASKED)
        score_ref[t] = score
        part = jnp.maximum(score[:, :HEAD_SIZE], score[:, HEAD_SIZE:])
        top = part if top is None else jnp.maximum(top, part)
    top = jnp.max(top, axis=1, keepdims=True) * SCALE_LOG2
    total = jnp.zeros((rows, HEAD_SIZE), f32)
    mixed = jnp.zeros((rows, HEAD_SIZE), f32)
    for t in range(blocks):
        weights = jnp.exp2(score_ref[t] * SCALE_LOG2 - top)
        total = total + weights[:, :HEAD_SIZE] + weights[:, HEAD_SIZE:]
        value = seen_block(spot, keys_ref, own_ref, t)[:, HEAD_SIZE:]
        mixed = mixed + dot(weights.astype(bf16), value)
    total = jnp.sum(total, axis=1, keepdims=True)
    log_ref[0] = jnp.broadcast_to(top + jnp.log2(total), (rows, HEAD_SIZE)).T[:8]
    mixed = mixed / total
    out_ref[...] = mixed
    low_out_ref[...] = mixed.astype(bf16)


def attend(place, low, mine, theirs, keys, own):
    blocks, rows = keys.shape[0] + 1, mine.shape[0]
    whole = lambda *shape: pl.BlockSpec(shape, lambda h, place: (0,) * len(shape))
    by_head = pl.BlockSpec((rows, HEAD_SIZE), lambda h, place: (0, h))
    by_half = pl.BlockSpec((rows, HEAD_SIZE), lambda h, place: (0, lax.rem(h, GROUP // 2)))
    return pl.pallas_call(
        attend_kernel,
        grid_spec=pltpu.PrefetchScalarGridSpec(
            num_scalar_prefetch=1,
            grid=(GROUP,),
            in_specs=[whole(rows, HEAD_SIZE), by_half, by_half, whole(*keys.shape), whole(*own.shape)],
            out_specs=[by_head, by_head, pl.BlockSpec((1, 8, rows), lambda h, place: (h, 0, 0))],
            scratch_shapes=[pltpu.VMEM((blocks, rows, rows), f32)],
        ),
        out_shape=[
            jax.ShapeDtypeStruct((rows, HALF_WIDTH), f32),
            jax.ShapeDtypeStruct((rows, HALF_WIDTH), bf16),
            jax.ShapeDtypeStruct((GROUP, 8, rows), f32),
        ],
        compiler_params=pltpu.CompilerParams(vmem_limit_bytes=FAR_BYTES),
        cost_estimate=pl.CostEstimate(flops=20_000_000_000, bytes_accessed=4_000_000, transcendentals=7_000_000),
        name="attend",
    )(place, low, mine, theirs, keys, own)


def pack_kernel(core_ref, key_ref, value_ref, gain_ref, query_ref, out_weight_ref, own_ref, other_ref):
    for k in range(2):
        at = slice(k * HEAD_SIZE, (k + 1) * HEAD_SIZE)
        wide = slice(k * HALF_WIDTH, (k + 1) * HALF_WIDTH)
        parts = [key_ref[:, at], value_ref[:, at], gain_ref[...], query_ref[:, wide], out_weight_ref[:, wide]]
        part = jnp.concatenate(parts, axis=1)

        @pl.when(core_ref[0] == k)
        def _(part=part):
            own_ref[...] = part

        @pl.when(core_ref[0] != k)
        def _(part=part):
            other_ref[...] = part


def unpack_kernel(core_ref, own_ref, other_ref, weights_ref, out_ref):
    rows = own_ref.shape[0]
    at = lax.broadcasted_iota(jnp.int32, (2 * rows, rows), 0) - lax.broadcasted_iota(jnp.int32, (2 * rows, rows), 1)
    place = lambda first: jnp.where(at == first, 1.0, 0.0).astype(bf16)
    core = core_ref[0]
    full = (dot(place(core * rows), own_ref[...]) + dot(place((1 - core) * rows), other_ref[...])).astype(bf16)
    kv_width, quarter = 3 * HEAD_SIZE, HALF_WIDTH // 2
    for k in range(2):
        first = kv_width + k * quarter
        part = jnp.concatenate([full[:, :kv_width], full[:, first : first + quarter]], axis=1)
        for chip in range(k, weights_ref.shape[0], 2):
            weights_ref[chip] = part
    for spot in range(out_ref.shape[0]):
        out_ref[spot] = full[:, kv_width + HALF_WIDTH :]


def place_rows_kernel(route_ref, gate_ref, placed_ref, placed_by_token_ref, token_gate_ref, slot_gate_ref):
    tokens, top = route_ref.shape
    slots = EXPERTS * CAP
    expert = lax.broadcasted_iota(jnp.int32, (tokens, HEAD_SIZE), 1)
    chosen = jnp.zeros((tokens, HEAD_SIZE), f32)
    gate = jnp.zeros((tokens, HEAD_SIZE), f32)
    for k in range(top):
        hit = route_ref[:, k : k + 1] == expert
        chosen = chosen + jnp.where(hit, 1.0, 0.0)
        gate = gate + jnp.where(hit, gate_ref[:, k : k + 1], 0.0)
    square = (tokens, tokens)
    earlier = lax.broadcasted_iota(jnp.int32, square, 1) < lax.broadcasted_iota(jnp.int32, square, 0)
    chosen = chosen.astype(bf16)
    before = dot(jnp.where(earlier, 1.0, 0.0).astype(bf16), chosen)
    first = lax.broadcasted_iota(jnp.int32, (HEAD_SIZE, slots), 0) * CAP
    slot = lax.broadcasted_iota(jnp.int32, (HEAD_SIZE, slots), 1)
    within = (slot >= first) & (slot < first + CAP)
    spread = jnp.where(within, 1.0, 0.0).astype(bf16)
    slot_in = jnp.sum(jnp.where(within, slot - first, 0).astype(f32), axis=0, keepdims=True)
    here = (dot(chosen, spread) > 0.5) & (jnp.abs(dot(before.astype(bf16), spread) - slot_in) < 0.5)
    high = gate.astype(bf16)
    low = (gate - high.astype(f32)).astype(bf16)
    high_at = jnp.where(here, dot(high, spread), 0.0)
    low_at = jnp.where(here, dot(low, spread), 0.0)
    placed = jnp.where(here, 1.0, 0.0)
    placed_by_token_ref[...] = placed.astype(bf16)
    by_slot = placed.T.astype(bf16)
    placed_ref[:, :tokens] = by_slot
    placed_ref[:, tokens:] = by_slot
    token_gate_ref[:tokens] = high_at.astype(bf16)
    token_gate_ref[tokens:] = low_at.astype(bf16)
    total = jnp.sum((high_at + low_at).T, axis=1, keepdims=True)
    slot_gate_ref[...] = jnp.broadcast_to(total, (slots, HEAD_SIZE))


def place_rows(routes, gates):
    tokens, slots = routes.shape[0], EXPERTS * CAP
    by_token = jax.ShapeDtypeStruct((tokens, slots), bf16)
    return pl.pallas_call(
        place_rows_kernel,
        out_shape=[
            jax.ShapeDtypeStruct((slots, 2 * tokens), bf16),
            by_token,
            jax.ShapeDtypeStruct((2 * tokens, slots), bf16),
            jax.ShapeDtypeStruct((slots, HEAD_SIZE), f32),
        ],
        compiler_params=pltpu.CompilerParams(vmem_limit_bytes=NEAR_BYTES),
        name="place_rows",
    )(routes, gates)


def normed_rows(values, gain_row):
    inverse = lax.rsqrt(jnp.mean(values * values, axis=-1, keepdims=True) + NORM_EPS)
    return (values * inverse * gain_row).astype(bf16)


def put_rows(target_ref, core, own, other):
    rows = own.shape[0]
    target_ref[pl.ds(pl.multiple_of(core * rows, rows), rows), :] = own
    target_ref[pl.ds(pl.multiple_of((1 - core) * rows, rows), rows), :] = other


def project_keys_kernel(
    place_ref, own_ref, other_ref, before_own_ref, before_other_ref, weight_ref,
    cosine_ref, sine_ref, before_cosine_ref, before_sine_ref,
    normed_ref, kv_ref, sent_ref, gain_ref, before_normed_ref, before_kv_ref,
):
    core, spot = place_ref[0], place_ref[1]
    pick = lax.broadcasted_iota(jnp.int32, (16, HEAD_SIZE), 0) == lax.broadcasted_iota(jnp.int32, (16, HEAD_SIZE), 1)
    gains = dot(pick.astype(bf16), weight_ref[:, 2 * HEAD_SIZE :], NT)
    gain_ref[...] = gains[:8]
    for rows_refs, tables, normed, target in (
        ((own_ref, other_ref), (cosine_ref, sine_ref), normed_ref, kv_ref),
        ((before_own_ref, before_other_ref), (before_cosine_ref, before_sine_ref), before_normed_ref, before_kv_ref),
    ):
        put_rows(normed, core, *(normed_rows(ref[...].astype(f32), gains[0:1]) for ref in rows_refs))
        linear = dot(normed[...], weight_ref[:, : 2 * HEAD_SIZE])
        key = linear[:, :HEAD_SIZE]
        turned = key * tables[0][...] + pltpu.roll(key, HEAD_SIZE // 2, 1) * tables[1][...]
        target[:, :HEAD_SIZE] = turned.astype(bf16)
        target[:, HEAD_SIZE:] = linear[:, HEAD_SIZE:].astype(bf16)
    for j in range(sent_ref.shape[0]):

        @pl.when(j > spot)
        def _(j=j):
            sent_ref[j] = kv_ref[...]

        @pl.when(j <= spot)
        def _(j=j):
            sent_ref[j] = before_kv_ref[...]


def project_keys(place, acts, before_acts, weights, cosine, sine, spots):
    rows, width = 2 * acts[0].shape[0], acts[0].shape[1]
    whole = lambda *shape: pl.BlockSpec(shape, lambda i: (0,) * len(shape))
    table = lambda k: pl.BlockSpec((rows, HEAD_SIZE), lambda i: (k, 0))
    half = whole(rows // 2, width)
    return pl.pallas_call(
        project_keys_kernel,
        grid=(1,),
        in_specs=[pl.BlockSpec(memory_space=pltpu.SMEM)]
        + [half] * 4
        + [whole(width, 3 * HEAD_SIZE), table(0), table(0), table(2), table(2)],
        out_specs=[
            whole(rows, width), whole(rows, 2 * HEAD_SIZE), whole(spots, rows, 2 * HEAD_SIZE), whole(8, width),
        ],
        out_shape=[
            jax.ShapeDtypeStruct((rows, width), bf16),
            jax.ShapeDtypeStruct((rows, 2 * HEAD_SIZE), bf16),
            jax.ShapeDtypeStruct((spots, rows, 2 * HEAD_SIZE), bf16),
            jax.ShapeDtypeStruct((8, width), f32),
        ],
        scratch_shapes=[pltpu.VMEM((rows, width), bf16), pltpu.VMEM((rows, 2 * HEAD_SIZE), bf16)],
        compiler_params=pltpu.CompilerParams(vmem_limit_bytes=FAR_BYTES),
        name="project_keys",
    )(place, *acts, *before_acts, weights, cosine, sine, cosine, sine)


def project_kernel(
    place_ref, rows_ref, own_ref, other_ref, gain_ref, weight_ref, cosine_ref, sine_ref, pair_cosine_ref, pair_sine_ref,
    normed_ref, out_ref, pair_out_ref,
):
    gain = gain_ref[0:1, :]
    put_rows(normed_ref, place_ref[0], *(normed_rows(ref[...].astype(f32), gain) for ref in (own_ref, other_ref)))
    for values_ref, cos_ref, sin_ref, target in (
        (rows_ref, cosine_ref, sine_ref, out_ref),
        (normed_ref, pair_cosine_ref, pair_sine_ref, pair_out_ref),
    ):
        linear = dot(values_ref[...], weight_ref[...])
        for h in range(GROUP // 2):
            at = slice(h * HEAD_SIZE, (h + 1) * HEAD_SIZE)
            head = linear[:, at]
            turned = head * cos_ref[...] + pltpu.roll(head, HEAD_SIZE // 2, 1) * sin_ref[...]
            target[:, at] = turned.astype(bf16)


def project(place, rows, pair_acts, gains, weights, cosine, sine):
    count, width = rows.shape
    quarter = HALF_WIDTH // 2
    whole = lambda *shape: pl.BlockSpec(shape, lambda i: (0,) * len(shape))
    table = lambda k: pl.BlockSpec((count, HEAD_SIZE), lambda i: (k, 0))
    half = whole(count // 2, width)
    shape = jax.ShapeDtypeStruct((count, quarter), bf16)
    return pl.pallas_call(
        project_kernel,
        grid=(1,),
        in_specs=[
            pl.BlockSpec(memory_space=pltpu.SMEM), whole(count, width), half, half, whole(8, width),
            pl.BlockSpec((width, quarter), lambda i: (0, 1)), table(0), table(0), table(1), table(1),
        ],
        out_specs=[whole(count, width), whole(count, quarter), whole(count, quarter)],
        out_shape=[jax.ShapeDtypeStruct(rows.shape, bf16), shape, shape],
        compiler_params=pltpu.CompilerParams(vmem_limit_bytes=FAR_BYTES),
        name="project",
    )(place, rows, *pair_acts, gains, weights, cosine, sine, cosine, sine)


def dispatch_kernel(branch_ref, came_ref, acts_ref, gain_ref, placed_ref, hidden_ref, rows_ref):
    hidden = acts_ref[...].astype(f32) + branch_ref[...] + came_ref[...]
    hidden_ref[...] = hidden
    rows_ref[...] = dot(placed_ref[:, : hidden.shape[0]], normed_rows(hidden, gain_ref[1:2, :])).astype(bf16)


def combine_kernel(
    valid_ref, scale_ref, returned_ref, token_gate_ref, hidden_ref, teacher_ref, placed_ref, gate_ref,
    out_ref, grad_ref, rows_ref,
):
    mixture = dot(token_gate_ref[...], returned_ref[...])
    tokens = hidden_ref.shape[0]
    hidden = hidden_ref[...] + mixture[:tokens] + mixture[tokens:]
    out_ref[...] = hidden.astype(bf16)
    position = valid_ref[1] + lax.broadcasted_iota(jnp.int32, hidden.shape, 0)
    grad = jnp.where(position < valid_ref[0], scale_ref[0] * (hidden - teacher_ref[...].astype(f32)), 0.0)
    grad_ref[...] = grad
    high = grad.astype(bf16)
    low = (grad - high.astype(f32)).astype(bf16)
    picked = dot(placed_ref[...], jnp.concatenate([high, low]))
    rows_ref[...] = (gate_ref[:, 0:1] * picked).astype(bf16)


def combine(bounds, scale, returned, token_gate, hidden, teacher, placed, gate):
    (slots, width), rows, steps = returned.shape, hidden.shape[0], 3
    whole = lambda shape: pl.BlockSpec(shape, lambda i: (0,) * len(shape))
    columns = lambda count: pl.BlockSpec((count, width // steps), lambda i: (0, i))
    smem = pl.BlockSpec(memory_space=pltpu.SMEM)
    return pl.pallas_call(
        combine_kernel,
        grid=(steps,),
        in_specs=[
            smem, smem, columns(slots), whole(token_gate.shape), columns(rows), columns(rows),
            whole(placed.shape), whole(gate.shape),
        ],
        out_specs=[columns(rows), columns(rows), columns(slots)],
        out_shape=[
            jax.ShapeDtypeStruct(hidden.shape, bf16),
            jax.ShapeDtypeStruct(hidden.shape, f32),
            jax.ShapeDtypeStruct(returned.shape, bf16),
        ],
        compiler_params=pltpu.CompilerParams(vmem_limit_bytes=FAR_BYTES),
        name="combine",
    )(bounds, scale, returned, token_gate, hidden, teacher, placed, gate)


def norm_back_kernel(returned_ref, placed_ref, hidden_ref, gain_ref, grad_ref, out_ref, low_out_ref, gain_grad_ref):
    hidden = hidden_ref[...]
    inverse = lax.rsqrt(jnp.mean(hidden * hidden, axis=-1, keepdims=True) + NORM_EPS)
    input_grad, gain_grad = norm_backward(
        hidden, inverse, gain_ref[1:2, :], dot(placed_ref[...], returned_ref[...])
    )
    total = grad_ref[...] + input_grad
    out_ref[...] = total
    low_out_ref[...] = total.astype(bf16)
    gain_grad_ref[...] = jnp.broadcast_to(gain_grad, gain_grad_ref.shape)


def query_columns_kernel(rows_ref, pair_rows_ref, grad_ref, pair_grad_ref, partial_ref):
    queries = dot(rows_ref[...], grad_ref[...], TN) + dot(pair_rows_ref[...], pair_grad_ref[...], TN)
    partial_ref[...] = queries.astype(bf16)


def split_grads_kernel(place_ref, came_ref, own_ref, later_ref, before_ref):
    spot = place_ref[1]
    later = own_ref[...].astype(f32)
    before = jnp.zeros_like(later)
    for j in range(came_ref.shape[0]):
        grad = came_ref[j].astype(f32)
        later = later + jnp.where(j > spot, grad, 0.0)
        before = before + jnp.where(j > spot, 0.0, grad)
    later_ref[...] = later
    before_ref[...] = before.astype(bf16)


def keys_back_kernel(
    place_ref, later_ref, next_ref, cosine_ref, sine_ref, rows_ref, weight_ref, side_ref,
    partial_ref, own_ref, other_ref, sum_ref,
):
    total = (later_ref[...] + next_ref[...].astype(f32)).astype(bf16)
    key = total[:, :HEAD_SIZE].astype(f32)
    turned = key * cosine_ref[...] - pltpu.roll(key, HEAD_SIZE // 2, 1) * sine_ref[...]
    linear = jnp.concatenate([turned.astype(bf16), total[:, HEAD_SIZE:]], axis=1)
    partial_ref[...] = dot(rows_ref[...], linear, TN).astype(bf16)
    sum_ref[...] = side_ref[...] + dot(linear, weight_ref[...], NT)
    core, rows = place_ref[0], own_ref.shape[0]
    own_ref[...] = sum_ref[pl.ds(pl.multiple_of(core * rows, rows), rows), :]
    other_ref[...] = sum_ref[pl.ds(pl.multiple_of((1 - core) * rows, rows), rows), :]


def acts_back_kernel(
    own_ref, swapped_ref, pair_ref, acts_ref, gain_ref, grad_ref, gain_grad_ref, keys_ref, queries_ref,
    out_ref, partial_ref,
):
    values = acts_ref[...].astype(f32)
    inverse = lax.rsqrt(jnp.mean(values * values, axis=-1, keepdims=True) + NORM_EPS)
    normed_grad = own_ref[...] + swapped_ref[...] + pair_ref[...].astype(f32)
    input_grad, gain_grad = norm_backward(values, inverse, gain_ref[0:1, :], normed_grad)
    out_ref[...] = grad_ref[...] + input_grad
    row = lax.broadcasted_iota(jnp.int32, (16, values.shape[1]), 0)
    gain_rows = jnp.where(row == 0, gain_grad, jnp.where(row == 1, gain_grad_ref[0:1, :], 0.0))
    square = (16, HEAD_SIZE)
    unit = lax.broadcasted_iota(jnp.int32, square, 0) == lax.broadcasted_iota(jnp.int32, square, 1)
    width = keys_ref.shape[1]
    partial_ref[:, :width] = keys_ref[...]
    partial_ref[:, width : width + HEAD_SIZE] = dot(gain_rows.astype(bf16), unit.astype(bf16), TN).astype(bf16)


def whole_call(
    kernel, name, out_shape, *args, words=0, scratch_shapes=(), blocks=(), out_blocks=(), aliases=(), near=True
):
    blocks, out_blocks = dict(blocks), dict(out_blocks)
    whole = lambda shape: pl.BlockSpec(shape, lambda i: (0,) * len(shape))
    specs = [
        pl.BlockSpec(memory_space=pltpu.SMEM) if k < words else blocks.get(k, whole(arg.shape))
        for k, arg in enumerate(args)
    ]
    return pl.pallas_call(
        kernel,
        grid=(1,),
        in_specs=specs,
        out_specs=[out_blocks.get(k, whole(out.shape)) for k, out in enumerate(out_shape)],
        out_shape=out_shape,
        input_output_aliases=dict(aliases),
        scratch_shapes=list(scratch_shapes),
        compiler_params=pltpu.CompilerParams(vmem_limit_bytes=NEAR_BYTES if near else FAR_BYTES),
        name=name,
    )(*args)


def piece_at(place_ref, k, shape):
    depth, width = shape
    row_half = lax.rem(place_ref[4] + k % 2, 2)
    column_half = lax.rem(place_ref[3] + k // 2, 2)
    return (
        pl.ds(pl.multiple_of(row_half * depth, HEAD_SIZE), depth),
        pl.ds(pl.multiple_of(column_half * width, HEAD_SIZE), width),
    )


def out_project_kernel(place_ref, attn_ref, *refs):
    pieces, (own_ref, other_ref, sum_ref) = refs[:-3], refs[-3:]
    rows = own_ref.shape[0]
    sum_ref[...] = jnp.zeros_like(sum_ref)
    for k, piece in enumerate(pieces):
        features, columns = piece_at(place_ref, k, piece.shape)
        sum_ref[:, columns] += dot(attn_ref[:, features], piece[...])
    core = place_ref[0]
    own_ref[...] = sum_ref[pl.ds(pl.multiple_of(core * rows, rows), rows), :]
    other_ref[...] = sum_ref[pl.ds(pl.multiple_of((1 - core) * rows, rows), rows), :]


def out_project(place, attn, pieces):
    rows, width = attn.shape[0], 2 * pieces[0].shape[1]
    shape = jax.ShapeDtypeStruct((rows // 2, width), f32)
    vmem = pl.BlockSpec(memory_space=pltpu.VMEM)
    return pl.pallas_call(
        out_project_kernel,
        in_specs=[pl.BlockSpec(memory_space=pltpu.SMEM)] + [vmem] * (1 + len(pieces)),
        out_specs=[vmem, vmem],
        out_shape=[shape, shape],
        scratch_shapes=[pltpu.VMEM((rows, width), f32)],
        compiler_params=pltpu.CompilerParams(vmem_limit_bytes=NEAR_BYTES),
        name="out_project",
    )(place, attn, *pieces)


def out_project_back_kernel(place_ref, own_ref, other_ref, attn_ref, *refs):
    pieces, (out_ref, partial_ref, grad_ref, sum_ref) = refs[:-4], refs[-4:]
    put_rows(grad_ref, place_ref[0], own_ref[...], other_ref[...])
    sum_ref[...] = jnp.zeros_like(sum_ref)
    for k, piece in enumerate(pieces):
        features, columns = piece_at(place_ref, k, piece.shape)
        sum_ref[:, features] += dot(grad_ref[:, columns], piece[...], NT)
    out_ref[...] = sum_ref[...].astype(bf16)
    spots, planes, rows, width = partial_ref.shape
    for h in range(2):
        partial = dot(attn_ref[...], grad_ref[:, h * width : (h + 1) * width], TN)
        for l in range(planes // 2):
            for j in range(spots):
                first = (l * spots + j) * rows
                partial_ref[j, h * (planes // 2) + l] = partial[first : first + rows].astype(bf16)


def out_project_back(place, own, other, attn, pieces, spots):
    rows, width = attn.shape
    vmem = pl.BlockSpec(memory_space=pltpu.VMEM)
    return pl.pallas_call(
        out_project_back_kernel,
        in_specs=[pl.BlockSpec(memory_space=pltpu.SMEM)] + [vmem] * (3 + len(pieces)),
        out_specs=[vmem, vmem],
        out_shape=[
            jax.ShapeDtypeStruct((rows, width), bf16),
            jax.ShapeDtypeStruct((spots, 4, width // (2 * spots), width), bf16),
        ],
        scratch_shapes=[pltpu.VMEM((rows, 2 * width), bf16), pltpu.VMEM((rows, width), f32)],
        compiler_params=pltpu.CompilerParams(vmem_limit_bytes=FAR_BYTES),
        name="out_project_back",
    )(place, own, other, attn, *pieces)


def attend_back_kernel(
    place_ref, low_ref, mine_ref, theirs_ref, cosine_ref, sine_ref, keys_ref, own_ref, out_ref, grad_ref, log_ref,
    query_grad_ref, keys_grad_ref, own_grad_ref, sum_ref, turned_key_ref, weight_ref, score_ref,
):
    h, heads = pl.program_id(0), pl.num_programs(0)
    blocks, rows = keys_ref.shape[0] + 1, mine_ref.shape[0]
    spot = place_ref[1]

    @pl.when(h == 0)
    def _():
        sum_ref[...] = jnp.zeros_like(sum_ref)
        for t in range(blocks):
            turned_key_ref[t] = seen_block(spot, keys_ref, own_ref, t)[:, :HEAD_SIZE].T

    query, out_grad = side_block(place_ref, mine_ref, theirs_ref), grad_ref[...]
    delta = jnp.sum((out_grad.astype(f32) * out_ref[...]).T, axis=0, keepdims=True)
    log_total, low = log_ref[0, 0:1, :], low_ref[0:1, :]
    for t in range(blocks):
        block = seen_block(spot, keys_ref, own_ref, t)
        key, value = block[:, :HEAD_SIZE], block[:, HEAD_SIZE:]
        weights = jnp.exp2(dot(key, query, NT) * SCALE_LOG2 - log_total)
        weights = jnp.where(block_mask(low, t, blocks, rows, 0), weights, 0.0)
        weight_ref[t] = weights.astype(bf16)
        score_ref[t] = (weights * (dot(value, out_grad, NT) - delta)).astype(bf16)
    query_grad = jnp.zeros((HEAD_SIZE, rows), f32)
    for t in range(blocks):
        query_grad = query_grad + dot(turned_key_ref[t], score_ref[t])
    query_grad = (query_grad * SCALE).T.astype(bf16).astype(f32)
    turned = query_grad * cosine_ref[...] - pltpu.roll(query_grad, HEAD_SIZE // 2, 1) * sine_ref[...]
    query_grad_ref[...] = turned.astype(bf16)
    for t in range(blocks):
        sum_ref[t, :, :HEAD_SIZE] += dot(score_ref[t], query)
        sum_ref[t, :, HEAD_SIZE:] += dot(weight_ref[t], out_grad)

    @pl.when(h == heads - 1)
    def _():
        for t in range(blocks):
            target = seen_block(spot, keys_grad_ref, own_grad_ref, t)
            target[:, :HEAD_SIZE] = (sum_ref[t, :, :HEAD_SIZE] * SCALE).astype(bf16)
            target[:, HEAD_SIZE:] = sum_ref[t, :, HEAD_SIZE:].astype(bf16)


def attend_back(place, low, mine, theirs, cosine, sine, keys, own, out, out_grad, log_total):
    blocks, rows = keys.shape[0] + 1, mine.shape[0]
    whole = lambda *shape: pl.BlockSpec(shape, lambda h, place: (0,) * len(shape))
    by_head = pl.BlockSpec((rows, HEAD_SIZE), lambda h, place: (0, h))
    by_half = pl.BlockSpec((rows, HEAD_SIZE), lambda h, place: (0, lax.rem(h, GROUP // 2)))
    table = pl.BlockSpec((rows, HEAD_SIZE), lambda h, place: (0, 0))
    return pl.pallas_call(
        attend_back_kernel,
        grid_spec=pltpu.PrefetchScalarGridSpec(
            num_scalar_prefetch=1,
            grid=(GROUP,),
            in_specs=[
                whole(8, rows), by_half, by_half, table, table, whole(*keys.shape), whole(*own.shape), by_head, by_head,
                pl.BlockSpec((1, 8, rows), lambda h, place: (h, 0, 0)),
            ],
            out_specs=[by_head, whole(*keys.shape), whole(*own.shape)],
            scratch_shapes=[
                pltpu.VMEM((blocks, rows, 2 * HEAD_SIZE), f32),
                pltpu.VMEM((blocks, HEAD_SIZE, rows), bf16),
                pltpu.VMEM((blocks, rows, rows), bf16),
                pltpu.VMEM((blocks, rows, rows), bf16),
            ],
        ),
        out_shape=[
            jax.ShapeDtypeStruct((rows, HALF_WIDTH), bf16),
            jax.ShapeDtypeStruct(keys.shape, bf16),
            jax.ShapeDtypeStruct(own.shape, bf16),
        ],
        compiler_params=pltpu.CompilerParams(vmem_limit_bytes=FAR_BYTES),
        cost_estimate=pl.CostEstimate(flops=28_000_000_000, bytes_accessed=8_000_000, transcendentals=7_000_000),
        name="attend_back",
    )(place, low, mine, theirs, cosine, sine, keys, own, out, out_grad, log_total)


def body(
    acts, teacher, valid, doc_starts, routes, gates,
    w_query, key_weight, value_weight, w_out, gain_attn, gain_ffn, w_gate, w_up, w_down,
):
    half, core = lax.axis_index("xh"), lax.axis_index("c")
    plane, spot = lax.axis_index(("xh", "xl")), lax.axis_index(PLANE_CHIPS)
    chip = lax.axis_index(CHIPS)
    tok_rows, model_dim = acts.shape
    chip_rows = 2 * tok_rows
    spots = lax.axis_size(PLANE_CHIPS)
    planes = lax.axis_size(("xh", "xl"))
    chips = spots * planes
    total_tokens = chips * chip_rows
    shard_rows = w_query.shape[0]

    side = chip % 2
    place = jnp.stack([core, spot, side, half, lax.axis_index("xl")]).astype(jnp.int32)
    gain_pair = jnp.pad(jnp.stack([gain_attn, gain_ffn], axis=1), ((0, 0), (0, HEAD_SIZE - 2)))
    kv_width = 3 * HEAD_SIZE
    quarter = HALF_WIDTH // 2
    core_word = core.astype(jnp.int32).reshape(1)
    packed = jax.ShapeDtypeStruct((shard_rows, kv_width + 2 * HALF_WIDTH), bf16)
    own_part, other_part = whole_call(
        pack_kernel, "pack", [packed, packed], core_word, key_weight, value_weight, gain_pair, w_query, w_out, words=1
    )
    weights_sent, out_sent = whole_call(
        unpack_kernel, "unpack",
        [
            jax.ShapeDtypeStruct((chips, 2 * shard_rows, kv_width + quarter), bf16),
            jax.ShapeDtypeStruct((spots, 2 * shard_rows, HALF_WIDTH), bf16),
        ],
        core_word, own_part, core_swap(other_part), words=1,
    )
    weights = exchange(weights_sent, CHIPS)

    first_token = chip * chip_rows
    chip_pos = first_token + jnp.arange(chip_rows, dtype=jnp.int32)
    begin = doc_begin(chip_pos, doc_starts)
    table_pos = jnp.concatenate([chip_pos, chip_pos + (1 - 2 * side) * chip_rows, chip_pos - spots * chip_rows])
    cosine, sine = rope_tables(table_pos - doc_begin(table_pos, doc_starts))
    low = jnp.maximum(begin, chip_pos - (WINDOW - 1)) - (first_token - WINDOW)
    low_rows = jnp.broadcast_to(low[None, :], (8, chip_rows))
    low_columns = jnp.broadcast_to(low[:, None], (chip_rows, HEAD_SIZE))
    block_at = jnp.arange(spots, dtype=jnp.int32)

    own_acts, cosine, sine, low_columns, out_sent = lax.optimization_barrier((acts, cosine, sine, low_columns, out_sent))
    chip_acts = (own_acts, core_swap(acts))
    pair_acts = lax.ppermute(own_acts, "z", PAIR)
    pair_acts = (pair_acts, core_swap(pair_acts))
    before_acts = lax.ppermute(own_acts, ("xh", "xl"), [(p, p + 1) for p in range(planes - 1)])
    before_acts = (before_acts, core_swap(before_acts))

    weights, out_sent, chip_acts, pair_acts, before_acts, low_columns, cosine, sine = lax.optimization_barrier(
        (weights, out_sent, chip_acts, pair_acts, before_acts, low_columns, cosine, sine)
    )
    out_rows = exchange(out_sent, PLANE_CHIPS)
    weights = weights.reshape(model_dim, -1)

    normed_one, own_kv, kv_sent, gain_rows = project_keys(
        place, chip_acts, before_acts, weights, cosine, sine, spots
    )
    kv_sent, out_rows = lax.optimization_barrier((kv_sent, out_rows))
    seen_kv = exchange(kv_sent, PLANE_CHIPS)
    placed, placed_by_token, token_gate, slot_gate = place_rows(routes, gates)
    all_slots = EXPERTS * CAP

    out_rows = out_rows.reshape(-1, HALF_WIDTH)
    out_pieces = [
        lax.ppermute(
            out_rows,
            ("xh", "xl", "c"),
            [
                (c * 4 + (l ^ k % 2) * 2 + (h ^ k // 2), h * 4 + l * 2 + c)
                for h in range(2)
                for l in range(2)
                for c in range(2)
            ],
        )
        for k in range(4)
    ]
    seen_kv, out_pieces = lax.optimization_barrier((seen_kv, out_pieces))

    pair_normed, query_mine, query_theirs = project(
        place, normed_one, pair_acts, gain_rows, weights, cosine, sine
    )
    query_theirs = lax.ppermute(query_theirs, "z", PAIR)
    query_theirs, placed, slot_gate, token_gate, placed_by_token = lax.optimization_barrier(
        (query_theirs, placed, slot_gate, token_gate, placed_by_token)
    )
    attn_wide, attn, log_total = attend(place, low_columns, query_mine, query_theirs, seen_kv, own_kv)

    branch, other_branch = out_project(place, attn, out_pieces)
    wide = jax.ShapeDtypeStruct((tok_rows, model_dim), f32)
    slim = jax.ShapeDtypeStruct((tok_rows, model_dim), bf16)
    slot_rows = jax.ShapeDtypeStruct((all_slots, model_dim), bf16)
    hidden_one, sent_rows = whole_call(
        dispatch_kernel, "dispatch", [wide, slot_rows], branch, core_swap(other_branch), acts, gain_rows, placed
    )

    def to_experts(rows):
        mine = exchange(rows.reshape(EXPERTS, CAP, model_dim), HALF_CHIPS).reshape(all_slots, model_dim)
        return mine, core_swap(mine)

    def from_experts(mine, theirs):
        both = mine + core_swap(theirs.astype(bf16)).astype(f32)
        both = both.astype(bf16).reshape(EXPERTS, CAP, model_dim)
        return exchange(both, HALF_CHIPS).reshape(all_slots, model_dim)

    units = w_gate.shape[1]
    gate_up = jnp.concatenate([w_gate, w_up], axis=1)

    def expert_hidden(rows):
        both = dot(rows, gate_up)
        gate_pre, up_pre = both[:, :units], both[:, units:]
        return gate_pre, up_pre, (jax.nn.silu(gate_pre) * up_pre).astype(bf16)

    def hidden_backward(kept, grad_rows):
        gate_pre, up_pre = kept[0], kept[1]
        grad_hidden = dot(grad_rows, w_down, NT)
        sigmoid = jax.nn.sigmoid(gate_pre)
        grad_gate = (grad_hidden * up_pre * sigmoid * (1.0 + gate_pre * (1.0 - sigmoid))).astype(bf16)
        grad_up = (grad_hidden * gate_pre * sigmoid).astype(bf16)
        return jnp.concatenate([grad_gate, grad_up], axis=1)

    def rows_backward(back):
        return dot(back, gate_up, NT)

    rows_mine, rows_theirs = to_experts(sent_rows)
    kept_mine = expert_hidden(rows_mine)
    kept_mine, rows_theirs = lax.optimization_barrier((kept_mine, rows_theirs))
    kept_theirs = expert_hidden(rows_theirs)
    returned = from_experts(dot(kept_mine[2], w_down), dot(kept_theirs[2], w_down))
    bounds = jnp.stack([valid[0], first_token + core * tok_rows]).astype(jnp.int32)
    loss_scale = (total_tokens / valid.astype(f32)).reshape(1)
    activations, grad_two, grad_slots = combine(
        bounds, loss_scale, returned, token_gate, hidden_one, teacher, placed, slot_gate
    )
    grads_mine, grads_theirs = to_experts(grad_slots)
    back_mine = hidden_backward(kept_mine, grads_mine)
    back_mine, grads_theirs = lax.optimization_barrier((back_mine, grads_theirs))
    back_theirs = hidden_backward(kept_theirs, grads_theirs)
    grad_returned = from_experts(rows_backward(back_mine), rows_backward(back_theirs))

    expert_parts = (
        (dot(rows_mine, back_mine, TN) + dot(rows_theirs, back_theirs, TN)).astype(bf16),
        (dot(kept_mine[2], grads_mine, TN) + dot(kept_theirs[2], grads_theirs, TN)).astype(bf16),
    )
    expert_part = jnp.concatenate(
        [expert_parts[0], expert_parts[1][:, :HALF_WIDTH], expert_parts[1][:, HALF_WIDTH:]]
    )

    expert_part, grad_returned = lax.optimization_barrier((expert_part, grad_returned))
    grad_one, grad_branch, gain_two_grad = whole_call(
        norm_back_kernel, "norm_back", [wide, slim, jax.ShapeDtypeStruct((8, model_dim), f32)],
        grad_returned, placed_by_token, hidden_one, gain_rows, grad_two, near=False,
    )
    grad_attn, out_partial = out_project_back(place, grad_branch, core_swap(grad_branch), attn, out_pieces, spots)

    def send_to_chips(partial):
        return exchange(partial.astype(bf16).reshape(chips, 2 * shard_rows, -1), CHIPS)

    expert_other = lax.ppermute(expert_part, "xh", SWAP)
    out_received = exchange(out_partial, PLANE_CHIPS)

    query_lin_grad, kv_grad, own_kv_grad = attend_back(
        place, low_rows, query_mine, query_theirs, cosine, sine, seen_kv, own_kv, attn_wide, grad_attn, log_total
    )
    query_left, query_right = query_lin_grad[:, :quarter], query_lin_grad[:, quarter:]
    pair_query_grad = lax.ppermute(jnp.where(side == 0, query_right, query_left), "z", PAIR)
    kv_grad, out_received = lax.optimization_barrier((kv_grad, out_received))
    came = exchange(kv_grad, PLANE_CHIPS)
    side_query_grad = jnp.where(side == 0, query_left, query_right)
    pair_normed_grad = dot(pair_query_grad, weights[:, kv_width:], NT)
    pair_normed_grad = of_core(core, pair_normed_grad, True) + core_swap(of_core(core, pair_normed_grad, False))
    back_normed_grad = lax.ppermute(pair_normed_grad.astype(bf16), "z", PAIR)
    side_normed_grad = dot(side_query_grad, weights[:, kv_width:], NT)
    came, expert_other, side_query_grad, pair_query_grad = lax.optimization_barrier(
        (came, expert_other, side_query_grad, pair_query_grad)
    )
    square = (chip_rows, 2 * HEAD_SIZE)
    later_grad, before_grad = whole_call(
        split_grads_kernel, "split_grads", [jax.ShapeDtypeStruct(square, f32), jax.ShapeDtypeStruct(square, bf16)],
        place, came, own_kv_grad, words=1,
    )
    next_grad = lax.ppermute(before_grad, ("xh", "xl"), [(p + 1, p) for p in range(planes - 1)])
    (partial,) = whole_call(
        query_columns_kernel, "query_columns", [jax.ShapeDtypeStruct((model_dim, 2 * quarter), bf16)],
        normed_one, pair_normed, side_query_grad, pair_query_grad,
        out_blocks={0: pl.BlockSpec((model_dim, quarter), lambda i: (0, 1))}, near=False,
    )
    next_grad, back_normed_grad, partial = lax.optimization_barrier((next_grad, back_normed_grad, partial))
    table = pl.BlockSpec((chip_rows, HEAD_SIZE), lambda i: (0, 0))
    kv_partial, normed_grad, other_normed_grad = whole_call(
        keys_back_kernel, "keys_back", [jax.ShapeDtypeStruct((model_dim, 2 * HEAD_SIZE), bf16), wide, wide],
        place, later_grad, next_grad, cosine, sine, normed_one, weights, side_normed_grad, words=1,
        blocks={3: table, 4: table, 6: pl.BlockSpec((model_dim, 2 * HEAD_SIZE), lambda i: (0, 0))},
        scratch_shapes=[pltpu.VMEM((chip_rows, model_dim), f32)],
    )
    grad_acts, partial = whole_call(
        acts_back_kernel, "acts_back", [wide, jax.ShapeDtypeStruct(partial.shape, bf16)],
        normed_grad, core_swap(other_normed_grad), back_normed_grad, acts, gain_rows, grad_one, gain_two_grad,
        kv_partial, partial, near=False, blocks={8: pl.BlockSpec((16, HEAD_SIZE), lambda i: (0, 0))},
        out_blocks={1: pl.BlockSpec((model_dim, kv_width), lambda i: (0, 0))}, aliases={8: 1},
    )
    partial, expert_other, out_received = lax.optimization_barrier((partial, expert_other, out_received))
    received = send_to_chips(partial)
    expert_grad = expert_part.astype(f32) + expert_other.astype(f32)
    expert_grads = (
        expert_grad[:model_dim, :units],
        expert_grad[:model_dim, units:],
        jnp.concatenate([expert_grad[model_dim : model_dim + units], expert_grad[model_dim + units :]], axis=1),
    )
    plane_sums = jnp.sum(out_received.astype(f32), axis=0).astype(bf16)
    plane_sums = plane_sums.reshape(2, 2, 2, shard_rows, -1)
    grad_w_out = 0.0
    for k in range(4):
        piece = lax.dynamic_index_in_dim(plane_sums, (lax.axis_index("xl") + k) % 2, 1, False)
        piece = lax.dynamic_index_in_dim(piece, (half + k // 2) % 2, 1, False)
        piece = lax.ppermute(
            piece,
            ("xh", "xl", "c"),
            [
                (h * 4 + l * 2 + c, c * 4 + (l ^ k % 2) * 2 + (h ^ k // 2))
                for h in range(2)
                for l in range(2)
                for c in range(2)
            ],
        )
        grad_w_out = grad_w_out + piece.astype(f32)
    grad_w_out = jnp.concatenate([grad_w_out[0], grad_w_out[1]], axis=1)
    received = received.astype(f32).reshape(chips // 2, 2, 2 * shard_rows, -1)
    sums = jnp.sum(received, axis=0)
    sums = jnp.concatenate(
        [sums[0, :, :kv_width] + sums[1, :, :kv_width], sums[0, :, kv_width:], sums[1, :, kv_width:]], axis=1
    ).reshape(2, shard_rows, -1)
    given = core_swap(jnp.where(core == 0, sums[1], sums[0]))
    kept = jnp.where(core == 0, sums[0], sums[1])
    sums = (jnp.where(core == 0, kept, given), jnp.where(core == 0, given, kept))

    def columns(begin_at, width):
        return jnp.concatenate([part[:, begin_at : begin_at + width] for part in sums], axis=1)

    gain_sums = sums[0][:, 2 * HEAD_SIZE : 2 * HEAD_SIZE + 2] + sums[1][:, 2 * HEAD_SIZE : 2 * HEAD_SIZE + 2]
    return (
        activations,
        grad_acts,
        columns(kv_width, HALF_WIDTH),
        columns(0, HEAD_SIZE),
        columns(HEAD_SIZE, HEAD_SIZE),
        grad_w_out,
        gain_sums[:, 0],
        gain_sums[:, 1],
        *expert_grads,
    )


def solution(mesh):
    fine_mesh = jax.sharding.Mesh(mesh.devices.reshape(2, 2, 4, 4, 2), ALL)
    rows, vector = P(ALL, None), P(ALL)
    wide, tall = P(None, ("xl", "y", "z", "c")), P(("xl", "y", "z", "c"), None)
    return jax.shard_map(
        body,
        mesh=fine_mesh,
        in_specs=(
            rows, rows, P(), P(), rows, rows, rows, rows, rows, rows, vector, vector, wide, wide, tall,
        ),
        out_specs=(rows, rows, rows, rows, rows, rows, vector, vector, wide, wide, tall),
        check_vma=False,
    )
```

time: 517 us -> 495 us (0.957)
  Pallas kernels: 51.2 us -> 83.1 us
  matrix products: 45.2 us -> 27.2 us
  other arithmetic: 39.1 us -> 21.8 us
  blocking collectives: 86 us -> 75.4 us
  waiting for transfers between devices: 150 us -> 143 us
    pallas_call x2 -> x11, Pallas kernels: 2.5 us -> 32.9 us  [the longest x8 18 us: whole_call(): pl.pallas_call(kernel, grid=(1,), in_specs=specs, out_specs=[out_blocks.g...]
    dot_general x26 -> x14, matrix products: 45.2 us -> 27.2 us  [dot(): return lax.dot_general(a, b, (dims, ((), ())), preferred_element_type=f32)]
    ppermute x15 -> x8, waiting for transfers between devices: 64.4 us -> 49 us  [the longest x1 24 us: body(): lax.ppermute(own_acts, ('xh', 'xl'), [(p, p + 1) for p in range(planes -...]
    ppermute x15 -> x8, starting transfers between devices: 31.4 us -> 19 us  [the longest x4 9.75 us: body(): lax.ppermute(out_rows, ('xh', 'xl', 'c'), [(c * 4 + (l ^ k % 2) * 2 + (h...]
    unnamed x206 -> x161, local copies, waits for them, and re-layouts: 13.7 us -> 25.8 us
    all_to_all x4 -> x2, blocking collectives: 86 us -> 75.4 us  [exchange(): return lax.all_to_all(value, axes, 0, 0, tiled=True)]
    all_to_all x7 -> x8, waiting for transfers between devices: 47 us -> 56.5 us  [exchange(): return lax.all_to_all(value, axes, 0, 0, tiled=True)]
    ppermute x1, waiting for transfers between devices: 6.53 us -> 0.01 us  [body(): lax.ppermute(jnp.where(side == 0, query_right, query_left), 'z', PAIR)]
  transfers between devices with their start and end apart: 39 -> 36, of which waited for: 20 -> 20; matrix products, arithmetic and copies ran while one was open for 12% -> 8% of each run, Pallas kernels for 6% -> 10%
where the time goes in v3:
time: 495 us; the launch traced here: 486 us
  waiting for transfers between devices  143 us (29%)
  starting transfers between devices  102 us (21%)
  Pallas kernels  83.1 us (17%)
  blocking collectives  75.4 us (15%)
  local copies, waits for them, and re-layouts  32 us (6%)
  matrix products  27.2 us (5%)
  other arithmetic  21.8 us (4%)
    all_to_all x2, blocking collectives, exchange(): return lax.all_to_all(value, axes, 0, 0, tiled=True)  75.4 us
    all_to_all x8, waiting for transfers between devices, exchange(): return lax.all_to_all(value, axes, 0, 0, tiled=True)  56.5 us
    all_to_all x8, starting transfers between devices, exchange(): return lax.all_to_all(value, axes, 0, 0, tiled=True)  49.6 us
    dot_general x14, matrix products, dot(): return lax.dot_general(a, b, (dims, ((), ())), preferred_element_type=f32)  27.2 us
    unnamed x161, local copies, waits for them, and re-layouts  25.8 us
    pallas_call x1, Pallas kernels, attend_back(): pl.pallas_call(attend_back_kernel, grid_spec=pltpu.PrefetchScalarGridSpec...  24.9 us
    ppermute x1, waiting for transfers between devices, body(): lax.ppermute(own_acts, ('xh', 'xl'), [(p, p + 1) for p in range(planes -...  24 us
    ppermute x1, waiting for transfers between devices, body(): expert_other = lax.ppermute(expert_part, 'xh', SWAP)  21.5 us
  transfers between devices with their start and end apart: 36, of which 20 were waited for; matrix products, arithmetic and copies ran while one was open for 8% of the time, Pallas kernels for 10%

profile of v3, /device:TPU:1, one launch (start us, length us, event | category | flops | bytes accessed | tf_op | source)
XLA Modules:
  0.0 486.5 jit_solution(16777754690510206108)
XLA Ops:
  9.6 11.3 %all-to-all-start = ((bf16[64,24,768]{2,1,0:T(8,128)(2,1)}), bf16[64,24,768]{2,1,0:T(8,128)(2,1)S(1)}, u32[]{:S(2)}, u32[]{:S(2)}) async-start(bf16[64,24,768]{2,1,0:T(8,128)(2,1)} %copy-done.10), calls=%async_computation | async-start | bytes 4718592 | tf_op jit(solution)/shard_map/all_to_all | solution.py:50
  30.2 24.0 %collective-permute-done.4.before_own_ref = bf16[128,1536]{1,0:T(8,128)(2,1)S(1)} collective-permute-done((bf16[128,1536]{1,0:T(8,128)(2,1)}, bf16[128,1536]{1,0:T(8,128)(2,1)S(1)}, u32[]{:S(2)}, u32[]{:S(2)}) %collective-permute-start.4) | collective-permute-done | bytes 393248 | tf_op jit(solution)/shard_map/ppermute | solution.py:667
  59.1 6.0 %all-to-all-start.1 = ((bf16[16,24,768]{2,1,0:T(8,128)(2,1)}), bf16[16,24,768]{2,1,0:T(8,128)(2,1)}, u32[]{:S(2)}, u32[]{:S(2)}) async-start(bf16[16,24,768]{2,1,0:T(8,128)(2,1)} %copy-done.21), calls=%async_computation.1 | async-start | bytes 1179648 | tf_op jit(solution)/shard_map/all_to_all | solution.py:50
  65.7 5.2 %project_keys.1 = (bf16[256,1536]{1,0:T(8,128)(2,1)}, bf16[256,256]{1,0:T(8,128)(2,1)}, bf16[16,256,256]{2,1,0:T(8,128)(2,1)}, f32[8,1536]{1,0:T(8,128)}) custom-call(s32[5]{0:T(128)} %stack.40.place_ref, bf16[128,1536]{1,0:T(8,128)(2,1)} %acts_ref.3, bf16[128,1536]{1,0:T(8,128)(2,1)} %copy-done.62, bf16[128,1536]{1,0:T(8,128)(2,1)} %copy-done.61, ...), custom_call_target="tpu_custom_call" | custom-call | tf_op jit(solution)/shard_map/project_keys/pallas_call | solution.py:281
  70.9 5.2 %all-to-all-done.1 = bf16[16,24,768]{2,1,0:T(8,128)(2,1)} async-done(((bf16[16,24,768]{2,1,0:T(8,128)(2,1)}), bf16[16,24,768]{2,1,0:T(8,128)(2,1)}, u32[]{:S(2)}, u32[]{:S(2)}) %all-to-all-start.1) | async-done | bytes 589856 | tf_op jit(solution)/shard_map/all_to_all | solution.py:50
  76.0 4.4 all-to-all-start.2
  102.7 8.0 %collective-permute-done.6.theirs_ref = bf16[256,384]{1,0:T(8,128)(2,1)} collective-permute-done((bf16[256,384]{1,0:T(8,128)(2,1)}, bf16[256,384]{1,0:T(8,128)(2,1)}, u32[]{:S(2)}, u32[]{:S(2)}) %collective-permute-start.6) | collective-permute-done | bytes 196640 | tf_op jit(solution)/shard_map/ppermute | solution.py:703
  112.5 17.3 %attend.1 = (f32[256,768]{1,0:T(8,128)}, bf16[256,768]{1,0:T(8,128)(2,1)}, f32[6,8,256]{2,1,0:T(8,128)}) custom-call(s32[5]{0:T(128)} %stack.40.place_ref, s32[256,128]{1,0:T(8,128)} %broadcast_in_dim.36.low_ref, bf16[256,384]{1,0:T(8,128)(2,1)} %get-tuple-element.120.mine_ref, bf16[256,384]{1,0:T(8,128)(2,1)} %collective-permute-done.6.theirs_ref, ...), custom_call_target="tpu_custom_call" | custom-call | flops 20000000000 | bytes 4000000 | tf_op jit(solution)/shard_map/attend/pallas_call | solution.py:132
  136.4 38.2 %all_to_all.50 = bf16[32,24,1536]{2,1,0:T(8,128)(2,1)S(1)} all-to-all(bf16[32,24,1536]{2,1,0:T(8,128)(2,1)S(1)} %bitcast.81), channel_id=1, replica_groups=mesh['xh'=2,'xl'=2,'y'=4,'z'=4,'c'=2] {'xl','y','z'}, dimensions={0} | all-to-all | bytes 4718592 | tf_op jit(solution)/shard_map/all_to_all | solution.py:50
  186.5 4.2 collective-permute-done.13
  198.8 28.8 %all-to-all-done.4 = bf16[32,24,1536]{2,1,0:T(8,128)(2,1)S(1)} async-done(((bf16[32,24,1536]{2,1,0:T(8,128)(2,1)}), bf16[32,24,1536]{2,1,0:T(8,128)(2,1)S(1)}, u32[]{:S(2)}, u32[]{:S(2)}) %all-to-all-start.4) | async-done | bytes 2359328 | tf_op jit(solution)/shard_map/all_to_all | solution.py:50
  229.0 5.8 %combine.1 = (bf16[128,1536]{1,0:T(8,128)(2,1)}, f32[128,1536]{1,0:T(8,128)}, bf16[768,1536]{1,0:T(8,128)(2,1)}) custom-call(s32[2]{0:T(128)} %pad_add_fusion.1.valid_ref, f32[1]{0:T(128)S(6)} %div.14.scale_ref, bf16[768,1536]{1,0:T(8,128)(2,1)} %bitcast.83, bf16[256,768]{1,0:T(8,128)(2,1)} %copy-done.22, f32[128,1536]{1,0:T(8,128)} %copy-done.9, ...), custom_call_target="tpu_custom_call" | custom-call | tf_op jit(solution)/shard_map/combine/pallas_call | solution.py:369
  234.8 37.2 %all_to_all.51 = bf16[32,24,1536]{2,1,0:T(8,128)(2,1)S(1)} all-to-all(bf16[32,24,1536]{2,1,0:T(8,128)(2,1)} %bitcast.94), channel_id=1, replica_groups=mesh['xh'=2,'xl'=2,'y'=4,'z'=4,'c'=2] {'xl','y','z'}, dimensions={0} | all-to-all | bytes 4718592 | tf_op jit(solution)/shard_map/all_to_all | solution.py:50
  284.0 4.2 collective-permute-done.15
  291.6 4.6 all-to-all-start.6
  307.3 18.9 %all-to-all-done.6 = bf16[32,24,1536]{2,1,0:T(8,128)(2,1)S(1)} async-done(((bf16[32,24,1536]{2,1,0:T(8,128)(2,1)}), bf16[32,24,1536]{2,1,0:T(8,128)(2,1)S(1)}, u32[]{:S(2)}, u32[]{:S(2)}) %all-to-all-start.6) | async-done | bytes 2359328 | tf_op jit(solution)/shard_map/all_to_all | solution.py:50
  338.0 5.2 %out_project_back.1 = (bf16[256,768]{1,0:T(8,128)(2,1)}, bf16[16,4,24,768]{3,2,1,0:T(8,128)(2,1)}) custom-call(s32[5]{0:T(128)} %stack.40.place_ref, bf16[128,1536]{1,0:T(8,128)(2,1)} %get-tuple-element.157.own_ref, bf16[128,1536]{1,0:T(8,128)(2,1)} %copy-done.64, bf16[256,768]{1,0:T(8,128)(2,1)} %get-tuple-element.133.attn_ref, ...), custom_call_target="tpu_custom_call" | custom-call | tf_op jit(solution)/shard_map/out_project_back/pallas_call | solution.py:528
  343.1 4.9 %all-to-all-start.7 = ((bf16[16,4,24,768]{3,2,1,0:T(8,128)(2,1)}), bf16[16,4,24,768]{3,2,1,0:T(8,128)(2,1)}, u32[]{:S(2)}, u32[]{:S(2)}) async-start(bf16[16,4,24,768]{3,2,1,0:T(8,128)(2,1)} %get-tuple-element.161), calls=%async_computation.7 | async-start | bytes 4718592 | tf_op jit(solution)/shard_map/all_to_all | solution.py:50
  348.7 24.9 %attend_back.1 = (bf16[256,768]{1,0:T(8,128)(2,1)}, bf16[16,256,256]{2,1,0:T(8,128)(2,1)}, bf16[256,256]{1,0:T(8,128)(2,1)}) custom-call(s32[5]{0:T(128)} %stack.40.place_ref, s32[8,256]{1,0:T(8,128)} %broadcast_in_dim.54.low_ref, bf16[256,384]{1,0:T(8,128)(2,1)} %get-tuple-element.120.mine_ref, bf16[256,384]{1,0:T(8,128)(2,1)} %collective-permute-done.6.theirs_ref, ...), custom_call_target="tpu_custom_call" | custom-call | flops 28000000000 | bytes 8000000 | tf_op jit(solution)/shard_map/attend_back/pallas_call | solution.py:590
  380.0 5.9 %all-to-all-start.8 = ((bf16[16,256,256]{2,1,0:T(8,128)(2,1)}), bf16[16,256,256]{2,1,0:T(8,128)(2,1)}, u32[]{:S(2)}, u32[]{:S(2)}) async-start(bf16[16,256,256]{2,1,0:T(8,128)(2,1)} %get-tuple-element.162), calls=%async_computation.8 | async-start | bytes 4194304 | tf_op jit(solution)/shard_map/all_to_all | solution.py:50
  392.9 21.5 %collective-permute-done.17 = bf16[2304,768]{1,0:T(8,128)(2,1)} collective-permute-done((bf16[2304,768]{1,0:T(8,128)(2,1)}, bf16[2304,768]{1,0:T(8,128)(2,1)}, u32[]{:S(2)}, u32[]{:S(2)}) %collective-permute-start.17) | collective-permute-done | bytes 3538976 | tf_op jit(solution)/shard_map/ppermute | solution.py:779
  436.5 4.2 acts_back.1
  440.7 8.3 %all-to-all-start.9 = ((bf16[64,24,768]{2,1,0:T(8,128)(2,1)}), bf16[64,24,768]{2,1,0:T(8,128)(2,1)S(1)}, u32[]{:S(2)}, u32[]{:S(2)}) async-start(bf16[64,24,768]{2,1,0:T(8,128)(2,1)} %bitcast.82), calls=%async_computation.9 | async-start | bytes 4718592 | tf_op jit(solution)/shard_map/all_to_all | solution.py:50
  467.6 10.2 %collective-permute-done.25 = bf16[2,12,768]{2,0,1:T(2,128)(2,1)S(1)} collective-permute-done((bf16[2,12,768]{2,0,1:T(2,128)(2,1)S(1)}, bf16[2,12,768]{2,0,1:T(2,128)(2,1)S(1)}, u32[]{:S(2)}, u32[]{:S(2)}) %collective-permute-start.25) | collective-permute-done | bytes 36896 | tf_op jit(solution)/shard_map/ppermute | solution.py:836
  (292 shorter events, 175.7 us)
Async XLA Ops:
  9.6 49.5 %all-to-all-start = ((bf16[64,24,768]{2,1,0:T(8,128)(2,1)}), bf16[64,24,768]{2,1,0:T(8,128)(2,1)S(1)}, u32[]{:S(2)}, u32[]{:S(2)}) async-start(bf16[64,24,768]{2,1,0:T(8,128)(2,1)} %copy-done.10), calls=%async_computation | async-start | bytes 4718592 | tf_op jit(solution)/shard_map/all_to_all | solution.py:50
  24.5 29.7 %collective-permute-start.4 = (bf16[128,1536]{1,0:T(8,128)(2,1)}, bf16[128,1536]{1,0:T(8,128)(2,1)S(1)}, u32[]{:S(2)}, u32[]{:S(2)}) collective-permute-start(bf16[128,1536]{1,0:T(8,128)(2,1)} %acts_ref.3), channel_id=1, source_target_pairs={{0,32},{32,64},{64,96},{1,33},{33,65},{65,97},{2,34},{34,66},{66,9... | collective-permute-start | bytes 1179656 | tf_op jit(solution)/shard_map/ppermute | solution.py:667
  27.5 29.6 %collective-permute-start.2 = (bf16[128,1536]{1,0:T(8,128)(2,1)}, bf16[128,1536]{1,0:T(8,128)(2,1)S(1)}, u32[]{:S(2)}, u32[]{:S(2)}) collective-permute-start(bf16[128,1536]{1,0:T(8,128)(2,1)} %acts_ref.3), channel_id=1, source_target_pairs={{0,2},{2,0},{4,6},{6,4},{1,3},{3,1},{5,7},{7,5},{8,10},{10,8},{12,... | collective-permute-start | bytes 1179656 | tf_op jit(solution)/shard_map/ppermute | solution.py:665
  28.7 28.9 %collective-permute-start.1 = (bf16[128,1536]{1,0:T(8,128)(2,1)}, bf16[128,1536]{1,0:T(8,128)(2,1)S(1)}, u32[]{:S(2)}, u32[]{:S(2)}) collective-permute-start(bf16[128,1536]{1,0:T(8,128)(2,1)} %acts_ref.3), channel_id=1, source_target_pairs={{0,1},{1,0},{2,3},{3,2},{4,5},{5,4},{6,7},{7,6},{8,9},{9,8},{10,11... | collective-permute-start | bytes 1179656 | tf_op jit(solution)/shard_map/ppermute | solution.py:46
  59.1 16.9 %all-to-all-start.1 = ((bf16[16,24,768]{2,1,0:T(8,128)(2,1)}), bf16[16,24,768]{2,1,0:T(8,128)(2,1)}, u32[]{:S(2)}, u32[]{:S(2)}) async-start(bf16[16,24,768]{2,1,0:T(8,128)(2,1)} %copy-done.21), calls=%async_computation.1 | async-start | bytes 1179648 | tf_op jit(solution)/shard_map/all_to_all | solution.py:50
  76.0 36.5 %all-to-all-start.2 = ((bf16[16,256,256]{2,1,0:T(8,128)(2,1)}), bf16[16,256,256]{2,1,0:T(8,128)(2,1)}, u32[]{:S(2)}, u32[]{:S(2)}) async-start(bf16[16,256,256]{2,1,0:T(8,128)(2,1)} %get-tuple-element.129), calls=%async_computation.2 | async-start | bytes 4194304 | tf_op jit(solution)/shard_map/all_to_all | solution.py:50
  80.5 30.2 %collective-permute-start.10 = (bf16[384,768]{1,0:T(8,128)(2,1)}, bf16[384,768]{1,0:T(8,128)(2,1)S(1)}, u32[]{:S(2)}, u32[]{:S(2)}) collective-permute-start(bf16[384,768]{1,0:T(8,128)(2,1)} %bitcast.9), channel_id=1, source_target_pairs={{33,0},{97,1},{1,32},{65,33},{32,64},{96,65},{0,96},{64,97},{35,2}... | collective-permute-start | bytes 1769480 | tf_op jit(solution)/shard_map/ppermute | solution.py:686
  84.4 26.3 %collective-permute-start.9 = (bf16[384,768]{1,0:T(8,128)(2,1)}, bf16[384,768]{1,0:T(8,128)(2,1)S(1)}, u32[]{:S(2)}, u32[]{:S(2)}) collective-permute-start(bf16[384,768]{1,0:T(8,128)(2,1)} %bitcast.9), channel_id=1, source_target_pairs={{1,0},{65,1},{33,32},{97,33},{0,64},{64,65},{32,96},{96,97},{3,2},... | collective-permute-start | bytes 1769480 | tf_op jit(solution)/shard_map/ppermute | solution.py:686
  86.6 25.9 %collective-permute-start.8 = (bf16[384,768]{1,0:T(8,128)(2,1)}, bf16[384,768]{1,0:T(8,128)(2,1)S(1)}, u32[]{:S(2)}, u32[]{:S(2)}) collective-permute-start(bf16[384,768]{1,0:T(8,128)(2,1)} %bitcast.9), channel_id=1, source_target_pairs={{32,0},{96,1},{0,32},{64,33},{33,64},{97,65},{1,96},{65,97},{34,2}... | collective-permute-start | bytes 1769480 | tf_op jit(solution)/shard_map/ppermute | solution.py:686
  86.6 25.9 %collective-permute-start.7 = (bf16[384,768]{1,0:T(8,128)(2,1)}, bf16[384,768]{1,0:T(8,128)(2,1)S(1)}, u32[]{:S(2)}, u32[]{:S(2)}) collective-permute-start(bf16[384,768]{1,0:T(8,128)(2,1)} %bitcast.9), channel_id=1, source_target_pairs={{0,0},{64,1},{32,32},{96,33},{1,64},{65,65},{33,96},{97,97},{2,2},... | collective-permute-start | bytes 1769480 | tf_op jit(solution)/shard_map/ppermute | solution.py:686
  94.2 16.5 %collective-permute-start.6 = (bf16[256,384]{1,0:T(8,128)(2,1)}, bf16[256,384]{1,0:T(8,128)(2,1)}, u32[]{:S(2)}, u32[]{:S(2)}) collective-permute-start(bf16[256,384]{1,0:T(8,128)(2,1)} %get-tuple-element.121), channel_id=1, source_target_pairs={{0,2},{2,0},{4,6},{6,4},{1,3},{3,1},{5,7},{7,5},{8,10},{10,8},{12,... | collective-permute-start | bytes 589832 | tf_op jit(solution)/shard_map/ppermute | solution.py:703
  193.5 34.1 %all-to-all-start.4 = ((bf16[32,24,1536]{2,1,0:T(8,128)(2,1)}), bf16[32,24,1536]{2,1,0:T(8,128)(2,1)S(1)}, u32[]{:S(2)}, u32[]{:S(2)}) async-start(bf16[32,24,1536]{2,1,0:T(8,128)(2,1)} %bitcast.93), calls=%async_computation.4 | async-start | bytes 4718592 | tf_op jit(solution)/shard_map/all_to_all | solution.py:50
  272.0 7.0 %collective-permute-start.14 = (bf16[768,1536]{1,0:T(8,128)(2,1)S(1)}, bf16[768,1536]{1,0:T(8,128)(2,1)S(1)}, u32[]{:S(2)}, u32[]{:S(2)}) collective-permute-start(bf16[768,1536]{1,0:T(8,128)(2,1)S(1)} %bitcast.89), channel_id=1, source_target_pairs={{0,1},{1,0},{2,3},{3,2},{4,5},{5,4},{6,7},{7,6},{8,9},{9,8},{10,11... | collective-permute-start | bytes 7077896 | tf_op jit(solution)/shard_map/ppermute | solution.py:46
  291.6 34.6 %all-to-all-start.6 = ((bf16[32,24,1536]{2,1,0:T(8,128)(2,1)}), bf16[32,24,1536]{2,1,0:T(8,128)(2,1)S(1)}, u32[]{:S(2)}, u32[]{:S(2)}) async-start(bf16[32,24,1536]{2,1,0:T(8,128)(2,1)} %bitcast.92), calls=%async_computation.6 | async-start | bytes 4718592 | tf_op jit(solution)/shard_map/all_to_all | solution.py:50
  333.4 81.0 %collective-permute-start.17 = (bf16[2304,768]{1,0:T(8,128)(2,1)}, bf16[2304,768]{1,0:T(8,128)(2,1)}, u32[]{:S(2)}, u32[]{:S(2)}) collective-permute-start(bf16[2304,768]{1,0:T(8,128)(2,1)} %pad_maximum_fusion), channel_id=1, source_target_pairs={{0,64},{64,0},{1,65},{65,1},{2,66},{66,2},{3,67},{67,3},{4,68},{68... | collective-permute-start | bytes 10616840 | tf_op jit(solution)/shard_map/ppermute | solution.py:779
  343.1 36.9 %all-to-all-start.7 = ((bf16[16,4,24,768]{3,2,1,0:T(8,128)(2,1)}), bf16[16,4,24,768]{3,2,1,0:T(8,128)(2,1)}, u32[]{:S(2)}, u32[]{:S(2)}) async-start(bf16[16,4,24,768]{3,2,1,0:T(8,128)(2,1)} %get-tuple-element.161), calls=%async_computation.7 | async-start | bytes 4718592 | tf_op jit(solution)/shard_map/all_to_all | solution.py:50
  374.8 11.1 %collective-permute-start.18 = (bf16[256,384]{1,0:T(8,128)(2,1)S(1)}, bf16[256,384]{1,0:T(8,128)(2,1)S(1)}, u32[]{:S(2)}, u32[]{:S(2)}) collective-permute-start(bf16[256,384]{1,0:T(8,128)(2,1)S(1)} %get-tuple-element.202), channel_id=1, source_target_pairs={{0,2},{2,0},{4,6},{6,4},{1,3},{3,1},{5,7},{7,5},{8,10},{10,8},{12,... | collective-permute-start | bytes 589832 | tf_op jit(solution)/shard_map/ppermute | solution.py:786
  380.0 34.4 %all-to-all-start.8 = ((bf16[16,256,256]{2,1,0:T(8,128)(2,1)}), bf16[16,256,256]{2,1,0:T(8,128)(2,1)}, u32[]{:S(2)}, u32[]{:S(2)}) async-start(bf16[16,256,256]{2,1,0:T(8,128)(2,1)} %get-tuple-element.162), calls=%async_computation.8 | async-start | bytes 4194304 | tf_op jit(solution)/shard_map/all_to_all | solution.py:50
  391.3 33.2 %collective-permute-start.21 = (bf16[128,1536]{1,0:T(8,128)(2,1)}, bf16[128,1536]{1,0:T(8,128)(2,1)}, u32[]{:S(2)}, u32[]{:S(2)}) collective-permute-start(bf16[128,1536]{1,0:T(8,128)(2,1)} %add_convert_fusion.3), channel_id=1, source_target_pairs={{0,2},{2,0},{4,6},{6,4},{1,3},{3,1},{5,7},{7,5},{8,10},{10,8},{12,... | collective-permute-start | bytes 1179656 | tf_op jit(solution)/shard_map/ppermute | solution.py:792
  440.7 40.2 %all-to-all-start.9 = ((bf16[64,24,768]{2,1,0:T(8,128)(2,1)}), bf16[64,24,768]{2,1,0:T(8,128)(2,1)S(1)}, u32[]{:S(2)}, u32[]{:S(2)}) async-start(bf16[64,24,768]{2,1,0:T(8,128)(2,1)} %bitcast.82), calls=%async_computation.9 | async-start | bytes 4718592 | tf_op jit(solution)/shard_map/all_to_all | solution.py:50
  451.6 26.1 %collective-permute-start.25 = (bf16[2,12,768]{2,0,1:T(2,128)(2,1)S(1)}, bf16[2,12,768]{2,0,1:T(2,128)(2,1)S(1)}, u32[]{:S(2)}, u32[]{:S(2)}) collective-permute-start(bf16[2,12,768]{2,0,1:T(2,128)(2,1)S(1)} %bitcast.105), channel_id=1, source_target_pairs={{0,32},{1,96},{32,0},{33,64},{64,33},{65,97},{96,1},{97,65},{2,34}... | collective-permute-start | bytes 110600 | tf_op jit(solution)/shard_map/ppermute | solution.py:836
  455.1 22.7 %collective-permute-start.26 = (bf16[2,12,768]{2,0,1:T(2,128)(2,1)S(1)}, bf16[2,12,768]{2,0,1:T(2,128)(2,1)S(1)}, u32[]{:S(2)}, u32[]{:S(2)}) collective-permute-start(bf16[2,12,768]{2,0,1:T(2,128)(2,1)S(1)} %bitcast.102), channel_id=1, source_target_pairs={{0,1},{1,65},{32,33},{33,97},{64,0},{65,64},{96,32},{97,96},{2,3},... | collective-permute-start | bytes 110600 | tf_op jit(solution)/shard_map/ppermute | solution.py:836
  455.4 22.5 %collective-permute-start.27 = (bf16[2,12,768]{2,0,1:T(2,128)(2,1)S(1)}, bf16[2,12,768]{2,0,1:T(2,128)(2,1)S(1)}, u32[]{:S(2)}, u32[]{:S(2)}) collective-permute-start(bf16[2,12,768]{2,0,1:T(2,128)(2,1)S(1)} %bitcast.99), channel_id=1, source_target_pairs={{0,33},{1,97},{32,1},{33,65},{64,32},{65,96},{96,0},{97,64},{2,35}... | collective-permute-start | bytes 110600 | tf_op jit(solution)/shard_map/ppermute | solution.py:836
  455.4 24.1 %collective-permute-start.24 = (bf16[2,12,768]{2,0,1:T(2,128)(2,1)S(1)}, bf16[2,12,768]{2,0,1:T(2,128)(2,1)S(1)}, u32[]{:S(2)}, u32[]{:S(2)}) collective-permute-start(bf16[2,12,768]{2,0,1:T(2,128)(2,1)S(1)} %bitcast.98), channel_id=1, source_target_pairs={{0,0},{1,64},{32,32},{33,96},{64,1},{65,65},{96,33},{97,97},{2,2},... | collective-permute-start | bytes 110600 | tf_op jit(solution)/shard_map/ppermute | solution.py:836
  (88 other events, 686.6 us)

commit v4 on v3

--- a/solution.py
+++ b/solution.py
@@ -396,21 +396,21 @@
     gain_grad_ref[...] = jnp.broadcast_to(gain_grad, gain_grad_ref.shape)
 
 
-def query_columns_kernel(rows_ref, pair_rows_ref, grad_ref, pair_grad_ref, partial_ref):
+def query_columns_kernel(rows_ref, pair_rows_ref, grad_ref, pair_grad_ref, before_ref, partial_ref):
+    del before_ref
     queries = dot(rows_ref[...], grad_ref[...], TN) + dot(pair_rows_ref[...], pair_grad_ref[...], TN)
     partial_ref[...] = queries.astype(bf16)
 
 
 def split_grads_kernel(place_ref, came_ref, own_ref, later_ref, before_ref):
-    spot = place_ref[1]
-    later = own_ref[...].astype(f32)
-    before = jnp.zeros_like(later)
-    for j in range(came_ref.shape[0]):
-        grad = came_ref[j].astype(f32)
-        later = later + jnp.where(j > spot, grad, 0.0)
-        before = before + jnp.where(j > spot, 0.0, grad)
-    later_ref[...] = later
-    before_ref[...] = before.astype(bf16)
+    spot, (spots, rows, width) = place_ref[1], came_ref.shape
+    step = rows // 8
+    for first in range(0, rows, step):
+        at = slice(first, first + step)
+        add = lambda j, total, at=at: total + came_ref[j, at, :].astype(f32)
+        before = lax.fori_loop(0, spot + 1, add, jnp.zeros((step, width), f32))
+        before_ref[at, :] = before.astype(bf16)
+        later_ref[at, :] = lax.fori_loop(spot + 1, spots, add, own_ref[at, :].astype(f32))
 
 
 def keys_back_kernel(
@@ -428,22 +428,24 @@
     other_ref[...] = sum_ref[pl.ds(pl.multiple_of((1 - core) * rows, rows), rows), :]
 
 
-def acts_back_kernel(
-    own_ref, swapped_ref, pair_ref, acts_ref, gain_ref, grad_ref, gain_grad_ref, keys_ref, queries_ref,
-    out_ref, partial_ref,
-):
+def gain_columns_kernel(own_ref, swapped_ref, pair_ref, acts_ref, gain_grad_ref, before_ref, partial_ref):
+    del before_ref
     values = acts_ref[...].astype(f32)
     inverse = lax.rsqrt(jnp.mean(values * values, axis=-1, keepdims=True) + NORM_EPS)
     normed_grad = own_ref[...] + swapped_ref[...] + pair_ref[...].astype(f32)
-    input_grad, gain_grad = norm_backward(values, inverse, gain_ref[0:1, :], normed_grad)
-    out_ref[...] = grad_ref[...] + input_grad
+    gain_grad = jnp.sum(normed_grad * values * inverse, axis=0, keepdims=True)
     row = lax.broadcasted_iota(jnp.int32, (16, values.shape[1]), 0)
     gain_rows = jnp.where(row == 0, gain_grad, jnp.where(row == 1, gain_grad_ref[0:1, :], 0.0))
     square = (16, HEAD_SIZE)
     unit = lax.broadcasted_iota(jnp.int32, square, 0) == lax.broadcasted_iota(jnp.int32, square, 1)
-    width = keys_ref.shape[1]
-    partial_ref[:, :width] = keys_ref[...]
-    partial_ref[:, width : width + HEAD_SIZE] = dot(gain_rows.astype(bf16), unit.astype(bf16), TN).astype(bf16)
+    partial_ref[...] = dot(gain_rows.astype(bf16), unit.astype(bf16), TN).astype(bf16)
+
+
+def acts_back_kernel(own_ref, swapped_ref, pair_ref, acts_ref, gain_ref, grad_ref, out_ref):
+    values = acts_ref[...].astype(f32)
+    inverse = lax.rsqrt(jnp.mean(values * values, axis=-1, keepdims=True) + NORM_EPS)
+    normed_grad = own_ref[...] + swapped_ref[...] + pair_ref[...].astype(f32)
+    out_ref[...] = grad_ref[...] + norm_backward(values, inverse, gain_ref[0:1, :], normed_grad)[0]
 
 
 def whole_call(
@@ -638,7 +640,8 @@
     core_word = core.astype(jnp.int32).reshape(1)
     packed = jax.ShapeDtypeStruct((shard_rows, kv_width + 2 * HALF_WIDTH), bf16)
     own_part, other_part = whole_call(
-        pack_kernel, "pack", [packed, packed], core_word, key_weight, value_weight, gain_pair, w_query, w_out, words=1
+        pack_kernel, "pack", [packed, packed], core_word, key_weight, value_weight, gain_pair, w_query, w_out, words=1,
+        near=False,
     )
     weights_sent, out_sent = whole_call(
         unpack_kernel, "unpack",
@@ -646,9 +649,15 @@
             jax.ShapeDtypeStruct((chips, 2 * shard_rows, kv_width + quarter), bf16),
             jax.ShapeDtypeStruct((spots, 2 * shard_rows, HALF_WIDTH), bf16),
         ],
-        core_word, own_part, core_swap(other_part), words=1,
-    )
+        core_word, own_part, core_swap(other_part), words=1, near=False,
+    )
+    pair_acts = lax.ppermute(acts, "z", PAIR)
+    before_acts = lax.ppermute(acts, ("xh", "xl"), [(p, p + 1) for p in range(planes - 1)])
+    weights_sent, pair_acts, before_acts = lax.optimization_barrier((weights_sent, pair_acts, before_acts))
     weights = exchange(weights_sent, CHIPS)
+    chip_acts = (acts, core_swap(acts))
+    pair_acts = (pair_acts, core_swap(pair_acts))
+    before_acts = (before_acts, core_swap(before_acts))
 
     first_token = chip * chip_rows
     chip_pos = first_token + jnp.arange(chip_rows, dtype=jnp.int32)
@@ -659,13 +668,6 @@
     low_rows = jnp.broadcast_to(low[None, :], (8, chip_rows))
     low_columns = jnp.broadcast_to(low[:, None], (chip_rows, HEAD_SIZE))
     block_at = jnp.arange(spots, dtype=jnp.int32)
-
-    own_acts, cosine, sine, low_columns, out_sent = lax.optimization_barrier((acts, cosine, sine, low_columns, out_sent))
-    chip_acts = (own_acts, core_swap(acts))
-    pair_acts = lax.ppermute(own_acts, "z", PAIR)
-    pair_acts = (pair_acts, core_swap(pair_acts))
-    before_acts = lax.ppermute(own_acts, ("xh", "xl"), [(p, p + 1) for p in range(planes - 1)])
-    before_acts = (before_acts, core_swap(before_acts))
 
     weights, out_sent, chip_acts, pair_acts, before_acts, low_columns, cosine, sine = lax.optimization_barrier(
         (weights, out_sent, chip_acts, pair_acts, before_acts, low_columns, cosine, sine)
@@ -719,7 +721,8 @@
         return mine, core_swap(mine)
 
     def from_experts(mine, theirs):
-        both = mine + core_swap(theirs.astype(bf16)).astype(f32)
+        mine, came = lax.optimization_barrier((mine.astype(bf16), core_swap(theirs.astype(bf16))))
+        both = mine.astype(f32) + came.astype(f32)
         both = both.astype(bf16).reshape(EXPERTS, CAP, model_dim)
         return exchange(both, HALF_CHIPS).reshape(all_slots, model_dim)
 
@@ -800,26 +803,35 @@
         place, came, own_kv_grad, words=1,
     )
     next_grad = lax.ppermute(before_grad, ("xh", "xl"), [(p + 1, p) for p in range(planes - 1)])
-    (partial,) = whole_call(
-        query_columns_kernel, "query_columns", [jax.ShapeDtypeStruct((model_dim, 2 * quarter), bf16)],
-        normed_one, pair_normed, side_query_grad, pair_query_grad,
-        out_blocks={0: pl.BlockSpec((model_dim, quarter), lambda i: (0, 1))}, near=False,
-    )
-    next_grad, back_normed_grad, partial = lax.optimization_barrier((next_grad, back_normed_grad, partial))
+    next_grad, back_normed_grad = lax.optimization_barrier((next_grad, back_normed_grad))
     table = pl.BlockSpec((chip_rows, HEAD_SIZE), lambda i: (0, 0))
-    kv_partial, normed_grad, other_normed_grad = whole_call(
-        keys_back_kernel, "keys_back", [jax.ShapeDtypeStruct((model_dim, 2 * HEAD_SIZE), bf16), wide, wide],
+    partial_shape = jax.ShapeDtypeStruct((model_dim, kv_width + quarter), bf16)
+    unread = pl.BlockSpec((16, HEAD_SIZE), lambda i: (0, 0))
+    partial, normed_grad, other_normed_grad = whole_call(
+        keys_back_kernel, "keys_back", [partial_shape, wide, wide],
         place, later_grad, next_grad, cosine, sine, normed_one, weights, side_normed_grad, words=1,
         blocks={3: table, 4: table, 6: pl.BlockSpec((model_dim, 2 * HEAD_SIZE), lambda i: (0, 0))},
+        out_blocks={0: pl.BlockSpec((model_dim, 2 * HEAD_SIZE), lambda i: (0, 0))},
         scratch_shapes=[pltpu.VMEM((chip_rows, model_dim), f32)],
     )
-    grad_acts, partial = whole_call(
-        acts_back_kernel, "acts_back", [wide, jax.ShapeDtypeStruct(partial.shape, bf16)],
-        normed_grad, core_swap(other_normed_grad), back_normed_grad, acts, gain_rows, grad_one, gain_two_grad,
-        kv_partial, partial, near=False, blocks={8: pl.BlockSpec((16, HEAD_SIZE), lambda i: (0, 0))},
-        out_blocks={1: pl.BlockSpec((model_dim, kv_width), lambda i: (0, 0))}, aliases={8: 1},
-    )
-    partial, expert_other, out_received = lax.optimization_barrier((partial, expert_other, out_received))
+    swapped_grad = core_swap(other_normed_grad)
+    (partial,) = whole_call(
+        query_columns_kernel, "query_columns", [partial_shape],
+        normed_one, pair_normed, side_query_grad, pair_query_grad, partial, blocks={4: unread},
+        out_blocks={0: pl.BlockSpec((model_dim, quarter), lambda i: (0, 1))}, aliases={4: 0}, near=False,
+    )
+    (partial,) = whole_call(
+        gain_columns_kernel, "gain_columns", [partial_shape],
+        normed_grad, swapped_grad, back_normed_grad, acts, gain_two_grad, partial, blocks={5: unread},
+        out_blocks={0: pl.BlockSpec((model_dim, HEAD_SIZE), lambda i: (0, 2))}, aliases={5: 0}, near=False,
+    )
+    partial, expert_other, out_received, grad_one = lax.optimization_barrier(
+        (partial, expert_other, out_received, grad_one)
+    )
+    (grad_acts,) = whole_call(
+        acts_back_kernel, "acts_back", [wide],
+        normed_grad, swapped_grad, back_normed_grad, acts, gain_rows, grad_one, near=False,
+    )
     received = send_to_chips(partial)
     expert_grad = expert_part.astype(f32) + expert_other.astype(f32)
     expert_grads = (

time: 495 us -> 484 us (0.978)
  waiting for transfers between devices: 143 us -> 124 us
  other arithmetic: 21.8 us -> 29.3 us
  Pallas kernels: 83.1 us -> 88.7 us
    ppermute x2, waiting for transfers between devices: 25.7 us -> 0.01 us  [the longest x1 0.01 us: body(): pair_acts = lax.ppermute(acts, 'z', PAIR)]
    all_to_all x8, waiting for transfers between devices: 56.5 us -> 76.6 us  [exchange(): return lax.all_to_all(value, axes, 0, 0, tiled=True)]
    ppermute x4, waiting for transfers between devices: 12 us -> 1.11 us  [body(): lax.ppermute(piece, ('xh', 'xl', 'c'), [(h * 4 + l * 2 + c, c * 4 + (l ^...]
    pallas_call x8 -> x9, Pallas kernels: 18 us -> 23.6 us  [whole_call(): pl.pallas_call(kernel, grid=(1,), in_specs=specs, out_specs=[out_blocks.g...]
    unnamed x161 -> x141, local copies, waits for them, and re-layouts: 25.8 us -> 20.4 us
    ppermute x13, waiting for transfers between devices: 17.3 us -> 12.4 us  [core_swap(): return lax.ppermute(value, 'c', SWAP)]
  transfers between devices with their start and end apart: 36 -> 36, of which waited for: 20 -> 18; matrix products, arithmetic and copies ran while one was open for 8% -> 11% of each run, Pallas kernels for 10% -> 11%
where the time goes in v4:
time: 484 us; the launch traced here: 476 us
  waiting for transfers between devices  124 us (26%)
  starting transfers between devices  101 us (21%)
  Pallas kernels  88.7 us (18%)
  blocking collectives  75 us (15%)
  local copies, waits for them, and re-layouts  31.4 us (6%)
  other arithmetic  29.3 us (6%)
  matrix products  24.1 us (5%)
    all_to_all x8, waiting for transfers between devices, exchange(): return lax.all_to_all(value, axes, 0, 0, tiled=True)  76.6 us
    all_to_all x2, blocking collectives, exchange(): return lax.all_to_all(value, axes, 0, 0, tiled=True)  75 us
    all_to_all x8, starting transfers between devices, exchange(): return lax.all_to_all(value, axes, 0, 0, tiled=True)  45.4 us
    pallas_call x1, Pallas kernels, attend_back(): pl.pallas_call(attend_back_kernel, grid_spec=pltpu.PrefetchScalarGridSpec...  24.9 us
    dot_general x14, matrix products, dot(): return lax.dot_general(a, b, (dims, ((), ())), preferred_element_type=f32)  24.1 us
    pallas_call x9, Pallas kernels, whole_call(): pl.pallas_call(kernel, grid=(1,), in_specs=specs, out_specs=[out_blocks.g...  23.6 us
    ppermute x1, waiting for transfers between devices, body(): expert_other = lax.ppermute(expert_part, 'xh', SWAP)  20.8 us
    unnamed x141, local copies, waits for them, and re-layouts  20.4 us
  transfers between devices with their start and end apart: 36, of which 18 were waited for; matrix products, arithmetic and copies ran while one was open for 11% of the time, Pallas kernels for 11%

profile of v4, /device:TPU:1, one launch (start us, length us, event | category | flops | bytes accessed | tf_op | source)
XLA Modules:
  0.0 476.3 jit_solution(6913517510275268915)
XLA Ops:
  15.9 10.5 %all-to-all-start = ((bf16[64,24,768]{2,1,0:T(8,128)(2,1)}), bf16[64,24,768]{2,1,0:T(8,128)(2,1)S(1)}, u32[]{:S(2)}, u32[]{:S(2)}) async-start(bf16[64,24,768]{2,1,0:T(8,128)(2,1)} %get-tuple-element.102), calls=%async_computation | async-start | bytes 4718592 | tf_op jit(solution)/shard_map/all_to_all | solution.py:50
  32.8 22.4 %all-to-all-done = bf16[64,24,768]{2,1,0:T(8,128)(2,1)S(1)} async-done(((bf16[64,24,768]{2,1,0:T(8,128)(2,1)}), bf16[64,24,768]{2,1,0:T(8,128)(2,1)S(1)}, u32[]{:S(2)}, u32[]{:S(2)}) %all-to-all-start) | async-done | bytes 2359328 | tf_op jit(solution)/shard_map/all_to_all | solution.py:50
  56.0 4.4 all-to-all-start.1
  61.1 5.2 %project_keys.1 = (bf16[256,1536]{1,0:T(8,128)(2,1)}, bf16[256,256]{1,0:T(8,128)(2,1)}, bf16[16,256,256]{2,1,0:T(8,128)(2,1)}, f32[8,1536]{1,0:T(8,128)}) custom-call(s32[5]{0:T(128)} %stack.40.place_ref, bf16[128,1536]{1,0:T(8,128)(2,1)} %acts_ref.5, bf16[128,1536]{1,0:T(8,128)(2,1)} %collective-permute-done.3.other_ref, bf16[128,1536]{1,0:T(8,128)(2,1)} %copy-done.51, ...), custom_call_target="tpu_custom_call" | custom-call | tf_op jit(solution)/shard_map/project_keys/pallas_call | solution.py:281
  69.8 4.4 all-to-all-start.2
  74.3 6.3 %collective-permute-start.10 = (bf16[384,768]{1,0:T(8,128)(2,1)}, bf16[384,768]{1,0:T(8,128)(2,1)S(1)}, u32[]{:S(2)}, u32[]{:S(2)}) collective-permute-start(bf16[384,768]{1,0:T(8,128)(2,1)} %bitcast.9), channel_id=1, source_target_pairs={{33,0},{97,1},{1,32},{65,33},{32,64},{96,65},{0,96},{64,97},{35,2}... | collective-permute-start | bytes 1769480 | tf_op jit(solution)/shard_map/ppermute | solution.py:688
  98.8 6.6 %collective-permute-done.6.theirs_ref = bf16[256,384]{1,0:T(8,128)(2,1)} collective-permute-done((bf16[256,384]{1,0:T(8,128)(2,1)}, bf16[256,384]{1,0:T(8,128)(2,1)}, u32[]{:S(2)}, u32[]{:S(2)}) %collective-permute-start.6) | collective-permute-done | bytes 196640 | tf_op jit(solution)/shard_map/ppermute | solution.py:705
  108.6 17.3 %attend.1 = (f32[256,768]{1,0:T(8,128)}, bf16[256,768]{1,0:T(8,128)(2,1)}, f32[6,8,256]{2,1,0:T(8,128)}) custom-call(s32[5]{0:T(128)} %stack.40.place_ref, s32[256,128]{1,0:T(8,128)} %broadcast_in_dim.33.low_ref, bf16[256,384]{1,0:T(8,128)(2,1)} %get-tuple-element.118.mine_ref, bf16[256,384]{1,0:T(8,128)(2,1)} %collective-permute-done.6.theirs_ref, ...), custom_call_target="tpu_custom_call" | custom-call | flops 20000000000 | bytes 4000000 | tf_op jit(solution)/shard_map/attend/pallas_call | solution.py:132
  132.3 37.8 %all_to_all.50 = bf16[32,24,1536]{2,1,0:T(8,128)(2,1)S(1)} all-to-all(bf16[32,24,1536]{2,1,0:T(8,128)(2,1)S(1)} %bitcast.82), channel_id=1, replica_groups=mesh['xh'=2,'xl'=2,'y'=4,'z'=4,'c'=2] {'xl','y','z'}, dimensions={0} | all-to-all | bytes 4718592 | tf_op jit(solution)/shard_map/all_to_all | solution.py:50
  188.1 4.1 all-to-all-start.4
  193.5 28.8 %all-to-all-done.4 = bf16[32,24,1536]{2,1,0:T(8,128)(2,1)S(1)} async-done(((bf16[32,24,1536]{2,1,0:T(8,128)(2,1)}), bf16[32,24,1536]{2,1,0:T(8,128)(2,1)S(1)}, u32[]{:S(2)}, u32[]{:S(2)}) %all-to-all-start.4) | async-done | bytes 2359328 | tf_op jit(solution)/shard_map/all_to_all | solution.py:50
  223.6 5.8 %combine.1 = (bf16[128,1536]{1,0:T(8,128)(2,1)}, f32[128,1536]{1,0:T(8,128)}, bf16[768,1536]{1,0:T(8,128)(2,1)}) custom-call(s32[2]{0:T(128)} %pad_add_fusion.1.valid_ref, f32[1]{0:T(128)S(6)} %div.14.scale_ref, bf16[768,1536]{1,0:T(8,128)(2,1)} %bitcast.83, bf16[256,768]{1,0:T(8,128)(2,1)} %copy-done.19, f32[128,1536]{1,0:T(8,128)} %copy-done.10, ...), custom_call_target="tpu_custom_call" | custom-call | tf_op jit(solution)/shard_map/combine/pallas_call | solution.py:369
  229.4 37.2 %all_to_all.51 = bf16[32,24,1536]{2,1,0:T(8,128)(2,1)S(1)} all-to-all(bf16[32,24,1536]{2,1,0:T(8,128)(2,1)} %bitcast.92), channel_id=1, replica_groups=mesh['xh'=2,'xl'=2,'y'=4,'z'=4,'c'=2] {'xl','y','z'}, dimensions={0} | all-to-all | bytes 4718592 | tf_op jit(solution)/shard_map/all_to_all | solution.py:50
  284.7 4.4 all-to-all-start.6
  300.3 18.9 %all-to-all-done.6 = bf16[32,24,1536]{2,1,0:T(8,128)(2,1)S(1)} async-done(((bf16[32,24,1536]{2,1,0:T(8,128)(2,1)}), bf16[32,24,1536]{2,1,0:T(8,128)(2,1)S(1)}, u32[]{:S(2)}, u32[]{:S(2)}) %all-to-all-start.6) | async-done | bytes 2359328 | tf_op jit(solution)/shard_map/all_to_all | solution.py:50
  326.3 4.2 collective-permute-start.17
  331.3 5.2 %out_project_back.1 = (bf16[256,768]{1,0:T(8,128)(2,1)}, bf16[16,4,24,768]{3,2,1,0:T(8,128)(2,1)}) custom-call(s32[5]{0:T(128)} %stack.40.place_ref, bf16[128,1536]{1,0:T(8,128)(2,1)} %get-tuple-element.159.own_ref, bf16[128,1536]{1,0:T(8,128)(2,1)} %copy-done.53, bf16[256,768]{1,0:T(8,128)(2,1)} %get-tuple-element.131.attn_ref, ...), custom_call_target="tpu_custom_call" | custom-call | tf_op jit(solution)/shard_map/out_project_back/pallas_call | solution.py:530
  336.5 5.0 %all-to-all-start.7 = ((bf16[16,4,24,768]{3,2,1,0:T(8,128)(2,1)}), bf16[16,4,24,768]{3,2,1,0:T(8,128)(2,1)}, u32[]{:S(2)}, u32[]{:S(2)}) async-start(bf16[16,4,24,768]{3,2,1,0:T(8,128)(2,1)} %get-tuple-element.163), calls=%async_computation.7 | async-start | bytes 4718592 | tf_op jit(solution)/shard_map/all_to_all | solution.py:50
  342.1 24.9 %attend_back.1 = (bf16[256,768]{1,0:T(8,128)(2,1)}, bf16[16,256,256]{2,1,0:T(8,128)(2,1)}, bf16[256,256]{1,0:T(8,128)(2,1)}) custom-call(s32[5]{0:T(128)} %stack.40.place_ref, s32[8,256]{1,0:T(8,128)} %broadcast_in_dim.54.low_ref, bf16[256,384]{1,0:T(8,128)(2,1)} %get-tuple-element.118.mine_ref, bf16[256,384]{1,0:T(8,128)(2,1)} %collective-permute-done.6.theirs_ref, ...), custom_call_target="tpu_custom_call" | custom-call | flops 28000000000 | bytes 8000000 | tf_op jit(solution)/shard_map/attend_back/pallas_call | solution.py:592
  373.5 6.0 %all-to-all-start.8 = ((bf16[16,256,256]{2,1,0:T(8,128)(2,1)}), bf16[16,256,256]{2,1,0:T(8,128)(2,1)}, u32[]{:S(2)}, u32[]{:S(2)}) async-start(bf16[16,256,256]{2,1,0:T(8,128)(2,1)} %get-tuple-element.164), calls=%async_computation.8 | async-start | bytes 4194304 | tf_op jit(solution)/shard_map/all_to_all | solution.py:50
  387.0 20.8 %collective-permute-done.17 = bf16[2304,768]{1,0:T(8,128)(2,1)} collective-permute-done((bf16[2304,768]{1,0:T(8,128)(2,1)}, bf16[2304,768]{1,0:T(8,128)(2,1)}, u32[]{:S(2)}, u32[]{:S(2)}) %collective-permute-start.17) | collective-permute-done | bytes 3538976 | tf_op jit(solution)/shard_map/ppermute | solution.py:782
  432.4 6.6 %all-to-all-start.9 = ((bf16[64,24,768]{2,1,0:T(8,128)(2,1)}), bf16[64,24,768]{2,1,0:T(8,128)(2,1)S(1)}, u32[]{:S(2)}, u32[]{:S(2)}) async-start(bf16[64,24,768]{2,1,0:T(8,128)(2,1)} %bitcast.81), calls=%async_computation.9 | async-start | bytes 4718592 | tf_op jit(solution)/shard_map/all_to_all | solution.py:50
  439.0 6.8 %convert_add_fusion = f32[2304,768]{1,0:T(8,128)} fusion(bf16[2304,768]{1,0:T(8,128)(2,1)} %collective-permute-done.17, bf16[2304,768]{1,0:T(8,128)(2,1)} %pad_maximum_fusion), kind=kLoop, calls=%fused_computation | loop fusion | flops 5308416 | bytes 14155776 | tf_op jit(solution)/shard_map/add | solution.py:836
  458.6 4.9 %fusion.16 = (f32[1536,384]{1,0:T(8,128)}, f32[1536,384]{1,0:T(8,128)}) fusion(f32[2304,768]{1,0:T(8,128)} %convert_add_fusion), kind=kLoop, calls=%fused_computation.82 | loop fusion | bytes 9437184 | tf_op jit(solution)/shard_map/slice | solution.py:839
  (275 shorter events, 175.3 us)
Async XLA Ops:
  0.7 14.4 %collective-permute-start.1 = (bf16[128,1536]{1,0:T(8,128)(2,1)}, bf16[128,1536]{1,0:T(8,128)(2,1)S(1)}, u32[]{:S(2)}, u32[]{:S(2)}) collective-permute-start(bf16[128,1536]{1,0:T(8,128)(2,1)} %acts_ref.5), channel_id=1, source_target_pairs={{0,2},{2,0},{4,6},{6,4},{1,3},{3,1},{5,7},{7,5},{8,10},{10,8},{12,... | collective-permute-start | bytes 1179656 | tf_op jit(solution)/shard_map/ppermute | solution.py:654
  3.2 11.8 %collective-permute-start.2 = (bf16[128,1536]{1,0:T(8,128)(2,1)}, bf16[128,1536]{1,0:T(8,128)(2,1)S(1)}, u32[]{:S(2)}, u32[]{:S(2)}) collective-permute-start(bf16[128,1536]{1,0:T(8,128)(2,1)} %acts_ref.5), channel_id=1, source_target_pairs={{0,32},{32,64},{64,96},{1,33},{33,65},{65,97},{2,34},{34,66},{66,9... | collective-permute-start | bytes 1179656 | tf_op jit(solution)/shard_map/ppermute | solution.py:655
  15.9 39.2 %all-to-all-start = ((bf16[64,24,768]{2,1,0:T(8,128)(2,1)}), bf16[64,24,768]{2,1,0:T(8,128)(2,1)S(1)}, u32[]{:S(2)}, u32[]{:S(2)}) async-start(bf16[64,24,768]{2,1,0:T(8,128)(2,1)} %get-tuple-element.102), calls=%async_computation | async-start | bytes 4718592 | tf_op jit(solution)/shard_map/all_to_all | solution.py:50
  56.0 13.8 %all-to-all-start.1 = ((bf16[16,24,768]{2,1,0:T(8,128)(2,1)}), bf16[16,24,768]{2,1,0:T(8,128)(2,1)}, u32[]{:S(2)}, u32[]{:S(2)}) async-start(bf16[16,24,768]{2,1,0:T(8,128)(2,1)} %get-tuple-element.126), calls=%async_computation.1 | async-start | bytes 1179648 | tf_op jit(solution)/shard_map/all_to_all | solution.py:50
  69.8 38.8 %all-to-all-start.2 = ((bf16[16,256,256]{2,1,0:T(8,128)(2,1)}), bf16[16,256,256]{2,1,0:T(8,128)(2,1)}, u32[]{:S(2)}, u32[]{:S(2)}) async-start(bf16[16,256,256]{2,1,0:T(8,128)(2,1)} %get-tuple-element.127), calls=%async_computation.2 | async-start | bytes 4194304 | tf_op jit(solution)/shard_map/all_to_all | solution.py:50
  74.3 31.1 %collective-permute-start.10 = (bf16[384,768]{1,0:T(8,128)(2,1)}, bf16[384,768]{1,0:T(8,128)(2,1)S(1)}, u32[]{:S(2)}, u32[]{:S(2)}) collective-permute-start(bf16[384,768]{1,0:T(8,128)(2,1)} %bitcast.9), channel_id=1, source_target_pairs={{33,0},{97,1},{1,32},{65,33},{32,64},{96,65},{0,96},{64,97},{35,2}... | collective-permute-start | bytes 1769480 | tf_op jit(solution)/shard_map/ppermute | solution.py:688
  80.5 27.5 %collective-permute-start.7 = (bf16[384,768]{1,0:T(8,128)(2,1)}, bf16[384,768]{1,0:T(8,128)(2,1)S(1)}, u32[]{:S(2)}, u32[]{:S(2)}) collective-permute-start(bf16[384,768]{1,0:T(8,128)(2,1)} %bitcast.9), channel_id=1, source_target_pairs={{0,0},{64,1},{32,32},{96,33},{1,64},{65,65},{33,96},{97,97},{2,2},... | collective-permute-start | bytes 1769480 | tf_op jit(solution)/shard_map/ppermute | solution.py:688
  83.7 24.9 %collective-permute-start.8 = (bf16[384,768]{1,0:T(8,128)(2,1)}, bf16[384,768]{1,0:T(8,128)(2,1)S(1)}, u32[]{:S(2)}, u32[]{:S(2)}) collective-permute-start(bf16[384,768]{1,0:T(8,128)(2,1)} %bitcast.9), channel_id=1, source_target_pairs={{32,0},{96,1},{0,32},{64,33},{33,64},{97,65},{1,96},{65,97},{34,2}... | collective-permute-start | bytes 1769480 | tf_op jit(solution)/shard_map/ppermute | solution.py:688
  85.9 22.7 %collective-permute-start.9 = (bf16[384,768]{1,0:T(8,128)(2,1)}, bf16[384,768]{1,0:T(8,128)(2,1)S(1)}, u32[]{:S(2)}, u32[]{:S(2)}) collective-permute-start(bf16[384,768]{1,0:T(8,128)(2,1)} %bitcast.9), channel_id=1, source_target_pairs={{1,0},{65,1},{33,32},{97,33},{0,64},{64,65},{32,96},{96,97},{3,2},... | collective-permute-start | bytes 1769480 | tf_op jit(solution)/shard_map/ppermute | solution.py:688
  89.8 15.6 %collective-permute-start.6 = (bf16[256,384]{1,0:T(8,128)(2,1)}, bf16[256,384]{1,0:T(8,128)(2,1)}, u32[]{:S(2)}, u32[]{:S(2)}) collective-permute-start(bf16[256,384]{1,0:T(8,128)(2,1)} %get-tuple-element.119), channel_id=1, source_target_pairs={{0,2},{2,0},{4,6},{6,4},{1,3},{3,1},{5,7},{7,5},{8,10},{10,8},{12,... | collective-permute-start | bytes 589832 | tf_op jit(solution)/shard_map/ppermute | solution.py:705
  188.1 34.1 %all-to-all-start.4 = ((bf16[32,24,1536]{2,1,0:T(8,128)(2,1)}), bf16[32,24,1536]{2,1,0:T(8,128)(2,1)S(1)}, u32[]{:S(2)}, u32[]{:S(2)}) async-start(bf16[32,24,1536]{2,1,0:T(8,128)(2,1)} %bitcast.12), calls=%async_computation.4 | async-start | bytes 4718592 | tf_op jit(solution)/shard_map/all_to_all | solution.py:50
  266.6 7.0 %collective-permute-start.14 = (bf16[768,1536]{1,0:T(8,128)(2,1)S(1)}, bf16[768,1536]{1,0:T(8,128)(2,1)S(1)}, u32[]{:S(2)}, u32[]{:S(2)}) collective-permute-start(bf16[768,1536]{1,0:T(8,128)(2,1)S(1)} %bitcast.89), channel_id=1, source_target_pairs={{0,1},{1,0},{2,3},{3,2},{4,5},{5,4},{6,7},{7,6},{8,9},{9,8},{10,11... | collective-permute-start | bytes 7077896 | tf_op jit(solution)/shard_map/ppermute | solution.py:46
  284.7 34.4 %all-to-all-start.6 = ((bf16[32,24,1536]{2,1,0:T(8,128)(2,1)}), bf16[32,24,1536]{2,1,0:T(8,128)(2,1)S(1)}, u32[]{:S(2)}, u32[]{:S(2)}) async-start(bf16[32,24,1536]{2,1,0:T(8,128)(2,1)} %bitcast.16), calls=%async_computation.6 | async-start | bytes 4718592 | tf_op jit(solution)/shard_map/all_to_all | solution.py:50
  326.3 81.5 %collective-permute-start.17 = (bf16[2304,768]{1,0:T(8,128)(2,1)}, bf16[2304,768]{1,0:T(8,128)(2,1)}, u32[]{:S(2)}, u32[]{:S(2)}) collective-permute-start(bf16[2304,768]{1,0:T(8,128)(2,1)} %pad_maximum_fusion), channel_id=1, source_target_pairs={{0,64},{64,0},{1,65},{65,1},{2,66},{66,2},{3,67},{67,3},{4,68},{68... | collective-permute-start | bytes 10616840 | tf_op jit(solution)/shard_map/ppermute | solution.py:782
  336.5 36.9 %all-to-all-start.7 = ((bf16[16,4,24,768]{3,2,1,0:T(8,128)(2,1)}), bf16[16,4,24,768]{3,2,1,0:T(8,128)(2,1)}, u32[]{:S(2)}, u32[]{:S(2)}) async-start(bf16[16,4,24,768]{3,2,1,0:T(8,128)(2,1)} %get-tuple-element.163), calls=%async_computation.7 | async-start | bytes 4718592 | tf_op jit(solution)/shard_map/all_to_all | solution.py:50
  369.0 10.4 %collective-permute-start.18 = (bf16[256,384]{1,0:T(8,128)(2,1)S(1)}, bf16[256,384]{1,0:T(8,128)(2,1)S(1)}, u32[]{:S(2)}, u32[]{:S(2)}) collective-permute-start(bf16[256,384]{1,0:T(8,128)(2,1)S(1)} %get-tuple-element.202), channel_id=1, source_target_pairs={{0,2},{2,0},{4,6},{6,4},{1,3},{3,1},{5,7},{7,5},{8,10},{10,8},{12,... | collective-permute-start | bytes 589832 | tf_op jit(solution)/shard_map/ppermute | solution.py:789
  373.5 34.3 %all-to-all-start.8 = ((bf16[16,256,256]{2,1,0:T(8,128)(2,1)}), bf16[16,256,256]{2,1,0:T(8,128)(2,1)}, u32[]{:S(2)}, u32[]{:S(2)}) async-start(bf16[16,256,256]{2,1,0:T(8,128)(2,1)} %get-tuple-element.164), calls=%async_computation.8 | async-start | bytes 4194304 | tf_op jit(solution)/shard_map/all_to_all | solution.py:50
  385.4 28.6 %collective-permute-start.21 = (bf16[128,1536]{1,0:T(8,128)(2,1)}, bf16[128,1536]{1,0:T(8,128)(2,1)}, u32[]{:S(2)}, u32[]{:S(2)}) collective-permute-start(bf16[128,1536]{1,0:T(8,128)(2,1)} %add_convert_fusion.3), channel_id=1, source_target_pairs={{0,2},{2,0},{4,6},{6,4},{1,3},{3,1},{5,7},{7,5},{8,10},{10,8},{12,... | collective-permute-start | bytes 1179656 | tf_op jit(solution)/shard_map/ppermute | solution.py:795
  421.4 7.2 %collective-permute-start.22 = (f32[128,1536]{1,0:T(8,128)}, f32[128,1536]{1,0:T(8,128)S(1)}, u32[]{:S(2)}, u32[]{:S(2)}) collective-permute-start(f32[128,1536]{1,0:T(8,128)} %get-tuple-element.173), channel_id=1, source_target_pairs={{0,1},{1,0},{2,3},{3,2},{4,5},{5,4},{6,7},{7,6},{8,9},{9,8},{10,11... | collective-permute-start | bytes 2359304 | tf_op jit(solution)/shard_map/ppermute | solution.py:46
  432.4 38.5 %all-to-all-start.9 = ((bf16[64,24,768]{2,1,0:T(8,128)(2,1)}), bf16[64,24,768]{2,1,0:T(8,128)(2,1)S(1)}, u32[]{:S(2)}, u32[]{:S(2)}) async-start(bf16[64,24,768]{2,1,0:T(8,128)(2,1)} %bitcast.81), calls=%async_computation.9 | async-start | bytes 4718592 | tf_op jit(solution)/shard_map/all_to_all | solution.py:50
  448.3 20.2 %collective-permute-start.27 = (bf16[2,12,768]{2,0,1:T(2,128)(2,1)S(1)}, bf16[2,12,768]{2,0,1:T(2,128)(2,1)S(1)}, u32[]{:S(2)}, u32[]{:S(2)}) collective-permute-start(bf16[2,12,768]{2,0,1:T(2,128)(2,1)S(1)} %bitcast.99), channel_id=1, source_target_pairs={{0,33},{1,97},{32,1},{33,65},{64,32},{65,96},{96,0},{97,64},{2,35}... | collective-permute-start | bytes 110600 | tf_op jit(solution)/shard_map/ppermute | solution.py:848
  451.1 17.3 %collective-permute-start.26 = (bf16[2,12,768]{2,0,1:T(2,128)(2,1)S(1)}, bf16[2,12,768]{2,0,1:T(2,128)(2,1)S(1)}, u32[]{:S(2)}, u32[]{:S(2)}) collective-permute-start(bf16[2,12,768]{2,0,1:T(2,128)(2,1)S(1)} %bitcast.100), channel_id=1, source_target_pairs={{0,1},{1,65},{32,33},{33,97},{64,0},{65,64},{96,32},{97,96},{2,3},... | collective-permute-start | bytes 110600 | tf_op jit(solution)/shard_map/ppermute | solution.py:848
  452.9 15.6 %collective-permute-start.25 = (bf16[2,12,768]{2,0,1:T(2,128)(2,1)S(1)}, bf16[2,12,768]{2,0,1:T(2,128)(2,1)S(1)}, u32[]{:S(2)}, u32[]{:S(2)}) collective-permute-start(bf16[2,12,768]{2,0,1:T(2,128)(2,1)S(1)} %bitcast.101), channel_id=1, source_target_pairs={{0,32},{1,96},{32,0},{33,64},{64,33},{65,97},{96,1},{97,65},{2,34}... | collective-permute-start | bytes 110600 | tf_op jit(solution)/shard_map/ppermute | solution.py:848
  453.3 16.2 %collective-permute-start.24 = (bf16[2,12,768]{2,0,1:T(2,128)(2,1)S(1)}, bf16[2,12,768]{2,0,1:T(2,128)(2,1)S(1)}, u32[]{:S(2)}, u32[]{:S(2)}) collective-permute-start(bf16[2,12,768]{2,0,1:T(2,128)(2,1)S(1)} %bitcast.103), channel_id=1, source_target_pairs={{0,0},{1,64},{32,32},{33,96},{64,1},{65,65},{96,33},{97,97},{2,2},... | collective-permute-start | bytes 110600 | tf_op jit(solution)/shard_map/ppermute | solution.py:848
  (78 other events, 605.4 us)

commit v5 on v4

--- a/solution.py
+++ b/solution.py
@@ -396,10 +396,52 @@
     gain_grad_ref[...] = jnp.broadcast_to(gain_grad, gain_grad_ref.shape)
 
 
-def query_columns_kernel(rows_ref, pair_rows_ref, grad_ref, pair_grad_ref, before_ref, partial_ref):
-    del before_ref
+def early_columns_kernel(rows_ref, pair_rows_ref, grad_ref, pair_grad_ref, gain_grad_ref, partial_ref):
+    row = lax.broadcasted_iota(jnp.int32, (16, partial_ref.shape[0]), 0)
+    gain_rows = jnp.where(row == 0, gain_grad_ref[0:1, :], 0.0)
+    square = (16, HEAD_SIZE)
+    unit = lax.broadcasted_iota(jnp.int32, square, 0) == lax.broadcasted_iota(jnp.int32, square, 1)
+    partial_ref[:, :HEAD_SIZE] = dot(gain_rows.astype(bf16), unit.astype(bf16), TN).astype(bf16)
     queries = dot(rows_ref[...], grad_ref[...], TN) + dot(pair_rows_ref[...], pair_grad_ref[...], TN)
-    partial_ref[...] = queries.astype(bf16)
+    partial_ref[:, HEAD_SIZE:] = queries.astype(bf16)
+
+
+def add_pair_kernel(own_ref, other_ref, *out_refs):
+    total = own_ref[...].astype(f32) + other_ref[...].astype(f32)
+    width = out_refs[0].shape[1]
+    for k, ref in enumerate(out_refs):
+        ref[...] = total[:, k * width : (k + 1) * width]
+
+
+def expert_sums(own, other, depth):
+    width = own.shape[1]
+    units = width // 2
+    cost = pl.CostEstimate(flops=1, bytes_accessed=1, transcendentals=0)
+    params = pltpu.CompilerParams(vmem_limit_bytes=FAR_BYTES)
+    rows = depth // 6
+    part = pl.BlockSpec((rows, width), lambda i: (i, 0))
+    grad_gate, grad_up = pl.pallas_call(
+        add_pair_kernel,
+        grid=(6,),
+        in_specs=[part, part],
+        out_specs=[pl.BlockSpec((rows, units), lambda i: (i, 0))] * 2,
+        out_shape=[jax.ShapeDtypeStruct((depth, units), f32)] * 2,
+        compiler_params=params,
+        cost_estimate=cost,
+        name="add_gate_up",
+    )(own, other)
+    part = pl.BlockSpec((units, width), lambda i: (depth // units + i, 0))
+    grad_down = pl.pallas_call(
+        add_pair_kernel,
+        grid=(2,),
+        in_specs=[part, part],
+        out_specs=pl.BlockSpec((units, width), lambda i: (0, i)),
+        out_shape=jax.ShapeDtypeStruct((units, 2 * width), f32),
+        compiler_params=params,
+        cost_estimate=cost,
+        name="add_down",
+    )(own, other)
+    return grad_gate, grad_up, grad_down
 
 
 def split_grads_kernel(place_ref, came_ref, own_ref, later_ref, before_ref):
@@ -413,32 +455,14 @@
         later_ref[at, :] = lax.fori_loop(spot + 1, spots, add, own_ref[at, :].astype(f32))
 
 
-def keys_back_kernel(
-    place_ref, later_ref, next_ref, cosine_ref, sine_ref, rows_ref, weight_ref, side_ref,
-    partial_ref, own_ref, other_ref, sum_ref,
-):
+def key_columns_kernel(later_ref, next_ref, cosine_ref, sine_ref, rows_ref, before_ref, partial_ref, linear_ref):
+    del before_ref
     total = (later_ref[...] + next_ref[...].astype(f32)).astype(bf16)
     key = total[:, :HEAD_SIZE].astype(f32)
     turned = key * cosine_ref[...] - pltpu.roll(key, HEAD_SIZE // 2, 1) * sine_ref[...]
     linear = jnp.concatenate([turned.astype(bf16), total[:, HEAD_SIZE:]], axis=1)
+    linear_ref[...] = linear
     partial_ref[...] = dot(rows_ref[...], linear, TN).astype(bf16)
-    sum_ref[...] = side_ref[...] + dot(linear, weight_ref[...], NT)
-    core, rows = place_ref[0], own_ref.shape[0]
-    own_ref[...] = sum_ref[pl.ds(pl.multiple_of(core * rows, rows), rows), :]
-    other_ref[...] = sum_ref[pl.ds(pl.multiple_of((1 - core) * rows, rows), rows), :]
-
-
-def gain_columns_kernel(own_ref, swapped_ref, pair_ref, acts_ref, gain_grad_ref, before_ref, partial_ref):
-    del before_ref
-    values = acts_ref[...].astype(f32)
-    inverse = lax.rsqrt(jnp.mean(values * values, axis=-1, keepdims=True) + NORM_EPS)
-    normed_grad = own_ref[...] + swapped_ref[...] + pair_ref[...].astype(f32)
-    gain_grad = jnp.sum(normed_grad * values * inverse, axis=0, keepdims=True)
-    row = lax.broadcasted_iota(jnp.int32, (16, values.shape[1]), 0)
-    gain_rows = jnp.where(row == 0, gain_grad, jnp.where(row == 1, gain_grad_ref[0:1, :], 0.0))
-    square = (16, HEAD_SIZE)
-    unit = lax.broadcasted_iota(jnp.int32, square, 0) == lax.broadcasted_iota(jnp.int32, square, 1)
-    partial_ref[...] = dot(gain_rows.astype(bf16), unit.astype(bf16), TN).astype(bf16)
 
 
 def acts_back_kernel(own_ref, swapped_ref, pair_ref, acts_ref, gain_ref, grad_ref, out_ref):
@@ -449,7 +473,8 @@
 
 
 def whole_call(
-    kernel, name, out_shape, *args, words=0, scratch_shapes=(), blocks=(), out_blocks=(), aliases=(), near=True
+    kernel, name, out_shape, *args, words=0, scratch_shapes=(), blocks=(), out_blocks=(), aliases=(), near=True,
+    cost=None,
 ):
     blocks, out_blocks = dict(blocks), dict(out_blocks)
     whole = lambda shape: pl.BlockSpec(shape, lambda i: (0,) * len(shape))
@@ -466,6 +491,7 @@
         input_output_aliases=dict(aliases),
         scratch_shapes=list(scratch_shapes),
         compiler_params=pltpu.CompilerParams(vmem_limit_bytes=NEAR_BYTES if near else FAR_BYTES),
+        cost_estimate=cost,
         name=name,
     )(*args)
 
@@ -803,45 +829,38 @@
         place, came, own_kv_grad, words=1,
     )
     next_grad = lax.ppermute(before_grad, ("xh", "xl"), [(p + 1, p) for p in range(planes - 1)])
+    table = pl.BlockSpec((chip_rows, HEAD_SIZE), lambda i: (0, 0))
     next_grad, back_normed_grad = lax.optimization_barrier((next_grad, back_normed_grad))
-    table = pl.BlockSpec((chip_rows, HEAD_SIZE), lambda i: (0, 0))
-    partial_shape = jax.ShapeDtypeStruct((model_dim, kv_width + quarter), bf16)
-    unread = pl.BlockSpec((16, HEAD_SIZE), lambda i: (0, 0))
-    partial, normed_grad, other_normed_grad = whole_call(
-        keys_back_kernel, "keys_back", [partial_shape, wide, wide],
-        place, later_grad, next_grad, cosine, sine, normed_one, weights, side_normed_grad, words=1,
-        blocks={3: table, 4: table, 6: pl.BlockSpec((model_dim, 2 * HEAD_SIZE), lambda i: (0, 0))},
-        out_blocks={0: pl.BlockSpec((model_dim, 2 * HEAD_SIZE), lambda i: (0, 0))},
-        scratch_shapes=[pltpu.VMEM((chip_rows, model_dim), f32)],
-    )
-    swapped_grad = core_swap(other_normed_grad)
+    early = HEAD_SIZE + quarter
+    partial_shape = jax.ShapeDtypeStruct((model_dim, early + 2 * HEAD_SIZE), bf16)
     (partial,) = whole_call(
-        query_columns_kernel, "query_columns", [partial_shape],
-        normed_one, pair_normed, side_query_grad, pair_query_grad, partial, blocks={4: unread},
-        out_blocks={0: pl.BlockSpec((model_dim, quarter), lambda i: (0, 1))}, aliases={4: 0}, near=False,
-    )
-    (partial,) = whole_call(
-        gain_columns_kernel, "gain_columns", [partial_shape],
-        normed_grad, swapped_grad, back_normed_grad, acts, gain_two_grad, partial, blocks={5: unread},
-        out_blocks={0: pl.BlockSpec((model_dim, HEAD_SIZE), lambda i: (0, 2))}, aliases={5: 0}, near=False,
-    )
-    partial, expert_other, out_received, grad_one = lax.optimization_barrier(
-        (partial, expert_other, out_received, grad_one)
+        early_columns_kernel, "early_columns", [partial_shape],
+        normed_one, pair_normed, side_query_grad, pair_query_grad, gain_two_grad,
+        out_blocks={0: pl.BlockSpec((model_dim, early), lambda i: (0, 0))}, near=False,
+    )
+    partial, kv_lin_grad = whole_call(
+        key_columns_kernel, "key_columns", [partial_shape, jax.ShapeDtypeStruct(square, bf16)],
+        later_grad, next_grad, cosine, sine, normed_one, partial,
+        blocks={2: table, 3: table, 5: pl.BlockSpec((16, HEAD_SIZE), lambda i: (0, 0))},
+        out_blocks={0: pl.BlockSpec((model_dim, 2 * HEAD_SIZE), lambda i: (0, 2))}, aliases={5: 0}, near=False,
+    )
+    partial, expert_other, out_received, kv_lin_grad, side_normed_grad = lax.optimization_barrier(
+        (partial, expert_other, out_received, kv_lin_grad, side_normed_grad)
+    )
+    normed_grad = side_normed_grad + dot(kv_lin_grad, weights[:, : 2 * HEAD_SIZE], NT)
+    swapped_grad, expert_other = lax.optimization_barrier(
+        (core_swap(of_core(core, normed_grad, False)), expert_other)
     )
     (grad_acts,) = whole_call(
         acts_back_kernel, "acts_back", [wide],
-        normed_grad, swapped_grad, back_normed_grad, acts, gain_rows, grad_one, near=False,
+        of_core(core, normed_grad, True), swapped_grad, back_normed_grad, acts,
+        gain_rows, grad_one, near=False, cost=pl.CostEstimate(flops=1, bytes_accessed=1, transcendentals=0),
     )
     received = send_to_chips(partial)
-    expert_grad = expert_part.astype(f32) + expert_other.astype(f32)
-    expert_grads = (
-        expert_grad[:model_dim, :units],
-        expert_grad[:model_dim, units:],
-        jnp.concatenate([expert_grad[model_dim : model_dim + units], expert_grad[model_dim + units :]], axis=1),
-    )
+    expert_grads = expert_sums(expert_part, expert_other, model_dim)
     plane_sums = jnp.sum(out_received.astype(f32), axis=0).astype(bf16)
     plane_sums = plane_sums.reshape(2, 2, 2, shard_rows, -1)
-    grad_w_out = 0.0
+    pieces = []
     for k in range(4):
         piece = lax.dynamic_index_in_dim(plane_sums, (lax.axis_index("xl") + k) % 2, 1, False)
         piece = lax.dynamic_index_in_dim(piece, (half + k // 2) % 2, 1, False)
@@ -855,12 +874,15 @@
                 for c in range(2)
             ],
         )
-        grad_w_out = grad_w_out + piece.astype(f32)
+        pieces.append(piece)
+    pieces, expert_grads, grad_acts = lax.optimization_barrier((pieces, expert_grads, grad_acts))
+    grad_w_out = sum(piece.astype(f32) for piece in pieces)
     grad_w_out = jnp.concatenate([grad_w_out[0], grad_w_out[1]], axis=1)
     received = received.astype(f32).reshape(chips // 2, 2, 2 * shard_rows, -1)
     sums = jnp.sum(received, axis=0)
+    shared = sums[0] + sums[1]
     sums = jnp.concatenate(
-        [sums[0, :, :kv_width] + sums[1, :, :kv_width], sums[0, :, kv_width:], sums[1, :, kv_width:]], axis=1
+        [shared[:, early:], shared[:, :HEAD_SIZE], sums[0, :, HEAD_SIZE:early], sums[1, :, HEAD_SIZE:early]], axis=1
     ).reshape(2, shard_rows, -1)
     given = core_swap(jnp.where(core == 0, sums[1], sums[0]))
     kept = jnp.where(core == 0, sums[0], sums[1])
@@ -869,16 +891,24 @@
     def columns(begin_at, width):
         return jnp.concatenate([part[:, begin_at : begin_at + width] for part in sums], axis=1)
 
-    gain_sums = sums[0][:, 2 * HEAD_SIZE : 2 * HEAD_SIZE + 2] + sums[1][:, 2 * HEAD_SIZE : 2 * HEAD_SIZE + 2]
+    grad_query, grad_key, grad_value = columns(kv_width, HALF_WIDTH), columns(0, HEAD_SIZE), columns(HEAD_SIZE, HEAD_SIZE)
+    weight_columns = np.arange(kv_width + HALF_WIDTH)
+    weight_columns = (weight_columns < 2 * HEAD_SIZE) | (weight_columns >= kv_width)
+    halves = (jnp.where(core == 0, own_part, other_part), jnp.where(core == 0, other_part, own_part))
+    terms = [
+        jnp.where(weight_columns[None], weight[:, : kv_width + HALF_WIDTH].astype(f32) * grad, 0.0)
+        for weight, grad in zip(halves, sums)
+    ]
+    grad_gain_attn = jnp.sum(terms[0] + terms[1], axis=1) / gain_attn.astype(f32)
     return (
         activations,
         grad_acts,
-        columns(kv_width, HALF_WIDTH),
-        columns(0, HEAD_SIZE),
-        columns(HEAD_SIZE, HEAD_SIZE),
+        grad_query,
+        grad_key,
+        grad_value,
         grad_w_out,
-        gain_sums[:, 0],
-        gain_sums[:, 1],
+        grad_gain_attn,
+        sums[0][:, 2 * HEAD_SIZE] + sums[1][:, 2 * HEAD_SIZE],
         *expert_grads,
     )
 

time: 484 us -> 482 us (level)
  local copies, waits for them, and re-layouts: 31.4 us -> 19.8 us
  other arithmetic: 29.3 us -> 21.6 us
  starting transfers between devices: 101 us -> 107 us
  Pallas kernels: 88.7 us -> 94.6 us
    pallas_call x0 -> x2, Pallas kernels: none -> 8.65 us  [the longest x1 5.89 us: expert_sums(): pl.pallas_call(add_pair_kernel, grid=(6,), in_specs=[part, part], out_spe...]
    slice x3 -> x2, local copies, waits for them, and re-layouts: 7.34 us -> 0.01 us  [the longest x1 0.01 us: body(): shared[:, early:]]
    add x4 -> x3, other arithmetic: 6.79 us -> 0.66 us  [the longest x1 0.63 us: body(): sums[0][:, 2 * HEAD_SIZE] + sums[1][:, 2 * HEAD_SIZE]]
    unnamed x141 -> x143, local copies, waits for them, and re-layouts: 20.4 us -> 16.3 us
    pallas_call x9 -> x8, Pallas kernels: 23.6 us -> 20.4 us  [whole_call(): pl.pallas_call(kernel, grid=(1,), in_specs=specs, out_specs=[out_blocks.g...]
    dot_general x14 -> x15, matrix products: 24.1 us -> 27.4 us  [dot(): return lax.dot_general(a, b, (dims, ((), ())), preferred_element_type=f32)]
  transfers between devices with their start and end apart: 36 -> 36, of which waited for: 18 -> 17; matrix products, arithmetic and copies ran while one was open for 11% -> 7% of each run, Pallas kernels for 11% -> 13%
where the time goes in v5:
time: 482 us; the launch traced here: 473 us
  waiting for transfers between devices  125 us (26%)
  starting transfers between devices  107 us (22%)
  Pallas kernels  94.6 us (20%)
  blocking collectives  75 us (16%)
  matrix products  27.4 us (6%)
  other arithmetic  21.6 us (4%)
  local copies, waits for them, and re-layouts  19.8 us (4%)
    all_to_all x8, waiting for transfers between devices, exchange(): return lax.all_to_all(value, axes, 0, 0, tiled=True)  77.3 us
    all_to_all x2, blocking collectives, exchange(): return lax.all_to_all(value, axes, 0, 0, tiled=True)  75 us
    all_to_all x8, starting transfers between devices, exchange(): return lax.all_to_all(value, axes, 0, 0, tiled=True)  48.8 us
    dot_general x15, matrix products, dot(): return lax.dot_general(a, b, (dims, ((), ())), preferred_element_type=f32)  27.4 us
    pallas_call x1, Pallas kernels, attend_back(): pl.pallas_call(attend_back_kernel, grid_spec=pltpu.PrefetchScalarGridSpec...  24.9 us
    ppermute x13, starting transfers between devices, core_swap(): return lax.ppermute(value, 'c', SWAP)  21.4 us
    pallas_call x8, Pallas kernels, whole_call(): pl.pallas_call(kernel, grid=(1,), in_specs=specs, out_specs=[out_blocks.g...  20.4 us
    ppermute x1, waiting for transfers between devices, body(): expert_other = lax.ppermute(expert_part, 'xh', SWAP)  19.5 us
  transfers between devices with their start and end apart: 36, of which 17 were waited for; matrix products, arithmetic and copies ran while one was open for 7% of the time, Pallas kernels for 13%

profile of v5, /device:TPU:1, one launch (start us, length us, event | category | flops | bytes accessed | tf_op | source)
XLA Modules:
  0.0 473.2 jit_solution(7577350610502551171)
XLA Ops:
  15.1 11.0 %all-to-all-start = ((bf16[64,24,768]{2,1,0:T(8,128)(2,1)}), bf16[64,24,768]{2,1,0:T(8,128)(2,1)}, u32[]{:S(2)}, u32[]{:S(2)}) async-start(bf16[64,24,768]{2,1,0:T(8,128)(2,1)} %get-tuple-element.114), calls=%async_computation | async-start | bytes 4718592 | tf_op jit(solution)/shard_map/all_to_all | solution.py:50
  32.4 22.2 %all-to-all-done = bf16[64,24,768]{2,1,0:T(8,128)(2,1)} async-done(((bf16[64,24,768]{2,1,0:T(8,128)(2,1)}), bf16[64,24,768]{2,1,0:T(8,128)(2,1)}, u32[]{:S(2)}, u32[]{:S(2)}) %all-to-all-start) | async-done | bytes 2359328 | tf_op jit(solution)/shard_map/all_to_all | solution.py:50
  55.4 4.4 all-to-all-start.1
  60.4 5.2 %project_keys.1 = (bf16[256,1536]{1,0:T(8,128)(2,1)}, bf16[256,256]{1,0:T(8,128)(2,1)}, bf16[16,256,256]{2,1,0:T(8,128)(2,1)}, f32[8,1536]{1,0:T(8,128)}) custom-call(s32[5]{0:T(128)} %stack.40.place_ref, bf16[128,1536]{1,0:T(8,128)(2,1)} %acts_ref.3, bf16[128,1536]{1,0:T(8,128)(2,1)} %copy-done.46, bf16[128,1536]{1,0:T(8,128)(2,1)} %copy-done.45, ...), custom_call_target="tpu_custom_call" | custom-call | tf_op jit(solution)/shard_map/project_keys/pallas_call | solution.py:281
  69.2 4.4 all-to-all-start.2
  73.6 6.1 %collective-permute-start.10 = (bf16[384,768]{1,0:T(8,128)(2,1)}, bf16[384,768]{1,0:T(8,128)(2,1)S(1)}, u32[]{:S(2)}, u32[]{:S(2)}) collective-permute-start(bf16[384,768]{1,0:T(8,128)(2,1)} %bitcast.9), channel_id=1, source_target_pairs={{33,0},{97,1},{1,32},{65,33},{32,64},{96,65},{0,96},{64,97},{35,2}... | collective-permute-start | bytes 1769480 | tf_op jit(solution)/shard_map/ppermute | solution.py:714
  94.4 10.4 %collective-permute-done.6.theirs_ref = bf16[256,384]{1,0:T(8,128)(2,1)} collective-permute-done((bf16[256,384]{1,0:T(8,128)(2,1)}, bf16[256,384]{1,0:T(8,128)(2,1)}, u32[]{:S(2)}, u32[]{:S(2)}) %collective-permute-start.6) | collective-permute-done | bytes 196640 | tf_op jit(solution)/shard_map/ppermute | solution.py:731
  108.8 17.2 %attend.1 = (f32[256,768]{1,0:T(8,128)}, bf16[256,768]{1,0:T(8,128)(2,1)}, f32[6,8,256]{2,1,0:T(8,128)}) custom-call(s32[5]{0:T(128)} %stack.40.place_ref, s32[256,128]{1,0:T(8,128)} %broadcast_in_dim.72.low_ref, bf16[256,384]{1,0:T(8,128)(2,1)} %get-tuple-element.130.mine_ref, bf16[256,384]{1,0:T(8,128)(2,1)} %collective-permute-done.6.theirs_ref, ...), custom_call_target="tpu_custom_call" | custom-call | flops 20000000000 | bytes 4000000 | tf_op jit(solution)/shard_map/attend/pallas_call | solution.py:132
  134.7 37.8 %all_to_all.50 = bf16[32,24,1536]{2,1,0:T(8,128)(2,1)S(1)} all-to-all(bf16[32,24,1536]{2,1,0:T(8,128)(2,1)S(1)} %bitcast.77), channel_id=1, replica_groups=mesh['xh'=2,'xl'=2,'y'=4,'z'=4,'c'=2] {'xl','y','z'}, dimensions={0} | all-to-all | bytes 4718592 | tf_op jit(solution)/shard_map/all_to_all | solution.py:50
  190.6 4.1 all-to-all-start.4
  195.9 28.8 %all-to-all-done.4 = bf16[32,24,1536]{2,1,0:T(8,128)(2,1)S(1)} async-done(((bf16[32,24,1536]{2,1,0:T(8,128)(2,1)}), bf16[32,24,1536]{2,1,0:T(8,128)(2,1)S(1)}, u32[]{:S(2)}, u32[]{:S(2)}) %all-to-all-start.4) | async-done | bytes 2359328 | tf_op jit(solution)/shard_map/all_to_all | solution.py:50
  226.1 5.8 %combine.1 = (bf16[128,1536]{1,0:T(8,128)(2,1)}, f32[128,1536]{1,0:T(8,128)}, bf16[768,1536]{1,0:T(8,128)(2,1)}) custom-call(s32[2]{0:T(128)} %pad_add_fusion.1.valid_ref, f32[1]{0:T(128)S(6)} %div.17.scale_ref, bf16[768,1536]{1,0:T(8,128)(2,1)} %bitcast.79, bf16[256,768]{1,0:T(8,128)(2,1)} %copy-done.12, f32[128,1536]{1,0:T(8,128)} %copy-done.4, ...), custom_call_target="tpu_custom_call" | custom-call | tf_op jit(solution)/shard_map/combine/pallas_call | solution.py:369
  231.9 37.2 %all_to_all.51 = bf16[32,24,1536]{2,1,0:T(8,128)(2,1)S(1)} all-to-all(bf16[32,24,1536]{2,1,0:T(8,128)(2,1)} %bitcast.87), channel_id=1, replica_groups=mesh['xh'=2,'xl'=2,'y'=4,'z'=4,'c'=2] {'xl','y','z'}, dimensions={0} | all-to-all | bytes 4718592 | tf_op jit(solution)/shard_map/all_to_all | solution.py:50
  288.2 4.4 all-to-all-start.6
  303.7 18.9 %all-to-all-done.6 = bf16[32,24,1536]{2,1,0:T(8,128)(2,1)S(1)} async-done(((bf16[32,24,1536]{2,1,0:T(8,128)(2,1)}), bf16[32,24,1536]{2,1,0:T(8,128)(2,1)S(1)}, u32[]{:S(2)}, u32[]{:S(2)}) %all-to-all-start.6) | async-done | bytes 2359328 | tf_op jit(solution)/shard_map/all_to_all | solution.py:50
  329.8 4.2 collective-permute-start.17
  334.8 5.2 %out_project_back.1 = (bf16[256,768]{1,0:T(8,128)(2,1)}, bf16[16,4,24,768]{3,2,1,0:T(8,128)(2,1)}) custom-call(s32[5]{0:T(128)} %stack.40.place_ref, bf16[128,1536]{1,0:T(8,128)(2,1)} %get-tuple-element.171.own_ref, bf16[128,1536]{1,0:T(8,128)(2,1)} %copy-done.49, bf16[256,768]{1,0:T(8,128)(2,1)} %get-tuple-element.143.attn_ref, bf16[384,768]{1,0:T(8,128)(2,1)} %copy-done.6, ...), custom_call_target="tpu_custom_call" | custom-call | tf_op jit(solution)/shard_map/out_project_back/pallas_call | solution.py:556
  340.0 5.0 %all-to-all-start.7 = ((bf16[16,4,24,768]{3,2,1,0:T(8,128)(2,1)}), bf16[16,4,24,768]{3,2,1,0:T(8,128)(2,1)S(1)}, u32[]{:S(2)}, u32[]{:S(2)}) async-start(bf16[16,4,24,768]{3,2,1,0:T(8,128)(2,1)} %get-tuple-element.175), calls=%async_computation.7 | async-start | bytes 4718592 | tf_op jit(solution)/shard_map/all_to_all | solution.py:50
  345.5 24.9 %attend_back.1 = (bf16[256,768]{1,0:T(8,128)(2,1)}, bf16[16,256,256]{2,1,0:T(8,128)(2,1)}, bf16[256,256]{1,0:T(8,128)(2,1)}) custom-call(s32[5]{0:T(128)} %stack.40.place_ref, s32[8,256]{1,0:T(8,128)} %broadcast_in_dim.76.low_ref, bf16[256,384]{1,0:T(8,128)(2,1)} %get-tuple-element.130.mine_ref, bf16[256,384]{1,0:T(8,128)(2,1)} %collective-permute-done.6.theirs_ref, ...), custom_call_target="tpu_custom_call" | custom-call | flops 28000000000 | bytes 8000000 | tf_op jit(solution)/shard_map/attend_back/pallas_call | solution.py:618
  378.3 6.0 %all-to-all-start.8 = ((bf16[16,256,256]{2,1,0:T(8,128)(2,1)}), bf16[16,256,256]{2,1,0:T(8,128)(2,1)S(1)}, u32[]{:S(2)}, u32[]{:S(2)}) async-start(bf16[16,256,256]{2,1,0:T(8,128)(2,1)} %get-tuple-element.176), calls=%async_computation.8 | async-start | bytes 4194304 | tf_op jit(solution)/shard_map/all_to_all | solution.py:50
  391.8 19.5 %collective-permute-done.17.other_ref = bf16[2304,768]{1,0:T(8,128)(2,1)} collective-permute-done((bf16[2304,768]{1,0:T(8,128)(2,1)}, bf16[2304,768]{1,0:T(8,128)(2,1)}, u32[]{:S(2)}, u32[]{:S(2)}) %collective-permute-start.17) | collective-permute-done | bytes 3538976 | tf_op jit(solution)/shard_map/ppermute | solution.py:808
  423.8 9.6 %all-to-all-start.9 = ((bf16[64,24,768]{2,1,0:T(8,128)(2,1)}), bf16[64,24,768]{2,1,0:T(8,128)(2,1)}, u32[]{:S(2)}, u32[]{:S(2)}) async-start(bf16[64,24,768]{2,1,0:T(8,128)(2,1)} %bitcast.78), calls=%async_computation.9 | async-start | bytes 4718592 | tf_op jit(solution)/shard_map/all_to_all | solution.py:50
  440.1 5.5 %collective-permute-start.22 = (bf16[2,12,768]{2,0,1:T(2,128)(2,1)S(1)}, bf16[2,12,768]{2,0,1:T(2,128)(2,1)S(1)}, u32[]{:S(2)}, u32[]{:S(2)}) collective-permute-start(bf16[2,12,768]{2,0,1:T(2,128)(2,1)S(1)} %bitcast.94), channel_id=1, source_target_pairs={{0,0},{1,64},{32,32},{33,96},{64,1},{65,65},{96,33},{97,97},{2,2},... | collective-permute-start | bytes 110600 | tf_op jit(solution)/shard_map/ppermute | solution.py:867
  451.9 5.9 %add_gate_up.1 = (f32[1536,384]{1,0:T(8,128)}, f32[1536,384]{1,0:T(8,128)}) custom-call(bf16[2304,768]{1,0:T(8,128)(2,1)} %pad_maximum_fusion.own_ref, bf16[2304,768]{1,0:T(8,128)(2,1)} %collective-permute-done.17.other_ref), custom_call_target="tpu_custom_call" | custom-call | flops 1 | bytes 1 | tf_op jit(solution)/shard_map/add_gate_up/pallas_call | solution.py:423
  (279 shorter events, 167.0 us)
Async XLA Ops:
  0.7 14.4 %collective-permute-start.1 = (bf16[128,1536]{1,0:T(8,128)(2,1)}, bf16[128,1536]{1,0:T(8,128)(2,1)S(1)}, u32[]{:S(2)}, u32[]{:S(2)}) collective-permute-start(bf16[128,1536]{1,0:T(8,128)(2,1)} %acts_ref.3), channel_id=1, source_target_pairs={{0,2},{2,0},{4,6},{6,4},{1,3},{3,1},{5,7},{7,5},{8,10},{10,8},{12,... | collective-permute-start | bytes 1179656 | tf_op jit(solution)/shard_map/ppermute | solution.py:680
  3.2 11.8 %collective-permute-start.2 = (bf16[128,1536]{1,0:T(8,128)(2,1)}, bf16[128,1536]{1,0:T(8,128)(2,1)S(1)}, u32[]{:S(2)}, u32[]{:S(2)}) collective-permute-start(bf16[128,1536]{1,0:T(8,128)(2,1)} %acts_ref.3), channel_id=1, source_target_pairs={{0,32},{32,64},{64,96},{1,33},{33,65},{65,97},{2,34},{34,66},{66,9... | collective-permute-start | bytes 1179656 | tf_op jit(solution)/shard_map/ppermute | solution.py:681
  15.1 39.6 %all-to-all-start = ((bf16[64,24,768]{2,1,0:T(8,128)(2,1)}), bf16[64,24,768]{2,1,0:T(8,128)(2,1)}, u32[]{:S(2)}, u32[]{:S(2)}) async-start(bf16[64,24,768]{2,1,0:T(8,128)(2,1)} %get-tuple-element.114), calls=%async_computation | async-start | bytes 4718592 | tf_op jit(solution)/shard_map/all_to_all | solution.py:50
  55.4 13.8 %all-to-all-start.1 = ((bf16[16,24,768]{2,1,0:T(8,128)(2,1)}), bf16[16,24,768]{2,1,0:T(8,128)(2,1)}, u32[]{:S(2)}, u32[]{:S(2)}) async-start(bf16[16,24,768]{2,1,0:T(8,128)(2,1)} %get-tuple-element.138), calls=%async_computation.1 | async-start | bytes 1179648 | tf_op jit(solution)/shard_map/all_to_all | solution.py:50
  69.2 39.6 %all-to-all-start.2 = ((bf16[16,256,256]{2,1,0:T(8,128)(2,1)}), bf16[16,256,256]{2,1,0:T(8,128)(2,1)}, u32[]{:S(2)}, u32[]{:S(2)}) async-start(bf16[16,256,256]{2,1,0:T(8,128)(2,1)} %get-tuple-element.139), calls=%async_computation.2 | async-start | bytes 4194304 | tf_op jit(solution)/shard_map/all_to_all | solution.py:50
  73.6 31.1 %collective-permute-start.10 = (bf16[384,768]{1,0:T(8,128)(2,1)}, bf16[384,768]{1,0:T(8,128)(2,1)S(1)}, u32[]{:S(2)}, u32[]{:S(2)}) collective-permute-start(bf16[384,768]{1,0:T(8,128)(2,1)} %bitcast.9), channel_id=1, source_target_pairs={{33,0},{97,1},{1,32},{65,33},{32,64},{96,65},{0,96},{64,97},{35,2}... | collective-permute-start | bytes 1769480 | tf_op jit(solution)/shard_map/ppermute | solution.py:714
  79.7 27.7 %collective-permute-start.7 = (bf16[384,768]{1,0:T(8,128)(2,1)}, bf16[384,768]{1,0:T(8,128)(2,1)S(1)}, u32[]{:S(2)}, u32[]{:S(2)}) collective-permute-start(bf16[384,768]{1,0:T(8,128)(2,1)} %bitcast.9), channel_id=1, source_target_pairs={{0,0},{64,1},{32,32},{96,33},{1,64},{65,65},{33,96},{97,97},{2,2},... | collective-permute-start | bytes 1769480 | tf_op jit(solution)/shard_map/ppermute | solution.py:714
  83.1 24.8 %collective-permute-start.8 = (bf16[384,768]{1,0:T(8,128)(2,1)}, bf16[384,768]{1,0:T(8,128)(2,1)S(1)}, u32[]{:S(2)}, u32[]{:S(2)}) collective-permute-start(bf16[384,768]{1,0:T(8,128)(2,1)} %bitcast.9), channel_id=1, source_target_pairs={{32,0},{96,1},{0,32},{64,33},{33,64},{97,65},{1,96},{65,97},{34,2}... | collective-permute-start | bytes 1769480 | tf_op jit(solution)/shard_map/ppermute | solution.py:714
  85.2 23.6 %collective-permute-start.9 = (bf16[384,768]{1,0:T(8,128)(2,1)}, bf16[384,768]{1,0:T(8,128)(2,1)}, u32[]{:S(2)}, u32[]{:S(2)}) collective-permute-start(bf16[384,768]{1,0:T(8,128)(2,1)} %bitcast.9), channel_id=1, source_target_pairs={{1,0},{65,1},{33,32},{97,33},{0,64},{64,65},{32,96},{96,97},{3,2},... | collective-permute-start | bytes 1769480 | tf_op jit(solution)/shard_map/ppermute | solution.py:714
  89.2 15.6 %collective-permute-start.6 = (bf16[256,384]{1,0:T(8,128)(2,1)}, bf16[256,384]{1,0:T(8,128)(2,1)}, u32[]{:S(2)}, u32[]{:S(2)}) collective-permute-start(bf16[256,384]{1,0:T(8,128)(2,1)} %get-tuple-element.131), channel_id=1, source_target_pairs={{0,2},{2,0},{4,6},{6,4},{1,3},{3,1},{5,7},{7,5},{8,10},{10,8},{12,... | collective-permute-start | bytes 589832 | tf_op jit(solution)/shard_map/ppermute | solution.py:731
  190.6 34.1 %all-to-all-start.4 = ((bf16[32,24,1536]{2,1,0:T(8,128)(2,1)}), bf16[32,24,1536]{2,1,0:T(8,128)(2,1)S(1)}, u32[]{:S(2)}, u32[]{:S(2)}) async-start(bf16[32,24,1536]{2,1,0:T(8,128)(2,1)} %bitcast.12), calls=%async_computation.4 | async-start | bytes 4718592 | tf_op jit(solution)/shard_map/all_to_all | solution.py:50
  288.2 34.4 %all-to-all-start.6 = ((bf16[32,24,1536]{2,1,0:T(8,128)(2,1)}), bf16[32,24,1536]{2,1,0:T(8,128)(2,1)S(1)}, u32[]{:S(2)}, u32[]{:S(2)}) async-start(bf16[32,24,1536]{2,1,0:T(8,128)(2,1)} %bitcast.16), calls=%async_computation.6 | async-start | bytes 4718592 | tf_op jit(solution)/shard_map/all_to_all | solution.py:50
  329.8 81.5 %collective-permute-start.17 = (bf16[2304,768]{1,0:T(8,128)(2,1)}, bf16[2304,768]{1,0:T(8,128)(2,1)}, u32[]{:S(2)}, u32[]{:S(2)}) collective-permute-start(bf16[2304,768]{1,0:T(8,128)(2,1)} %pad_maximum_fusion.own_ref), channel_id=1, source_target_pairs={{0,64},{64,0},{1,65},{65,1},{2,66},{66,2},{3,67},{67,3},{4,68},{68... | collective-permute-start | bytes 10616840 | tf_op jit(solution)/shard_map/ppermute | solution.py:808
  340.0 36.9 %all-to-all-start.7 = ((bf16[16,4,24,768]{3,2,1,0:T(8,128)(2,1)}), bf16[16,4,24,768]{3,2,1,0:T(8,128)(2,1)S(1)}, u32[]{:S(2)}, u32[]{:S(2)}) async-start(bf16[16,4,24,768]{3,2,1,0:T(8,128)(2,1)} %get-tuple-element.175), calls=%async_computation.7 | async-start | bytes 4718592 | tf_op jit(solution)/shard_map/all_to_all | solution.py:50
  371.5 12.7 %collective-permute-start.18 = (bf16[256,384]{1,0:T(8,128)(2,1)S(1)}, bf16[256,384]{1,0:T(8,128)(2,1)S(1)}, u32[]{:S(2)}, u32[]{:S(2)}) collective-permute-start(bf16[256,384]{1,0:T(8,128)(2,1)S(1)} %get-tuple-element.225), channel_id=1, source_target_pairs={{0,2},{2,0},{4,6},{6,4},{1,3},{3,1},{5,7},{7,5},{8,10},{10,8},{12,... | collective-permute-start | bytes 589832 | tf_op jit(solution)/shard_map/ppermute | solution.py:815
  378.3 33.0 %all-to-all-start.8 = ((bf16[16,256,256]{2,1,0:T(8,128)(2,1)}), bf16[16,256,256]{2,1,0:T(8,128)(2,1)S(1)}, u32[]{:S(2)}, u32[]{:S(2)}) async-start(bf16[16,256,256]{2,1,0:T(8,128)(2,1)} %get-tuple-element.176), calls=%async_computation.8 | async-start | bytes 4194304 | tf_op jit(solution)/shard_map/all_to_all | solution.py:50
  390.1 30.2 %collective-permute-start.21 = (bf16[128,1536]{1,0:T(8,128)(2,1)S(1)}, bf16[128,1536]{1,0:T(8,128)(2,1)S(1)}, u32[]{:S(2)}, u32[]{:S(2)}) collective-permute-start(bf16[128,1536]{1,0:T(8,128)(2,1)S(1)} %add_convert_fusion.3), channel_id=1, source_target_pairs={{0,2},{2,0},{4,6},{6,4},{1,3},{3,1},{5,7},{7,5},{8,10},{10,8},{12,... | collective-permute-start | bytes 1179656 | tf_op jit(solution)/shard_map/ppermute | solution.py:821
  413.3 7.0 %collective-permute-start.19 = (bf16[256,256]{1,0:T(8,128)(2,1)S(1)}, bf16[256,256]{1,0:T(8,128)(2,1)S(1)}, u32[]{:S(2)}, u32[]{:S(2)}) collective-permute-start(bf16[256,256]{1,0:T(8,128)(2,1)S(1)} %get-tuple-element.182), channel_id=1, source_target_pairs={{32,0},{64,32},{96,64},{33,1},{65,33},{97,65},{34,2},{66,34},{98,6... | collective-permute-start | bytes 393224 | tf_op jit(solution)/shard_map/ppermute | solution.py:831
  423.8 39.8 %all-to-all-start.9 = ((bf16[64,24,768]{2,1,0:T(8,128)(2,1)}), bf16[64,24,768]{2,1,0:T(8,128)(2,1)}, u32[]{:S(2)}, u32[]{:S(2)}) async-start(bf16[64,24,768]{2,1,0:T(8,128)(2,1)} %bitcast.78), calls=%async_computation.9 | async-start | bytes 4718592 | tf_op jit(solution)/shard_map/all_to_all | solution.py:50
  436.0 13.1 %collective-permute-start.26 = (f32[128,1536]{1,0:T(8,128)S(1)}, f32[128,1536]{1,0:T(8,128)}, u32[]{:S(2)}, u32[]{:S(2)}) collective-permute-start(f32[128,1536]{1,0:T(8,128)S(1)} %get-tuple-element.222), channel_id=1, source_target_pairs={{0,1},{1,0},{2,3},{3,2},{4,5},{5,4},{6,7},{7,6},{8,9},{9,8},{10,11... | collective-permute-start | bytes 2359304 | tf_op jit(solution)/shard_map/ppermute | solution.py:46
  440.1 23.3 %collective-permute-start.22 = (bf16[2,12,768]{2,0,1:T(2,128)(2,1)S(1)}, bf16[2,12,768]{2,0,1:T(2,128)(2,1)S(1)}, u32[]{:S(2)}, u32[]{:S(2)}) collective-permute-start(bf16[2,12,768]{2,0,1:T(2,128)(2,1)S(1)} %bitcast.94), channel_id=1, source_target_pairs={{0,0},{1,64},{32,32},{33,96},{64,1},{65,65},{96,33},{97,97},{2,2},... | collective-permute-start | bytes 110600 | tf_op jit(solution)/shard_map/ppermute | solution.py:867
  445.7 17.7 %collective-permute-start.23 = (bf16[2,12,768]{2,0,1:T(2,128)(2,1)S(1)}, bf16[2,12,768]{2,0,1:T(2,128)(2,1)S(1)}, u32[]{:S(2)}, u32[]{:S(2)}) collective-permute-start(bf16[2,12,768]{2,0,1:T(2,128)(2,1)S(1)} %bitcast.95), channel_id=1, source_target_pairs={{0,32},{1,96},{32,0},{33,64},{64,33},{65,97},{96,1},{97,65},{2,34}... | collective-permute-start | bytes 110600 | tf_op jit(solution)/shard_map/ppermute | solution.py:867
  446.1 17.3 %collective-permute-start.24 = (bf16[2,12,768]{2,0,1:T(2,128)(2,1)S(1)}, bf16[2,12,768]{2,0,1:T(2,128)(2,1)S(1)}, u32[]{:S(2)}, u32[]{:S(2)}) collective-permute-start(bf16[2,12,768]{2,0,1:T(2,128)(2,1)S(1)} %bitcast.97), channel_id=1, source_target_pairs={{0,1},{1,65},{32,33},{33,97},{64,0},{65,64},{96,32},{97,96},{2,3},... | collective-permute-start | bytes 110600 | tf_op jit(solution)/shard_map/ppermute | solution.py:867
  446.3 17.2 %collective-permute-start.25 = (bf16[2,12,768]{2,0,1:T(2,128)(2,1)S(1)}, bf16[2,12,768]{2,0,1:T(2,128)(2,1)S(1)}, u32[]{:S(2)}, u32[]{:S(2)}) collective-permute-start(bf16[2,12,768]{2,0,1:T(2,128)(2,1)S(1)} %bitcast.98), channel_id=1, source_target_pairs={{0,33},{1,97},{32,1},{33,65},{64,32},{65,96},{96,0},{97,64},{2,35}... | collective-permute-start | bytes 110600 | tf_op jit(solution)/shard_map/ppermute | solution.py:867
  (79 other events, 740.0 us)
